TPU v7x, 32 devices: a whole 2x2x4 slice. The times are simulated.
32 devices in a mesh: cycle: 8 (over z, core), bin: 4 (over y, x).
Axes of the slice: x: 2, y: 2, z: 4, core: 2. Of those that a mesh axis runs over, the one named last changes fastest.
Arguments:
- obs_minus_bg: bfloat16 [16384, 640], P(('cycle', 'bin')), may hold values from -30 to 30, as said below
- obs_minus_an: bfloat16 [16384, 640], P(('cycle', 'bin')), may hold values from -30 to 30, as said below
- tile_of_row: int32 [16384, 1], P(('cycle', 'bin')), may hold values from 0 to 11; in each aligned block of 512 rows (0 to 511, 512 to 1023, ...) at most 85 rows name the same one
- owner_order: int32 [12], replicated, may hold values from 0 to 11, as said below
Outputs:
- error_cov: float32 [12, 640, 640], P('bin', 'cycle')
Inputs may be any that keep to these rules, and one draw needn't show every extreme that they name: `obs_minus_bg`: each row's value lies in this range. `obs_minus_an`: each row's value lies in this range. `tile_of_row`: the rows of one device name one tile at most 85 times; some tile reaches it; every tile is named by some row. `owner_order`: a permutation of the tiles in which entry b * 3 + i is a tile of instrument i, so each index of bin owns one scan bin of each instrument.
All inputs are finite; a program needn't handle non-finite values.
Results may differ from a plain program's by a relative error of at most 0.0003.
Values may be sent and summed in bfloat16 or wider, within the bound.
No kernel may reach another device: no remote copies, remote signals or barrier semaphores. Data moves between devices by JAX's collectives and lax.ppermute only.
A program may use at most 320 MiB of HBM per device.

v0:
```python
import jax
import jax.numpy as jnp
from jax import lax
from jax.sharding import PartitionSpec as P

C_IASI = 616
C_CRIS = 431
C_ATMS = 22


def combined_all(value, axis, join):
    pieces = jax.tree.map(lambda part: lax.all_gather(part, axis), value)
    head = jax.tree.map(lambda part: part[0], pieces)
    tail = jax.tree.map(lambda part: part[1:], pieces)
    subtotal, _ = lax.scan(lambda subtotal, piece: (join(subtotal, piece), None), head, tail)
    return subtotal


def add_tuple(left, right):
    return jax.tree.map(lambda a, b: a + b, left, right)


def make_moments(width, pieces):
    received, tile_counts = pieces
    part_bg = received[..., :width]
    part_an = received[..., width:]
    cross = jnp.einsum("skrc,skrd->kcd", part_bg, part_an, preferred_element_type=jnp.float32)
    sums = jnp.sum(received, axis=(0, 2), dtype=jnp.float32)
    number = jnp.sum(tile_counts, axis=0).astype(jnp.float32)
    return (cross, sums, number)


def on_device(obs_minus_bg, obs_minus_an, tile_of_row, owner_order):
    n_bin = lax.axis_size("bin")
    n_cycle = lax.axis_size("cycle")
    rows = tile_of_row.shape[0]
    width = obs_minus_bg.shape[1]
    tiles = owner_order.shape[0]
    per_owner = tiles // n_bin
    slot_cap = 2 * rows // tiles
    scan_bins = tiles // 3
    tile = tile_of_row[:, 0]
    instr = tile // scan_bins
    limit = jnp.where(instr == 0, C_IASI, jnp.where(instr == 1, C_CRIS, C_ATMS))
    keep = jnp.arange(width)[None, :] < limit[:, None]
    zero = jnp.zeros((), jnp.bfloat16)
    masked_bg = jnp.where(keep, obs_minus_bg, zero)
    masked_an = jnp.where(keep, obs_minus_an, zero)
    onehot = (tile[:, None] == jnp.arange(tiles)[None, :]).astype(jnp.int32)
    rank = jnp.sum((jnp.cumsum(onehot, axis=0) - 1) * onehot, axis=1)
    order_hits = (owner_order[:, None] == jnp.arange(tiles)[None, :]).astype(jnp.int32)
    position = jnp.sum(order_hits * jnp.arange(tiles, dtype=jnp.int32)[:, None], axis=0)
    row_position = jnp.sum(onehot * position[None, :], axis=1)
    counts = jnp.sum(onehot, axis=0)
    counts_owner = jnp.sum(order_hits * counts[None, :], axis=1).reshape(n_bin, per_owner)
    stacked = jnp.concatenate([masked_bg, masked_an], axis=1)
    dest = row_position * slot_cap + rank
    sendbuf = jnp.zeros((tiles * slot_cap, 2 * width), jnp.bfloat16).at[dest].set(stacked)
    sendbuf = sendbuf.reshape(n_bin, per_owner, slot_cap, 2 * width)
    cross, sums, number = make_moments(
        width,
        (
            lax.all_to_all(sendbuf, "bin", split_axis=0, concat_axis=0, tiled=True),
            lax.all_to_all(counts_owner, "bin", split_axis=0, concat_axis=0, tiled=True),
        ),
    )
    rows_c = width // n_cycle
    start = lax.axis_index("cycle") * rows_c
    cross, sums, number = combined_all((cross, sums, number), "cycle", add_tuple)
    cross_rows = lax.dynamic_slice_in_dim(cross, start, rows_c, 1)
    mean_bg = sums[:, :width] / number[:, None]
    mean_an = sums[:, width:] / number[:, None]
    mean_rows = lax.dynamic_slice_in_dim(mean_bg, start, rows_c, 1)
    return cross_rows / number[:, None, None] - mean_rows[:, :, None] * mean_an[:, None, :]


def solution(mesh):
    return jax.shard_map(
        on_device,
        mesh=mesh,
        in_specs=(
            P(("cycle", "bin"), None),
            P(("cycle", "bin"), None),
            P(("cycle", "bin"), None),
            P(),
        ),
        out_specs=P("bin", "cycle", None),
        check_vma=False,
    )
```

profile of v0, /device:TPU:0, one launch (start us, length us, event | category | flops | bytes accessed | tf_op | source)
XLA Modules:
  0.0 483.3 jit_solution(17128156222015660391)
XLA Ops:
  6.5 0.7 select_reduce_fusion.2
  7.3 0.7 compare_select_fusion.2
  8.0 0.7 fusion.12
  8.7 1.1 reduce-window.6
  9.8 0.2 slice_reduce_fusion
  10.2 0.9 convert_reduce_fusion.1
  11.1 2.5 fusion.9
  13.6 4.2 scatter_custom_fusion
  17.8 2.1 reshape.67
  19.9 37.2 %all_to_all.14 = bf16[4,3,85,1280]{3,2,1,0:T(8,128)(2,1)S(1)} all-to-all(bf16[4,3,85,1280]{3,2,1,0:T(8,128)(2,1)} %reshape.67), channel_id=1, replica_groups=mesh['cycle'=8,'bin'=4] {'bin'}, dimensions={0} | all-to-all | bytes 5222400 | tf_op jit(solution)/shard_map/all_to_all | solution.py:63
  57.0 0.2 fusion.13
  57.3 3.9 convolution_bitcast_fusion
  61.2 0.6 copy-done
  62.0 0.7 all_to_all.10
  62.7 3.2 all-to-all-start.1
  66.0 0.6 dynamic-slice
  67.1 3.4 all-to-all-done.1
  70.6 14.8 %all-reduce = f32[24]{0:T(128)S(1)} all-reduce(f32[24]{0:T(128)S(1)} %convert_dynamic-update-slice_fusion), channel_id=4, replica_groups=mesh['cycle'=8,'bin'=4] {'cycle'}, use_global_device_ids=true, to_apply=%add | all-reduce | flops 24 | bytes 192
  85.5 0.4 convert_reduce_fusion
  85.9 29.6 %all-gather.3 = f32[8,3,1280]{2,1,0:T(4,128)S(1)} all-gather(f32[1,3,1280]{2,1,0:T(4,128)S(1)} %bitcast.40), channel_id=3, replica_groups=mesh['cycle'=8,'bin'=4] {'cycle'}, dimensions={0}, use_global_device_ids=true | all-gather | bytes 138240 | tf_op jit(solution)/shard_map/all_gather | solution.py:12
  115.6 284.4 %all-gather.6.cloned.1.call-done = f32[24,640,640]{2,1,0:T(8,128)} async-done(((f32[3,640,640]{2,1,0:T(8,128)}), f32[24,640,640]{2,1,0:T(8,128)}) %all-gather.6.cloned.1.call-update) | async-done | bytes 39321616 | tf_op jit(solution)/shard_map/all_gather | solution.py:12
  400.0 4.9 %slice.59 = f32[3,640,640]{2,1,0:T(8,128)} slice(f32[24,640,640]{2,1,0:T(8,128)} %all-gather.6.cloned.1.call-done), slice={[0:3], [0:640], [0:640]} | slice | bytes 9830400 | tf_op jit(solution)/shard_map/slice | solution.py:13
  404.9 22.9 %slice.61 = f32[21,640,640]{2,1,0:T(8,128)} slice(f32[24,640,640]{2,1,0:T(8,128)} %all-gather.6.cloned.1.call-done), slice={[3:24], [0:640], [0:640]} | slice | bytes 68812800 | tf_op jit(solution)/shard_map/slice | solution.py:14
  427.8 46.4 %while.14 = (s32[]{:T(128)}, f32[3,640,640]{2,1,0:T(8,128)}, f32[3,1280]{1,0:T(4,128)S(1)}, f32[3]{0:T(128)S(1)}, f32[7,3,640,640]{3,2,1,0:T(8,128)}, /*index=5*...) while((s32[]{:T(128)}, f32[3,640,640]{2,1,0:T(8,128)}, f32[3,1280]{1,0:T(4,128)S(1)}, ...), condition=%wide.region_11.12_spmd, body=%wide.region_10.11_spmd.sunk | while | flops 1232645 | bytes 14791821 | solution.py:15
  427.9 6.6 %bitcast_add_fusion.4 = f32[3,640,640]{2,1,0:T(8,128)} fusion(f32[3,640,640]{2,1,0:T(8,128)} %get-tuple-element.122, f32[7,3,640,640]{3,2,1,0:T(8,128)} %get-tuple-element.133, s32[]{:T(128)S(6)} %copy.28), kind=kLoop, calls=%fused_computation.1.clone.1 | loop fusion | flops 1228800 | bytes 14745604 | tf_op jit(solution)/shard_map/while/body/eval_jaxpr/add | solution.py:20
  434.5 6.7 %bitcast_add_fusion.4 = f32[3,640,640]{2,1,0:T(8,128)} fusion(f32[3,640,640]{2,1,0:T(8,128)} %get-tuple-element.122, f32[7,3,640,640]{3,2,1,0:T(8,128)} %get-tuple-element.133, s32[]{:T(128)S(6)} %copy.28), kind=kLoop, calls=%fused_computation.1.clone.1 | loop fusion | flops 1228800 | bytes 14745604 | tf_op jit(solution)/shard_map/while/body/eval_jaxpr/add | solution.py:20
  441.2 6.6 %bitcast_add_fusion.4 = f32[3,640,640]{2,1,0:T(8,128)} fusion(f32[3,640,640]{2,1,0:T(8,128)} %get-tuple-element.122, f32[7,3,640,640]{3,2,1,0:T(8,128)} %get-tuple-element.133, s32[]{:T(128)S(6)} %copy.28), kind=kLoop, calls=%fused_computation.1.clone.1 | loop fusion | flops 1228800 | bytes 14745604 | tf_op jit(solution)/shard_map/while/body/eval_jaxpr/add | solution.py:20
  447.8 6.6 %bitcast_add_fusion.4 = f32[3,640,640]{2,1,0:T(8,128)} fusion(f32[3,640,640]{2,1,0:T(8,128)} %get-tuple-element.122, f32[7,3,640,640]{3,2,1,0:T(8,128)} %get-tuple-element.133, s32[]{:T(128)S(6)} %copy.28), kind=kLoop, calls=%fused_computation.1.clone.1 | loop fusion | flops 1228800 | bytes 14745604 | tf_op jit(solution)/shard_map/while/body/eval_jaxpr/add | solution.py:20
  454.4 6.6 %bitcast_add_fusion.4 = f32[3,640,640]{2,1,0:T(8,128)} fusion(f32[3,640,640]{2,1,0:T(8,128)} %get-tuple-element.122, f32[7,3,640,640]{3,2,1,0:T(8,128)} %get-tuple-element.133, s32[]{:T(128)S(6)} %copy.28), kind=kLoop, calls=%fused_computation.1.clone.1 | loop fusion | flops 1228800 | bytes 14745604 | tf_op jit(solution)/shard_map/while/body/eval_jaxpr/add | solution.py:20
  461.0 6.6 %bitcast_add_fusion.4 = f32[3,640,640]{2,1,0:T(8,128)} fusion(f32[3,640,640]{2,1,0:T(8,128)} %get-tuple-element.122, f32[7,3,640,640]{3,2,1,0:T(8,128)} %get-tuple-element.133, s32[]{:T(128)S(6)} %copy.28), kind=kLoop, calls=%fused_computation.1.clone.1 | loop fusion | flops 1228800 | bytes 14745604 | tf_op jit(solution)/shard_map/while/body/eval_jaxpr/add | solution.py:20
  467.7 6.6 %bitcast_add_fusion.4 = f32[3,640,640]{2,1,0:T(8,128)} fusion(f32[3,640,640]{2,1,0:T(8,128)} %get-tuple-element.122, f32[7,3,640,640]{3,2,1,0:T(8,128)} %get-tuple-element.133, s32[]{:T(128)S(6)} %copy.28), kind=kLoop, calls=%fused_computation.1.clone.1 | loop fusion | flops 1228800 | bytes 14745604 | tf_op jit(solution)/shard_map/while/body/eval_jaxpr/add | solution.py:20
  474.4 2.0 multiply_subtract_fusion
  (37 shorter events, 1.0 us)
Async XLA Ops:
  6.5 393.5 %all-gather.6.cloned.1.call-start = ((), (), s32[]{:S(2)}) async-start(), calls=%async_computation.2 | async-start | bytes 44236800 | tf_op jit(solution)/shard_map/all_gather | solution.py:12
  61.2 0.7 copy-start
  61.2 4.7 copy-start.1
  62.7 7.8 %all-to-all-start.1 = ((s32[4,1,3]{2,1,0:T(1,128)}), s32[4,1,3]{2,1,0:T(1,128)S(1)}, u32[]{:S(2)}, u32[]{:S(2)}) async-start(s32[4,1,3]{2,1,0:T(1,128)} %bitcast.13), calls=%async_computation.1 | async-start | bytes 4096 | tf_op jit(solution)/shard_map/all_to_all | solution.py:64
Sparse Core Ops, SparseCore 0:
  61.3 338.6 all-gather.5
where the time goes:
time: 484 us; the launch traced here: 483 us
  waiting for transfers between devices  288 us (60%)
  blocking collectives  81.6 us (17%)
  other arithmetic  60.3 us (12%)
  local copies, waits for them, and re-layouts  32.4 us (7%)
  between operations  14.1 us (3%)
    all_gather x1, waiting for transfers between devices, combined_all(): pieces = jax.tree.map(lambda part: lax.all_gather(part, axis), value)  284 us
    add x21, other arithmetic, add_tuple(): return jax.tree.map(lambda a, b: a + b, left, right)  46.4 us
    all_to_all x1, blocking collectives, on_device(): lax.all_to_all(sendbuf, 'bin', split_axis=0, concat_axis=0, tiled=True)  37.2 us
    all_gather x1, blocking collectives, combined_all(): pieces = jax.tree.map(lambda part: lax.all_gather(part, axis), value)  29.6 us
    slice x4, local copies, waits for them, and re-layouts, combined_all(): tail = jax.tree.map(lambda part: part[1:], pieces)  23.1 us
    unnamed x1, blocking collectives  14.8 us
  transfers between devices with their start and end apart: 2, of which 2 were waited for; matrix products, arithmetic and copies ran while one was open for 0% of the time, Pallas kernels for 0%

commit v1 on v0

v1 whole, which is shorter than its diff:
```python
import functools

import jax
import jax.numpy as jnp
from jax import lax
from jax.experimental import pallas as pl
from jax.experimental.pallas import tpu as pltpu
from jax.sharding import PartitionSpec as P

C_IASI = 616
C_CRIS = 431
C_ATMS = 22
WIDE = 640
MID = 512
ATMS_AT = 448
SUMS = 8

VMEM = pl.BlockSpec(memory_space=pltpu.VMEM)
SMEM = pl.BlockSpec(memory_space=pltpu.SMEM)
PARAMS = pltpu.CompilerParams(vmem_limit_bytes=48 * 1024 * 1024)


def row_keys(order_ref, tile_ref, me, n_bin, per_owner):
    rows = tile_ref.shape[1]
    tiles = n_bin * per_owner
    padded = -(-tiles // 16) * 16
    place = lax.broadcasted_iota(jnp.int32, (padded, rows), 0)
    wanted = jnp.full((padded, rows), -1, jnp.int32)
    for k in range(n_bin):
        for i in range(per_owner):
            wanted = jnp.where(place == k * per_owner + i, order_ref[(me ^ k) * per_owner + i], wanted)
    hits = wanted == tile_ref[...]
    before = lax.broadcasted_iota(jnp.int32, (rows, rows), 0) < lax.broadcasted_iota(jnp.int32, (rows, rows), 1)
    rank = jnp.dot(
        hits.astype(jnp.float32).astype(jnp.bfloat16),
        before.astype(jnp.float32).astype(jnp.bfloat16),
        preferred_element_type=jnp.float32,
    )
    return jnp.where(hits, rank, -1.0).astype(jnp.int32)


def placing(keys, instrument, n_bin, per_owner, slots):
    slot = lax.broadcasted_iota(jnp.int32, (slots, keys.shape[1]), 0)
    parts = [
        (slot == keys[k * per_owner + instrument : k * per_owner + instrument + 1, :]).astype(jnp.float32)
        for k in range(n_bin)
    ]
    return jnp.concatenate(parts, axis=0).astype(jnp.bfloat16)


def marked(values, limit, one_at):
    lane = lax.broadcasted_iota(jnp.int32, values.shape, 1)
    ones = jnp.where(lane == one_at, 1.0, 0.0)
    return jnp.where(lane < limit, values.astype(jnp.float32), ones).astype(jnp.bfloat16)


def place_wide_kernel(n_bin, per_owner, slots, order_ref, tile_ref, bg_ref, an_ref, *out_refs):
    me = lax.axis_index("bin")
    keys = row_keys(order_ref, tile_ref, me, n_bin, per_owner)
    select = placing(keys, 0, n_bin, per_owner, slots)
    for part, ref in enumerate((bg_ref, an_ref)):
        values = marked(ref[:, :WIDE], C_IASI, WIDE - 1)
        placed = jnp.dot(select, values, preferred_element_type=jnp.float32)
        for k in range(n_bin):
            out_refs[k][:, part * WIDE : (part + 1) * WIDE] = placed[k * slots : (k + 1) * slots].astype(jnp.bfloat16)


def place_mid_kernel(n_bin, per_owner, slots, order_ref, tile_ref, bg_ref, an_ref, *out_refs):
    me = lax.axis_index("bin")
    keys = row_keys(order_ref, tile_ref, me, n_bin, per_owner)
    select_cris = placing(keys, 1, n_bin, per_owner, slots)
    select_atms = placing(keys, 2, n_bin, per_owner, slots)
    shift = ATMS_AT % 128
    for part, ref in enumerate((bg_ref, an_ref)):
        cris = marked(ref[:, :MID], C_CRIS, MID - 1)
        atms = marked(ref[:, :128], C_ATMS, 126 - shift)
        placed = jnp.dot(select_cris, cris, preferred_element_type=jnp.float32)
        aside = jnp.dot(select_atms, atms, preferred_element_type=jnp.float32)
        placed_last = placed[:, MID - 128 :] + pltpu.roll(aside, shift, 1)
        for k in range(n_bin):
            at = slice(k * slots, (k + 1) * slots)
            out_refs[k][:, part * MID : (part + 1) * MID - 128] = placed[at, : MID - 128].astype(jnp.bfloat16)
            out_refs[k][:, (part + 1) * MID - 128 : (part + 1) * MID] = placed_last[at].astype(jnp.bfloat16)


def chunk_order(z):
    return (3 - 3 * (z % 2), 2 - z // 2, (2 * z + 1) % 5, z)


def moment_kernel(lanes, rows_c, n_cycle, n_in, *refs):
    in_refs, out_refs, cross_ref = refs[:n_in], refs[n_in:-1], refs[-1]
    cross = jnp.zeros((lanes, lanes), jnp.float32)
    for ref in in_refs:
        cross = cross + lax.dot_general(
            ref[:, :lanes], ref[:, lanes:], (((0,), (0,)), ((), ())), preferred_element_type=jnp.float32
        )
    cross_ref[:lanes, :] = cross
    if lanes == MID:
        cross_ref[lanes:, :] = jnp.zeros((cross_ref.shape[0] - lanes, lanes), jnp.float32)
        lane = lax.broadcasted_iota(jnp.int32, (24, 128), 1) + (MID - 128)
        moved = (lane >= ATMS_AT) & (lane < MID - 1)
        cross_ref[:24, MID - 128 :] = jnp.where(
            moved, cross_ref[ATMS_AT : ATMS_AT + 24, MID - 128 :], cross_ref[:24, MID - 128 :]
        )
    sums = cross_ref[lanes - SUMS : lanes, :]
    if len(out_refs) == 2:
        cycle = lax.axis_index("cycle")
        z, core = cycle // 2, cycle % 2
        for place, chip in enumerate(chunk_order(z)):
            for out_ref, c in zip(out_refs, (chip * 2 + core, chip * 2 + 1 - core)):
                out_ref[place, :rows_c, :] = cross_ref[pl.ds(pl.multiple_of(c * rows_c, 8), rows_c), :]
                out_ref[place, rows_c:, :] = sums
    else:
        for c in range(n_cycle):
            out_refs[0][c, :rows_c, :] = cross_ref[c * rows_c : (c + 1) * rows_c, :]
            out_refs[0][c, rows_c:, :] = sums


def finish_kernel(rows_c, wide_ref, mid_ref, out_ref):
    row = lax.broadcasted_iota(jnp.int32, (rows_c, WIDE), 0) + lax.axis_index("cycle") * rows_c
    lane = lax.broadcasted_iota(jnp.int32, (rows_c, WIDE), 1)
    last = rows_c + SUMS - 1
    n = wide_ref[last:, WIDE - 1 :]
    mean_bg = wide_ref[:rows_c, WIDE - 1 :] / n
    mean_an = wide_ref[last:, :] / n
    cov = wide_ref[:rows_c, :] / n - mean_bg * mean_an
    out_ref[0] = jnp.where((lane < C_IASI) & (row < C_IASI), cov, 0.0)

    n = mid_ref[last:, MID - 1 :]
    mean_bg = mid_ref[:rows_c, MID - 1 :] / n
    mean_an = mid_ref[last:, :] / n
    cov = mid_ref[:rows_c, :] / n - mean_bg * mean_an
    out_ref[1, :, :MID] = jnp.where((lane < C_CRIS) & (row < C_CRIS), jnp.pad(cov, ((0, 0), (0, WIDE - MID))), 0.0)[:, :MID]
    out_ref[1, :, MID:] = jnp.zeros((rows_c, WIDE - MID), jnp.float32)

    n = mid_ref[last - 1 : last, MID - 2 : MID - 1]
    shift = 128 - ATMS_AT % 128
    mean_bg = mid_ref[:rows_c, MID - 2 : MID - 1] / n
    mean_an = mid_ref[last - 1 : last, MID - 128 :] / n
    cov = pltpu.roll(mid_ref[:rows_c, MID - 128 :] / n - mean_bg * mean_an, shift, 1)
    out_ref[2, :, :128] = jnp.where((lane[:, :128] < C_ATMS) & (row[:, :128] < C_ATMS), cov, 0.0)
    out_ref[2, :, 128:] = jnp.zeros((rows_c, WIDE - 128), jnp.float32)


def to_owners(parts):
    n_bin = len(parts)
    return [parts[0]] + [
        lax.ppermute(parts[k], "bin", [(i, i ^ k) for i in range(n_bin)]) for k in range(1, n_bin)
    ]


def along(pairs):
    return [(2 * a + core, 2 * b + core) for a, b in pairs for core in range(2)]


def scatter_line(mine, other):
    here = [
        mine[p] + lax.ppermute(other[p], "cycle", [(i, i ^ 1) for i in range(8)]) for p in range(4)
    ]
    z = lax.axis_index("cycle") // 2
    outer = (z == 0) | (z == 3)
    r1 = lax.ppermute(here[0], "cycle", along([(0, 1), (1, 0), (2, 3), (3, 2)]))
    r2 = lax.ppermute(here[1], "cycle", along([(0, 1), (3, 2)]))
    r3 = lax.ppermute(here[2], "cycle", along([(0, 1), (3, 2)]))
    r5 = lax.ppermute(here[2] + r1, "cycle", along([(1, 3), (2, 0)]))
    r6 = lax.ppermute(here[1] + r2, "cycle", along([(1, 2), (2, 1)]))
    return here[3] + r3 + r5 + r6 + jnp.where(outer, r1, 0.0)


def on_device(obs_minus_bg, obs_minus_an, tile_of_row, owner_order):
    n_bin = lax.axis_size("bin")
    n_cycle = lax.axis_size("cycle")
    rows, width = obs_minus_bg.shape
    tiles = owner_order.shape[0]
    per_owner = tiles // n_bin
    slots = -(-(2 * rows // tiles) // 8) * 8
    rows_c = width // n_cycle
    tile = tile_of_row.reshape(1, rows)
    totals = []
    for lanes, place_kernel in ((MID, place_mid_kernel), (WIDE, place_wide_kernel)):
        parts = pl.pallas_call(
            functools.partial(place_kernel, n_bin, per_owner, slots),
            out_shape=[jax.ShapeDtypeStruct((slots, 2 * lanes), jnp.bfloat16)] * n_bin,
            in_specs=[SMEM, VMEM, VMEM, VMEM],
            out_specs=[VMEM] * n_bin,
            compiler_params=PARAMS,
        )(owner_order, tile, obs_minus_bg, obs_minus_an)
        parts = to_owners(parts)
        chunk = (rows_c + SUMS, lanes)
        if n_cycle == 8:
            shapes = [jax.ShapeDtypeStruct((4,) + chunk, jnp.float32)] * 2
        else:
            shapes = [jax.ShapeDtypeStruct((n_cycle,) + chunk, jnp.float32)]
        moments = pl.pallas_call(
            functools.partial(moment_kernel, lanes, rows_c, n_cycle, n_bin),
            out_shape=shapes,
            in_specs=[VMEM] * n_bin,
            out_specs=[VMEM] * len(shapes),
            scratch_shapes=[pltpu.VMEM((WIDE, lanes), jnp.float32)],
            compiler_params=PARAMS,
        )(*parts)
        if n_cycle == 8:
            totals.append(scatter_line(*moments))
        else:
            totals.append(lax.psum_scatter(moments[0], "cycle", scatter_dimension=0, tiled=False))
    return pl.pallas_call(
        functools.partial(finish_kernel, rows_c),
        out_shape=jax.ShapeDtypeStruct((per_owner, rows_c, width), jnp.float32),
        in_specs=[VMEM, VMEM],
        out_specs=VMEM,
        compiler_params=PARAMS,
    )(totals[1], totals[0])


def solution(mesh):
    return jax.shard_map(
        on_device,
        mesh=mesh,
        in_specs=(
            P(("cycle", "bin"), None),
            P(("cycle", "bin"), None),
            P(("cycle", "bin"), None),
            P(),
        ),
        out_specs=P("bin", "cycle", None),
        check_vma=False,
    )
```

time: 484 us -> 69.8 us (0.14)
  the two profiles are of different devices: /device:TPU:0 before, /device:TPU:8 now
where the time goes in v1:
time: 69.8 us; the launch traced here: 69.4 us
  starting transfers between devices  32.4 us (46%)
  waiting for transfers between devices  23.6 us (34%)
  Pallas kernels  5.92 us (8%)
  local copies, waits for them, and re-layouts  4.3 us (6%)
  other arithmetic  2.91 us (4%)
    ppermute x2, starting transfers between devices, scatter_line(): r5 = lax.ppermute(here[2] + r1, 'cycle', along([(1, 3), (2, 0)]))  9.57 us
    ppermute x6, waiting for transfers between devices, to_owners(): lax.ppermute(parts[k], 'bin', [(i, i ^ k) for i in range(n_bin)])  9.07 us
    ppermute x6, starting transfers between devices, to_owners(): lax.ppermute(parts[k], 'bin', [(i, i ^ k) for i in range(n_bin)])  8.5 us
    ppermute x2, waiting for transfers between devices, scatter_line(): r1 = lax.ppermute(here[0], 'cycle', along([(0, 1), (1, 0), (2, 3), (3, 2)]))  7.3 us
    ppermute x2, starting transfers between devices, scatter_line(): r6 = lax.ppermute(here[1] + r2, 'cycle', along([(1, 2), (2, 1)]))  5.83 us
    ppermute x2, waiting for transfers between devices, scatter_line(): r3 = lax.ppermute(here[2], 'cycle', along([(0, 1), (3, 2)]))  3.58 us
    unnamed x8, local copies, waits for them, and re-layouts  3.51 us
    pallas_call x2, Pallas kernels, on_device(): pl.pallas_call(functools.partial(place_kernel, n_bin, per_owner, slots),...  2.93 us
  transfers between devices with their start and end apart: 24, of which 9 were waited for; matrix products, arithmetic and copies ran while one was open for 5% of the time, Pallas kernels for 5%

profile of v1, /device:TPU:8, one launch (start us, length us, event | category | flops | bytes accessed | tf_op | source)
XLA Modules:
  0.0 69.4 jit_solution(12742287606236621784)
XLA Ops:
  0.7 1.1 %copy-done = bf16[512,640]{1,0:T(8,128)(2,1)S(1)} copy-done((bf16[512,640]{1,0:T(8,128)(2,1)S(1)}, bf16[512,640]{1,0:T(8,128)(2,1)}, u32[]{:S(2)}) %copy-start) | copy-done | bytes 655384
  1.7 1.1 %copy-done.1 = bf16[512,640]{1,0:T(8,128)(2,1)S(1)} copy-done((bf16[512,640]{1,0:T(8,128)(2,1)S(1)}, bf16[512,640]{1,0:T(8,128)(2,1)}, u32[]{:S(2)}) %copy-start.1) | copy-done | bytes 655384
  3.5 1.5 %shard_map.48 = (bf16[88,1024]{1,0:T(8,128)(2,1)S(1)}, bf16[88,1024]{1,0:T(8,128)(2,1)S(1)}, bf16[88,1024]{1,0:T(8,128)(2,1)S(1)}, bf16[88,1024]{1,0:T(8,128)(2,1)S(1)}) custom-call(s32[12]{0:T(128)S(1)} %copy-done.3, s32[1,512]{1,0:T(1,128)S(1)} %bitcast.51, bf16[512,640]{1,0:T(8,128)(2,1)S(1)} %copy-done, bf16[512,640]{1,0:T(8,128)(2,1)S(1)} %copy-done.1), custom_call_target="tpu_custom_call" | custom-call | tf_op jit(solution)/shard_map/pallas_call | solution.py:181
  5.0 1.5 %collective-permute-start.12 = (bf16[88,1024]{1,0:T(8,128)(2,1)S(1)}, bf16[88,1024]{1,0:T(8,128)(2,1)S(1)}, u32[]{:S(2)}, u32[]{:S(2)}) collective-permute-start(bf16[88,1024]{1,0:T(8,128)(2,1)S(1)} %get-tuple-element.24), channel_id=1, source_target_pairs={{0,1},{1,0},{2,3},{3,2},{4,5},{5,4},{6,7},{7,6},{8,9},{9,8},{10,11... | collective-permute-start | bytes 540680 | tf_op jit(solution)/shard_map/ppermute | solution.py:148
  6.6 1.5 %collective-permute-start.13 = (bf16[88,1024]{1,0:T(8,128)(2,1)S(1)}, bf16[88,1024]{1,0:T(8,128)(2,1)S(1)}, u32[]{:S(2)}, u32[]{:S(2)}) collective-permute-start(bf16[88,1024]{1,0:T(8,128)(2,1)S(1)} %get-tuple-element.25), channel_id=1, source_target_pairs={{0,2},{1,3},{2,0},{3,1},{4,6},{5,7},{6,4},{7,5},{8,10},{9,11},{10,... | collective-permute-start | bytes 540680 | tf_op jit(solution)/shard_map/ppermute | solution.py:148
  8.6 1.4 %shard_map.46 = (bf16[88,1280]{1,0:T(8,128)(2,1)S(1)}, bf16[88,1280]{1,0:T(8,128)(2,1)S(1)}, bf16[88,1280]{1,0:T(8,128)(2,1)S(1)}, bf16[88,1280]{1,0:T(8,128)(2,1)S(1)}) custom-call(s32[12]{0:T(128)S(1)} %copy-done.3, s32[1,512]{1,0:T(1,128)S(1)} %bitcast.52, bf16[512,640]{1,0:T(8,128)(2,1)S(1)} %copy-done, bf16[512,640]{1,0:T(8,128)(2,1)S(1)} %copy-done.1), custom_call_target="tpu_custom_call" | custom-call | tf_op jit(solution)/shard_map/pallas_call | solution.py:181
  10.0 1.5 %collective-permute-start = (bf16[88,1280]{1,0:T(8,128)(2,1)S(1)}, bf16[88,1280]{1,0:T(8,128)(2,1)S(1)}, u32[]{:S(2)}, u32[]{:S(2)}) collective-permute-start(bf16[88,1280]{1,0:T(8,128)(2,1)S(1)} %get-tuple-element.18), channel_id=1, source_target_pairs={{0,1},{1,0},{2,3},{3,2},{4,5},{5,4},{6,7},{7,6},{8,9},{9,8},{10,11... | collective-permute-start | bytes 675848 | tf_op jit(solution)/shard_map/ppermute | solution.py:148
  11.5 1.5 %collective-permute-start.1 = (bf16[88,1280]{1,0:T(8,128)(2,1)S(1)}, bf16[88,1280]{1,0:T(8,128)(2,1)S(1)}, u32[]{:S(2)}, u32[]{:S(2)}) collective-permute-start(bf16[88,1280]{1,0:T(8,128)(2,1)S(1)} %get-tuple-element.19), channel_id=1, source_target_pairs={{0,2},{1,3},{2,0},{3,1},{4,6},{5,7},{6,4},{7,5},{8,10},{9,11},{10,... | collective-permute-start | bytes 675848 | tf_op jit(solution)/shard_map/ppermute | solution.py:148
  13.1 1.9 %collective-permute-start.2 = (bf16[88,1280]{1,0:T(8,128)(2,1)S(1)}, bf16[88,1280]{1,0:T(8,128)(2,1)S(1)}, u32[]{:S(2)}, u32[]{:S(2)}) collective-permute-start(bf16[88,1280]{1,0:T(8,128)(2,1)S(1)} %get-tuple-element.20), channel_id=1, source_target_pairs={{0,3},{1,2},{2,1},{3,0},{4,7},{5,6},{6,5},{7,4},{8,11},{9,10},{10,... | collective-permute-start | bytes 675848 | tf_op jit(solution)/shard_map/ppermute | solution.py:148
  15.0 1.6 %collective-permute-done.13.refs_2_ = bf16[88,1024]{1,0:T(8,128)(2,1)S(1)} collective-permute-done((bf16[88,1024]{1,0:T(8,128)(2,1)S(1)}, bf16[88,1024]{1,0:T(8,128)(2,1)S(1)}, u32[]{:S(2)}, u32[]{:S(2)}) %collective-permute-start.13) | collective-permute-done | bytes 180256 | tf_op jit(solution)/shard_map/ppermute | solution.py:148
  16.6 0.8 %collective-permute-done.14.refs_3_ = bf16[88,1024]{1,0:T(8,128)(2,1)S(1)} collective-permute-done((bf16[88,1024]{1,0:T(8,128)(2,1)S(1)}, bf16[88,1024]{1,0:T(8,128)(2,1)S(1)}, u32[]{:S(2)}, u32[]{:S(2)}) %collective-permute-start.14) | collective-permute-done | bytes 180256 | tf_op jit(solution)/shard_map/ppermute | solution.py:148
  17.4 0.8 %shard_map.49 = (f32[4,88,512]{2,1,0:T(8,128)S(1)}, f32[4,88,512]{2,1,0:T(8,128)S(1)}) custom-call(bf16[88,1024]{1,0:T(8,128)(2,1)S(1)} %get-tuple-element.23.refs_0_, bf16[88,1024]{1,0:T(8,128)(2,1)S(1)} %collective-permute-done.12.refs_1_, bf16[88,1024]{1,0:T(8,128)(2,1)S(1)} %collective-permute-done.13.refs_2_, ...), custom_call_target="tpu_custom_call" | custom-call | tf_op jit(solution)/shard_map/pallas_call | solution.py:194
  19.4 1.8 %collective-permute-done.refs_1_ = bf16[88,1280]{1,0:T(8,128)(2,1)S(1)} collective-permute-done((bf16[88,1280]{1,0:T(8,128)(2,1)S(1)}, bf16[88,1280]{1,0:T(8,128)(2,1)S(1)}, u32[]{:S(2)}, u32[]{:S(2)}) %collective-permute-start) | collective-permute-done | bytes 225312 | tf_op jit(solution)/shard_map/ppermute | solution.py:148
  21.3 4.8 %collective-permute-done.1.refs_2_ = bf16[88,1280]{1,0:T(8,128)(2,1)S(1)} collective-permute-done((bf16[88,1280]{1,0:T(8,128)(2,1)S(1)}, bf16[88,1280]{1,0:T(8,128)(2,1)S(1)}, u32[]{:S(2)}, u32[]{:S(2)}) %collective-permute-start.1) | collective-permute-done | bytes 225312 | tf_op jit(solution)/shard_map/ppermute | solution.py:148
  26.1 1.2 %shard_map.47 = (f32[4,88,640]{2,1,0:T(8,128)S(1)}, f32[4,88,640]{2,1,0:T(8,128)S(1)}) custom-call(bf16[88,1280]{1,0:T(8,128)(2,1)S(1)} %get-tuple-element.17.refs_0_, bf16[88,1280]{1,0:T(8,128)(2,1)S(1)} %collective-permute-done.refs_1_, bf16[88,1280]{1,0:T(8,128)(2,1)S(1)} %collective-permute-done.1.refs_2_, ...), custom_call_target="tpu_custom_call" | custom-call | tf_op jit(solution)/shard_map/pallas_call | solution.py:194
  28.0 0.9 %collective-permute-done.6 = f32[88,640]{1,0:T(8,128)S(1)} collective-permute-done((f32[88,640]{1,0:T(8,128)S(1)}, f32[88,640]{1,0:T(8,128)S(1)}, u32[]{:S(2)}, u32[]{:S(2)}) %collective-permute-start.6) | collective-permute-done | bytes 225312 | tf_op jit(solution)/shard_map/ppermute | solution.py:158
  29.4 1.6 %collective-permute-start.7 = (f32[88,640]{1,0:T(8,128)S(1)}, f32[88,640]{1,0:T(8,128)S(1)}, u32[]{:S(2)}, u32[]{:S(2)}) collective-permute-start(f32[88,640]{1,0:T(8,128)S(1)} %bitcast_add_fusion.1), channel_id=1, source_target_pairs={{0,8},{4,12},{8,0},{12,4},{16,24},{20,28},{24,16},{28,20},{1,9},{5... | collective-permute-start | bytes 675848 | tf_op jit(solution)/shard_map/ppermute | solution.py:162
  31.0 5.3 %collective-permute-done.19 = f32[88,512]{1,0:T(8,128)S(1)} collective-permute-done((f32[88,512]{1,0:T(8,128)S(1)}, f32[88,512]{1,0:T(8,128)S(1)}, u32[]{:S(2)}, u32[]{:S(2)}) %collective-permute-start.19) | collective-permute-done | bytes 180256 | tf_op jit(solution)/shard_map/ppermute | solution.py:162
  36.3 0.8 %fusion.8 = (f32[88,512]{1,0:T(8,128)}, f32[88,512]{1,0:T(8,128)}, f32[88,512]{1,0:T(8,128)S(1)}) fusion(f32[88,512]{1,0:T(8,128)S(1)} %collective-permute-done.19, f32[88,512]{1,0:T(8,128)S(1)} %collective-permute-done.16, f32[4,88,512]{2,1,0:T(8,128)S(1)} %get-tuple-element.27, f32[88,512]{1,0:T(8,128)S(1)} %collective-permute-done.21), kind=kLoop, calls=%fused_computation.24 | loop fusion | flops 135168 | bytes 1441792 | tf_op jit(solution)/shard_map/add | solution.py:165
  37.1 1.3 %collective-permute-start.22 = (f32[88,512]{1,0:T(8,128)S(1)}, f32[88,512]{1,0:T(8,128)S(1)}, u32[]{:S(2)}, u32[]{:S(2)}) collective-permute-start(f32[88,512]{1,0:T(8,128)S(1)} %get-tuple-element.42), channel_id=1, source_target_pairs={{0,8},{4,12},{24,16},{28,20},{1,9},{5,13},{25,17},{29,21},{2,10},{... | collective-permute-start | bytes 540680 | tf_op jit(solution)/shard_map/ppermute | solution.py:163
  38.4 2.0 %collective-permute-done.7 = f32[88,640]{1,0:T(8,128)S(1)} collective-permute-done((f32[88,640]{1,0:T(8,128)S(1)}, f32[88,640]{1,0:T(8,128)S(1)}, u32[]{:S(2)}, u32[]{:S(2)}) %collective-permute-start.7) | collective-permute-done | bytes 225312 | tf_op jit(solution)/shard_map/ppermute | solution.py:162
  40.6 1.3 %collective-permute-start.10 = (f32[88,640]{1,0:T(8,128)S(1)}, f32[88,640]{1,0:T(8,128)S(1)}, u32[]{:S(2)}, u32[]{:S(2)}) collective-permute-start(f32[88,640]{1,0:T(8,128)S(1)} %get-tuple-element.37), channel_id=1, source_target_pairs={{0,8},{4,12},{24,16},{28,20},{1,9},{5,13},{25,17},{29,21},{2,10},{... | collective-permute-start | bytes 675848 | tf_op jit(solution)/shard_map/ppermute | solution.py:163
  41.9 5.6 %collective-permute-start.20 = (f32[88,512]{1,0:T(8,128)}, f32[88,512]{1,0:T(8,128)S(1)}, u32[]{:S(2)}, u32[]{:S(2)}) collective-permute-start(f32[88,512]{1,0:T(8,128)} %get-tuple-element.29), channel_id=1, source_target_pairs={{8,24},{12,28},{16,0},{20,4},{9,25},{13,29},{17,1},{21,5},{10,26},... | collective-permute-start | bytes 540680 | tf_op jit(solution)/shard_map/ppermute | solution.py:165
  47.6 1.3 %collective-permute-start.17 = (f32[88,512]{1,0:T(8,128)}, f32[88,512]{1,0:T(8,128)}, u32[]{:S(2)}, u32[]{:S(2)}) collective-permute-start(f32[88,512]{1,0:T(8,128)} %get-tuple-element.30), channel_id=1, source_target_pairs={{0,8},{4,12},{24,16},{28,20},{1,9},{5,13},{25,17},{29,21},{2,10},{... | collective-permute-start | bytes 540680 | tf_op jit(solution)/shard_map/ppermute | solution.py:164
  49.6 2.3 %collective-permute-start.23 = (f32[88,512]{1,0:T(8,128)}, f32[88,512]{1,0:T(8,128)}, u32[]{:S(2)}, u32[]{:S(2)}) collective-permute-start(f32[88,512]{1,0:T(8,128)} %add.78), channel_id=1, source_target_pairs={{8,16},{12,20},{16,8},{20,12},{9,17},{13,21},{17,9},{21,13},{10,18... | collective-permute-start | bytes 540680 | tf_op jit(solution)/shard_map/ppermute | solution.py:166
  52.1 4.0 %collective-permute-start.8 = (f32[88,640]{1,0:T(8,128)S(1)}, f32[88,640]{1,0:T(8,128)S(1)}, u32[]{:S(2)}, u32[]{:S(2)}) collective-permute-start(f32[88,640]{1,0:T(8,128)S(1)} %get-tuple-element.31), channel_id=1, source_target_pairs={{8,24},{12,28},{16,0},{20,4},{9,25},{13,29},{17,1},{21,5},{10,26},... | collective-permute-start | bytes 675848 | tf_op jit(solution)/shard_map/ppermute | solution.py:165
  56.0 1.3 %collective-permute-start.5 = (f32[88,640]{1,0:T(8,128)S(1)}, f32[88,640]{1,0:T(8,128)S(1)}, u32[]{:S(2)}, u32[]{:S(2)}) collective-permute-start(f32[88,640]{1,0:T(8,128)S(1)} %get-tuple-element.32), channel_id=1, source_target_pairs={{0,8},{4,12},{24,16},{28,20},{1,9},{5,13},{25,17},{29,21},{2,10},{... | collective-permute-start | bytes 675848 | tf_op jit(solution)/shard_map/ppermute | solution.py:164
  57.4 3.5 %collective-permute-start.11 = (f32[88,640]{1,0:T(8,128)S(1)}, f32[88,640]{1,0:T(8,128)S(1)}, u32[]{:S(2)}, u32[]{:S(2)}) collective-permute-start(f32[88,640]{1,0:T(8,128)S(1)} %add.68), channel_id=1, source_target_pairs={{8,16},{12,20},{16,8},{20,12},{9,17},{13,21},{17,9},{21,13},{10,18... | collective-permute-start | bytes 675848 | tf_op jit(solution)/shard_map/ppermute | solution.py:166
  60.9 1.1 %fusion.7.mid_ref = f32[88,512]{1,0:T(8,128)S(1)} fusion(f32[88,512]{1,0:T(8,128)} %collective-permute-done.23, f32[88,512]{1,0:T(8,128)S(1)} %collective-permute-done.20, f32[88,512]{1,0:T(8,128)} %collective-permute-done.17, f32[88,512]{1,0:T(8,128)S(1)} %collective-permute-done.15, f32[88,512]{1,0:T(8,128)S(1)} %collective-permute-done.19, ...), kind=kLoop, calls=%fused_computation.19 | loop fusion | flops 270336 | bytes 1261569 | tf_op jit(solution)/shard_map/add | solution.py:167
  62.0 3.6 %collective-permute-done.5 = f32[88,640]{1,0:T(8,128)S(1)} collective-permute-done((f32[88,640]{1,0:T(8,128)S(1)}, f32[88,640]{1,0:T(8,128)S(1)}, u32[]{:S(2)}, u32[]{:S(2)}) %collective-permute-start.5) | collective-permute-done | bytes 225312 | tf_op jit(solution)/shard_map/ppermute | solution.py:164
  65.6 2.7 %collective-permute-done.11 = f32[88,640]{1,0:T(8,128)S(1)} collective-permute-done((f32[88,640]{1,0:T(8,128)S(1)}, f32[88,640]{1,0:T(8,128)S(1)}, u32[]{:S(2)}, u32[]{:S(2)}) %collective-permute-start.11) | collective-permute-done | bytes 225312 | tf_op jit(solution)/shard_map/ppermute | solution.py:166
  68.4 1.0 %shard_map.50 = f32[3,80,640]{2,1,0:T(8,128)} custom-call(f32[88,640]{1,0:T(8,128)S(1)} %fusion.3.wide_ref, f32[88,512]{1,0:T(8,128)S(1)} %fusion.7.mid_ref), custom_call_target="tpu_custom_call" | custom-call | tf_op jit(solution)/shard_map/pallas_call | solution.py:206
  (39 shorter events, 5.4 us)
Async XLA Ops:
  0.0 0.7 copy-start.3
  0.7 1.1 %copy-start = (bf16[512,640]{1,0:T(8,128)(2,1)S(1)}, bf16[512,640]{1,0:T(8,128)(2,1)}, u32[]{:S(2)}) copy-start(bf16[512,640]{1,0:T(8,128)(2,1)} %bg_ref.3) | copy-start | bytes 1966084
  1.7 1.1 %copy-start.1 = (bf16[512,640]{1,0:T(8,128)(2,1)S(1)}, bf16[512,640]{1,0:T(8,128)(2,1)}, u32[]{:S(2)}) copy-start(bf16[512,640]{1,0:T(8,128)(2,1)} %an_ref.3) | copy-start | bytes 1966084
  2.8 0.7 copy-start.2
  5.0 8.0 %collective-permute-start.12 = (bf16[88,1024]{1,0:T(8,128)(2,1)S(1)}, bf16[88,1024]{1,0:T(8,128)(2,1)S(1)}, u32[]{:S(2)}, u32[]{:S(2)}) collective-permute-start(bf16[88,1024]{1,0:T(8,128)(2,1)S(1)} %get-tuple-element.24), channel_id=1, source_target_pairs={{0,1},{1,0},{2,3},{3,2},{4,5},{5,4},{6,7},{7,6},{8,9},{9,8},{10,11... | collective-permute-start | bytes 540680 | tf_op jit(solution)/shard_map/ppermute | solution.py:148
  6.6 10.0 %collective-permute-start.13 = (bf16[88,1024]{1,0:T(8,128)(2,1)S(1)}, bf16[88,1024]{1,0:T(8,128)(2,1)S(1)}, u32[]{:S(2)}, u32[]{:S(2)}) collective-permute-start(bf16[88,1024]{1,0:T(8,128)(2,1)S(1)} %get-tuple-element.25), channel_id=1, source_target_pairs={{0,2},{1,3},{2,0},{3,1},{4,6},{5,7},{6,4},{7,5},{8,10},{9,11},{10,... | collective-permute-start | bytes 540680 | tf_op jit(solution)/shard_map/ppermute | solution.py:148
  8.1 9.3 %collective-permute-start.14 = (bf16[88,1024]{1,0:T(8,128)(2,1)S(1)}, bf16[88,1024]{1,0:T(8,128)(2,1)S(1)}, u32[]{:S(2)}, u32[]{:S(2)}) collective-permute-start(bf16[88,1024]{1,0:T(8,128)(2,1)S(1)} %get-tuple-element.26), channel_id=1, source_target_pairs={{0,3},{1,2},{2,1},{3,0},{4,7},{5,6},{6,5},{7,4},{8,11},{9,10},{10,... | collective-permute-start | bytes 540680 | tf_op jit(solution)/shard_map/ppermute | solution.py:148
  10.0 11.3 %collective-permute-start = (bf16[88,1280]{1,0:T(8,128)(2,1)S(1)}, bf16[88,1280]{1,0:T(8,128)(2,1)S(1)}, u32[]{:S(2)}, u32[]{:S(2)}) collective-permute-start(bf16[88,1280]{1,0:T(8,128)(2,1)S(1)} %get-tuple-element.18), channel_id=1, source_target_pairs={{0,1},{1,0},{2,3},{3,2},{4,5},{5,4},{6,7},{7,6},{8,9},{9,8},{10,11... | collective-permute-start | bytes 675848 | tf_op jit(solution)/shard_map/ppermute | solution.py:148
  11.5 14.6 %collective-permute-start.1 = (bf16[88,1280]{1,0:T(8,128)(2,1)S(1)}, bf16[88,1280]{1,0:T(8,128)(2,1)S(1)}, u32[]{:S(2)}, u32[]{:S(2)}) collective-permute-start(bf16[88,1280]{1,0:T(8,128)(2,1)S(1)} %get-tuple-element.19), channel_id=1, source_target_pairs={{0,2},{1,3},{2,0},{3,1},{4,6},{5,7},{6,4},{7,5},{8,10},{9,11},{10,... | collective-permute-start | bytes 675848 | tf_op jit(solution)/shard_map/ppermute | solution.py:148
  13.1 13.0 %collective-permute-start.2 = (bf16[88,1280]{1,0:T(8,128)(2,1)S(1)}, bf16[88,1280]{1,0:T(8,128)(2,1)S(1)}, u32[]{:S(2)}, u32[]{:S(2)}) collective-permute-start(bf16[88,1280]{1,0:T(8,128)(2,1)S(1)} %get-tuple-element.20), channel_id=1, source_target_pairs={{0,3},{1,2},{2,1},{3,0},{4,7},{5,6},{6,5},{7,4},{8,11},{9,10},{10,... | collective-permute-start | bytes 675848 | tf_op jit(solution)/shard_map/ppermute | solution.py:148
  18.9 9.0 %collective-permute-start.18 = (f32[88,512]{1,0:T(8,128)S(1)}, f32[88,512]{1,0:T(8,128)S(1)}, u32[]{:S(2)}, u32[]{:S(2)}) collective-permute-start(f32[88,512]{1,0:T(8,128)S(1)} %get-tuple-element.40), channel_id=1, source_target_pairs={{0,4},{4,0},{8,12},{12,8},{16,20},{20,16},{24,28},{28,24},{1,5},{5... | collective-permute-start | bytes 540680 | tf_op jit(solution)/shard_map/ppermute | solution.py:158
  18.9 10.4 %collective-permute-start.16 = (f32[88,512]{1,0:T(8,128)S(1)}, f32[88,512]{1,0:T(8,128)S(1)}, u32[]{:S(2)}, u32[]{:S(2)}) collective-permute-start(f32[88,512]{1,0:T(8,128)S(1)} %get-tuple-element.41), channel_id=1, source_target_pairs={{0,4},{4,0},{8,12},{12,8},{16,20},{20,16},{24,28},{28,24},{1,5},{5... | collective-permute-start | bytes 540680 | tf_op jit(solution)/shard_map/ppermute | solution.py:158
  21.3 9.7 %collective-permute-start.21 = (f32[88,512]{1,0:T(8,128)S(1)}, f32[88,512]{1,0:T(8,128)S(1)}, u32[]{:S(2)}, u32[]{:S(2)}) collective-permute-start(f32[88,512]{1,0:T(8,128)S(1)} %get-tuple-element.39), channel_id=1, source_target_pairs={{0,4},{4,0},{8,12},{12,8},{16,20},{20,16},{24,28},{28,24},{1,5},{5... | collective-permute-start | bytes 540680 | tf_op jit(solution)/shard_map/ppermute | solution.py:158
  27.3 1.5 %collective-permute-start.6 = (f32[88,640]{1,0:T(8,128)S(1)}, f32[88,640]{1,0:T(8,128)S(1)}, u32[]{:S(2)}, u32[]{:S(2)}) collective-permute-start(f32[88,640]{1,0:T(8,128)S(1)} %get-tuple-element.35), channel_id=1, source_target_pairs={{0,4},{4,0},{8,12},{12,8},{16,20},{20,16},{24,28},{28,24},{1,5},{5... | collective-permute-start | bytes 675848 | tf_op jit(solution)/shard_map/ppermute | solution.py:158
  27.4 11.0 %collective-permute-start.4 = (f32[88,640]{1,0:T(8,128)S(1)}, f32[88,640]{1,0:T(8,128)S(1)}, u32[]{:S(2)}, u32[]{:S(2)}) collective-permute-start(f32[88,640]{1,0:T(8,128)S(1)} %get-tuple-element.36), channel_id=1, source_target_pairs={{0,4},{4,0},{8,12},{12,8},{16,20},{20,16},{24,28},{28,24},{1,5},{5... | collective-permute-start | bytes 675848 | tf_op jit(solution)/shard_map/ppermute | solution.py:158
  27.9 10.5 %collective-permute-start.9 = (f32[88,640]{1,0:T(8,128)S(1)}, f32[88,640]{1,0:T(8,128)S(1)}, u32[]{:S(2)}, u32[]{:S(2)}) collective-permute-start(f32[88,640]{1,0:T(8,128)S(1)} %get-tuple-element.34), channel_id=1, source_target_pairs={{0,4},{4,0},{8,12},{12,8},{16,20},{20,16},{24,28},{28,24},{1,5},{5... | collective-permute-start | bytes 675848 | tf_op jit(solution)/shard_map/ppermute | solution.py:158
  28.9 7.4 %collective-permute-start.19 = (f32[88,512]{1,0:T(8,128)S(1)}, f32[88,512]{1,0:T(8,128)S(1)}, u32[]{:S(2)}, u32[]{:S(2)}) collective-permute-start(f32[88,512]{1,0:T(8,128)S(1)} %bitcast_add_fusion.5), channel_id=1, source_target_pairs={{0,8},{4,12},{8,0},{12,4},{16,24},{20,28},{24,16},{28,20},{1,9},{5... | collective-permute-start | bytes 540680 | tf_op jit(solution)/shard_map/ppermute | solution.py:162
  29.4 11.1 %collective-permute-start.7 = (f32[88,640]{1,0:T(8,128)S(1)}, f32[88,640]{1,0:T(8,128)S(1)}, u32[]{:S(2)}, u32[]{:S(2)}) collective-permute-start(f32[88,640]{1,0:T(8,128)S(1)} %bitcast_add_fusion.1), channel_id=1, source_target_pairs={{0,8},{4,12},{8,0},{12,4},{16,24},{20,28},{24,16},{28,20},{1,9},{5... | collective-permute-start | bytes 675848 | tf_op jit(solution)/shard_map/ppermute | solution.py:162
  37.1 11.7 %collective-permute-start.22 = (f32[88,512]{1,0:T(8,128)S(1)}, f32[88,512]{1,0:T(8,128)S(1)}, u32[]{:S(2)}, u32[]{:S(2)}) collective-permute-start(f32[88,512]{1,0:T(8,128)S(1)} %get-tuple-element.42), channel_id=1, source_target_pairs={{0,8},{4,12},{24,16},{28,20},{1,9},{5,13},{25,17},{29,21},{2,10},{... | collective-permute-start | bytes 540680 | tf_op jit(solution)/shard_map/ppermute | solution.py:163
  40.6 11.4 %collective-permute-start.10 = (f32[88,640]{1,0:T(8,128)S(1)}, f32[88,640]{1,0:T(8,128)S(1)}, u32[]{:S(2)}, u32[]{:S(2)}) collective-permute-start(f32[88,640]{1,0:T(8,128)S(1)} %get-tuple-element.37), channel_id=1, source_target_pairs={{0,8},{4,12},{24,16},{28,20},{1,9},{5,13},{25,17},{29,21},{2,10},{... | collective-permute-start | bytes 675848 | tf_op jit(solution)/shard_map/ppermute | solution.py:163
  41.9 10.2 %collective-permute-start.15 = (f32[88,512]{1,0:T(8,128)}, f32[88,512]{1,0:T(8,128)S(1)}, u32[]{:S(2)}, u32[]{:S(2)}) collective-permute-start(f32[88,512]{1,0:T(8,128)} %get-tuple-element.38), channel_id=1, source_target_pairs={{0,4},{4,0},{8,12},{12,8},{16,20},{20,16},{24,28},{28,24},{1,5},{5... | collective-permute-start | bytes 540680 | tf_op jit(solution)/shard_map/ppermute | solution.py:158
  41.9 14.1 %collective-permute-start.20 = (f32[88,512]{1,0:T(8,128)}, f32[88,512]{1,0:T(8,128)S(1)}, u32[]{:S(2)}, u32[]{:S(2)}) collective-permute-start(f32[88,512]{1,0:T(8,128)} %get-tuple-element.29), channel_id=1, source_target_pairs={{8,24},{12,28},{16,0},{20,4},{9,25},{13,29},{17,1},{21,5},{10,26},... | collective-permute-start | bytes 540680 | tf_op jit(solution)/shard_map/ppermute | solution.py:165
  47.6 9.8 %collective-permute-start.17 = (f32[88,512]{1,0:T(8,128)}, f32[88,512]{1,0:T(8,128)}, u32[]{:S(2)}, u32[]{:S(2)}) collective-permute-start(f32[88,512]{1,0:T(8,128)} %get-tuple-element.30), channel_id=1, source_target_pairs={{0,8},{4,12},{24,16},{28,20},{1,9},{5,13},{25,17},{29,21},{2,10},{... | collective-permute-start | bytes 540680 | tf_op jit(solution)/shard_map/ppermute | solution.py:164
  49.6 11.3 %collective-permute-start.23 = (f32[88,512]{1,0:T(8,128)}, f32[88,512]{1,0:T(8,128)}, u32[]{:S(2)}, u32[]{:S(2)}) collective-permute-start(f32[88,512]{1,0:T(8,128)} %add.78), channel_id=1, source_target_pairs={{8,16},{12,20},{16,8},{20,12},{9,17},{13,21},{17,9},{21,13},{10,18... | collective-permute-start | bytes 540680 | tf_op jit(solution)/shard_map/ppermute | solution.py:166
  51.9 10.1 %collective-permute-start.3 = (f32[88,640]{1,0:T(8,128)S(1)}, f32[88,640]{1,0:T(8,128)S(1)}, u32[]{:S(2)}, u32[]{:S(2)}) collective-permute-start(f32[88,640]{1,0:T(8,128)S(1)} %get-tuple-element.33), channel_id=1, source_target_pairs={{0,4},{4,0},{8,12},{12,8},{16,20},{20,16},{24,28},{28,24},{1,5},{5... | collective-permute-start | bytes 675848 | tf_op jit(solution)/shard_map/ppermute | solution.py:158
  52.1 9.9 %collective-permute-start.8 = (f32[88,640]{1,0:T(8,128)S(1)}, f32[88,640]{1,0:T(8,128)S(1)}, u32[]{:S(2)}, u32[]{:S(2)}) collective-permute-start(f32[88,640]{1,0:T(8,128)S(1)} %get-tuple-element.31), channel_id=1, source_target_pairs={{8,24},{12,28},{16,0},{20,4},{9,25},{13,29},{17,1},{21,5},{10,26},... | collective-permute-start | bytes 675848 | tf_op jit(solution)/shard_map/ppermute | solution.py:165
  56.0 9.5 %collective-permute-start.5 = (f32[88,640]{1,0:T(8,128)S(1)}, f32[88,640]{1,0:T(8,128)S(1)}, u32[]{:S(2)}, u32[]{:S(2)}) collective-permute-start(f32[88,640]{1,0:T(8,128)S(1)} %get-tuple-element.32), channel_id=1, source_target_pairs={{0,8},{4,12},{24,16},{28,20},{1,9},{5,13},{25,17},{29,21},{2,10},{... | collective-permute-start | bytes 675848 | tf_op jit(solution)/shard_map/ppermute | solution.py:164
  57.4 11.0 %collective-permute-start.11 = (f32[88,640]{1,0:T(8,128)S(1)}, f32[88,640]{1,0:T(8,128)S(1)}, u32[]{:S(2)}, u32[]{:S(2)}) collective-permute-start(f32[88,640]{1,0:T(8,128)S(1)} %add.68), channel_id=1, source_target_pairs={{8,16},{12,20},{16,8},{20,12},{9,17},{13,21},{17,9},{21,13},{10,18... | collective-permute-start | bytes 675848 | tf_op jit(solution)/shard_map/ppermute | solution.py:166

commit v2 on v1

v2 whole, which is shorter than its diff:
```python
import functools

import jax
import jax.numpy as jnp
from jax import lax
from jax.experimental import pallas as pl
from jax.experimental.pallas import tpu as pltpu
from jax.sharding import PartitionSpec as P

C_IASI = 616
C_CRIS = 431
C_ATMS = 22
WIDE = 640
MID = 512
ATMS_AT = 448
SUMS = 8

VMEM = pl.BlockSpec(memory_space=pltpu.VMEM)
HBM = pl.BlockSpec(memory_space=pltpu.HBM)
ANY = pl.BlockSpec(memory_space=pl.ANY)
FIRST_VMEM = 62 * 1024 * 1024
PARAMS = pltpu.CompilerParams(vmem_limit_bytes=48 * 1024 * 1024)


def row_keys(order_ref, tile_ref, me, n_bin, per_owner):
    rows = tile_ref.shape[1]
    tiles = n_bin * per_owner
    padded = -(-tiles // 16) * 16
    place = lax.broadcasted_iota(jnp.int32, (padded, rows), 0)
    wanted = jnp.full((padded, rows), -1, jnp.int32)
    for k in range(n_bin):
        for i in range(per_owner):
            wanted = jnp.where(place == k * per_owner + i, order_ref[(me ^ k) * per_owner + i], wanted)
    hits = wanted == tile_ref[...]
    before = lax.broadcasted_iota(jnp.int32, (rows, rows), 0) < lax.broadcasted_iota(jnp.int32, (rows, rows), 1)
    rank = jnp.dot(
        hits.astype(jnp.float32).astype(jnp.bfloat16),
        before.astype(jnp.float32).astype(jnp.bfloat16),
        preferred_element_type=jnp.float32,
    )
    return jnp.where(hits, rank, -1.0).astype(jnp.int32)


def placing(keys, instrument, n_bin, per_owner, slots):
    slot = lax.broadcasted_iota(jnp.int32, (slots, keys.shape[1]), 0)
    parts = [
        (slot == keys[k * per_owner + instrument : k * per_owner + instrument + 1, :]).astype(jnp.float32)
        for k in range(n_bin)
    ]
    return jnp.concatenate(parts, axis=0).astype(jnp.bfloat16)


def marked(values, limit, one_at):
    lane = lax.broadcasted_iota(jnp.int32, values.shape, 1)
    ones = jnp.where(lane == one_at, 1.0, 0.0)
    return jnp.where(lane < limit, values.astype(jnp.float32), ones).astype(jnp.bfloat16)


def place_mid_kernel(n_bin, per_owner, slots, order_hbm, tile_hbm, bg_hbm, an_hbm, *refs):
    out_refs, (keys_ref, bg_ref, an_ref, order_ref, tile_ref, sem) = refs[:n_bin], refs[n_bin:]
    copies = [
        pltpu.make_async_copy(source, target, sem.at[i])
        for i, (source, target) in enumerate(
            ((order_hbm, order_ref), (tile_hbm, tile_ref), (bg_hbm, bg_ref), (an_hbm, an_ref))
        )
    ]
    for copy in copies:
        copy.start()
    copies[0].wait()
    copies[1].wait()
    keys = row_keys(order_ref, tile_ref, lax.axis_index("bin"), n_bin, per_owner)
    keys_ref[...] = keys
    select_cris, select_atms = (placing(keys, instrument, n_bin, per_owner, slots) for instrument in (1, 2))
    shift = ATMS_AT % 128
    for part, ref in enumerate((bg_ref, an_ref)):
        copies[2 + part].wait()
        cris = jnp.dot(select_cris, marked(ref[:, :MID], C_CRIS, MID - 1), preferred_element_type=jnp.float32)
        atms = jnp.dot(select_atms, marked(ref[:, :128], C_ATMS, 126 - shift), preferred_element_type=jnp.float32)
        last = pltpu.roll(atms, shift, 1) + cris[:, MID - 128 :]
        first, middle, end = part * MID, (part + 1) * MID - 128, (part + 1) * MID
        for k in range(n_bin):
            at = slice(k * slots, (k + 1) * slots)
            out_refs[k][:, first:middle] = cris[at, : MID - 128].astype(jnp.bfloat16)
            out_refs[k][:, middle:end] = last[at].astype(jnp.bfloat16)


def place_wide_kernel(n_bin, per_owner, slots, keys_ref, bg_ref, an_ref, own_ref, *refs):
    *out_refs, own_out_ref = refs
    own_out_ref[...] = own_ref[...]
    select = placing(keys_ref[...], 0, n_bin, per_owner, slots)
    for part, ref in enumerate((bg_ref, an_ref)):
        placed = jnp.dot(select, marked(ref[...], C_IASI, WIDE - 1), preferred_element_type=jnp.float32)
        for k in range(n_bin):
            out_refs[k][:, part * WIDE : (part + 1) * WIDE] = placed[k * slots : (k + 1) * slots].astype(jnp.bfloat16)


def offset_of(place, n):
    bits = n.bit_length() - 1
    return sum(1 << i for i in range(bits) if not place >> (bits - 1 - i) & 1)


def moment_kernel(lanes, rows_c, n_cycle, n_in, *refs):
    in_refs, out_refs, cross_ref = refs[:n_in], refs[n_in:-1], refs[-1]
    cross = jnp.zeros((lanes, lanes), jnp.float32)
    for ref in in_refs:
        cross = cross + lax.dot_general(
            ref[:, :lanes], ref[:, lanes:], (((0,), (0,)), ((), ())), preferred_element_type=jnp.float32
        )
    cross_ref[:lanes, :] = cross
    if lanes == MID:
        cross_ref[lanes:, :] = jnp.zeros((cross_ref.shape[0] - lanes, lanes), jnp.float32)
        lane = lax.broadcasted_iota(jnp.int32, (24, 128), 1) + (MID - 128)
        moved = (lane >= ATMS_AT) & (lane < MID - 1)
        cross_ref[:24, MID - 128 :] = jnp.where(
            moved, cross_ref[ATMS_AT : ATMS_AT + 24, MID - 128 :], cross_ref[:24, MID - 128 :]
        )
    sums = cross_ref[lanes - SUMS : lanes, :]
    me = lax.axis_index("cycle")
    chunk = rows_c + SUMS
    spans = []
    for out_ref in out_refs:
        start = spans[-1][2] if spans else 0
        spans.append((out_ref, start, start + out_ref.shape[0]))
    for place in range(n_cycle):
        c = me ^ offset_of(place, n_cycle)
        first = pl.multiple_of(c * rows_c, 8)
        for out_ref, start, end in spans:
            low, high = max(start, place * chunk), min(end, place * chunk + rows_c)
            if low < high:
                out_ref[low - start : high - start, :] = cross_ref[pl.ds(first + (low - place * chunk), high - low), :]
            if start <= place * chunk + rows_c < end:
                at = place * chunk + rows_c - start
                out_ref[at : at + SUMS, :] = sums


def finish_kernel(rows_c, wide_a_ref, wide_b_ref, mid_a_ref, mid_b_ref, out_ref):
    row = lax.broadcasted_iota(jnp.int32, (rows_c, WIDE), 0) + lax.axis_index("cycle") * rows_c
    lane = lax.broadcasted_iota(jnp.int32, (rows_c, WIDE), 1)
    last = rows_c + SUMS - 1
    total = wide_a_ref[...] + wide_b_ref[...]
    n = total[last:, WIDE - 1 :]
    cov = total[:rows_c] / n - (total[:rows_c, WIDE - 1 :] / n) * (total[last:] / n)
    out_ref[0] = jnp.where((lane < C_IASI) & (row < C_IASI), cov, 0.0)

    total = mid_a_ref[...] + mid_b_ref[...]
    n = total[last:, MID - 1 :]
    cov = total[:rows_c] / n - (total[:rows_c, MID - 1 :] / n) * (total[last:] / n)
    out_ref[1, :, :MID] = jnp.where((lane[:, :MID] < C_CRIS) & (row[:, :MID] < C_CRIS), cov, 0.0)
    out_ref[1, :, MID:] = jnp.zeros((rows_c, WIDE - MID), jnp.float32)

    n = total[last - 1 : last, MID - 2 : MID - 1]
    cov = total[:rows_c, MID - 128 :] / n - (total[:rows_c, MID - 2 : MID - 1] / n) * (total[last - 1 : last, MID - 128 :] / n)
    cov = pltpu.roll(cov, 128 - ATMS_AT % 128, 1)
    out_ref[2, :, :128] = jnp.where((lane[:, :128] < C_ATMS) & (row[:, :128] < C_ATMS), cov, 0.0)
    out_ref[2, :, 128:] = jnp.zeros((rows_c, WIDE - 128), jnp.float32)


def to_owners(parts):
    n_bin = len(parts)
    return [parts[0]] + [
        lax.ppermute(parts[k], "bin", [(i, i ^ k) for i in range(n_bin)]) for k in range(n_bin - 1, 0, -1)
    ]


def swap(value, bit, n):
    return lax.ppermute(value, "cycle", [(i, i ^ bit) for i in range(n)])


def add_kernel(near_ref, *refs):
    at = 0
    for ref in refs[:-1]:
        end = at + ref.shape[0]
        refs[-1][at:end] = near_ref[at:end] + ref[...]
        at = end


def add_after_kernel(n_after, near_ref, *refs):
    add_kernel(near_ref, *refs[: -1 - n_after], refs[-1])


def on_device(obs_minus_bg, obs_minus_an, tile_of_row, owner_order):
    n_bin = lax.axis_size("bin")
    n_cycle = lax.axis_size("cycle")
    rows, width = obs_minus_bg.shape
    tiles = owner_order.shape[0]
    per_owner = tiles // n_bin
    slots = -(-(2 * rows // tiles) // 8) * 8
    rows_c = width // n_cycle
    tile = tile_of_row.reshape(1, rows)
    padded = -(-tiles // 16) * 16
    *mid, keys, bg, an = pl.pallas_call(
        functools.partial(place_mid_kernel, n_bin, per_owner, slots),
        out_shape=[jax.ShapeDtypeStruct((slots, 2 * MID), jnp.bfloat16)] * n_bin
        + [jax.ShapeDtypeStruct((padded, rows), jnp.int32)]
        + [jax.ShapeDtypeStruct((rows, width), jnp.bfloat16)] * 2,
        in_specs=[HBM] * 4,
        out_specs=[VMEM] * (n_bin + 3),
        scratch_shapes=[
            pltpu.SMEM((tiles,), jnp.int32),
            pltpu.VMEM((1, rows), jnp.int32),
            pltpu.SemaphoreType.DMA((4,)),
        ],
        compiler_params=pltpu.CompilerParams(vmem_limit_bytes=FIRST_VMEM),
    )(owner_order, tile, obs_minus_bg, obs_minus_an)
    *wide, own = pl.pallas_call(
        functools.partial(place_wide_kernel, n_bin, per_owner, slots),
        out_shape=[jax.ShapeDtypeStruct((slots, 2 * WIDE), jnp.bfloat16)] * n_bin
        + [jax.ShapeDtypeStruct((slots, 2 * MID), jnp.bfloat16)],
        in_specs=[VMEM] * 4,
        out_specs=[VMEM] * (n_bin + 1),
        compiler_params=PARAMS,
    )(keys, bg, an, mid[0])

    eighth = n_cycle // 8 * (rows_c + SUMS)

    def moments(lanes, parts, cuts):
        sizes = list(cuts) + [eighth] * 7
        return pl.pallas_call(
            functools.partial(moment_kernel, lanes, rows_c, n_cycle, n_bin),
            out_shape=[jax.ShapeDtypeStruct((size, lanes), jnp.float32) for size in sizes],
            in_specs=[VMEM] * n_bin,
            out_specs=[VMEM] * len(sizes),
            scratch_shapes=[pltpu.VMEM((WIDE, lanes), jnp.float32)],
            compiler_params=PARAMS,
        )(*parts)

    def add(near, *terms, after=()):
        return pl.pallas_call(
            functools.partial(add_after_kernel, len(after)),
            out_shape=jax.ShapeDtypeStruct(near.shape, jnp.float32),
            in_specs=[VMEM] * (1 + len(terms)) + [ANY] * len(after),
            out_specs=VMEM,
            compiler_params=PARAMS,
        )(near, *terms, *after)

    def finer(send, keep, bit):
        while True:
            got = swap(send, bit, n_cycle)
            bit *= 2
            if bit == n_cycle:
                return keep, got
            half = keep.shape[0] // 2
            send, keep = keep[:half] + got[:half], keep[half:] + got[half:]

    mid_got = [own] + to_owners(mid)[1:]
    wide_got = to_owners(wide)
    far_a, far_b, far_c, far_d, near_a, near_b, near_c, near_d = moments(MID, mid_got, (eighth,))
    core_a, core_b, core_c, core_d = (swap(part, 1, n_cycle) for part in (far_a, far_b, far_c, far_d))
    mid_z_a = swap(add(near_a, core_a), 2, n_cycle)
    mid_z_b = swap(add(near_b, core_b), 2, n_cycle)
    mid_send = add(add(near_c, core_c), mid_z_a)
    mid_total = finer(mid_send, add(add(near_d, core_d), mid_z_b), 4)

    cut = eighth * 8 // 11 // 8 * 8
    far_a, far_a2, far_b, far_c, far_d, near_a, near_b, near_c, near_d = moments(
        WIDE, wide_got, (cut, eighth - cut)
    )
    core_a, core_a2, core_b, core_c, core_d = (
        swap(part, 1, n_cycle) for part in (far_a, far_a2, far_b, far_c, far_d)
    )
    wide_z_a = swap(add(near_a, core_a, core_a2, after=(mid_z_a, mid_z_b)), 2, n_cycle)
    wide_z_b = swap(add(near_b, core_b), 2, n_cycle)
    wide_send = add(add(near_c, core_c), wide_z_a, after=mid_total[1:])
    wide_keep = add(add(near_d, core_d), wide_z_b)
    wide_total = finer(wide_send, wide_keep, 4)
    return pl.pallas_call(
        functools.partial(finish_kernel, rows_c),
        out_shape=jax.ShapeDtypeStruct((per_owner, rows_c, width), jnp.float32),
        in_specs=[VMEM] * 4,
        out_specs=VMEM,
        compiler_params=PARAMS,
    )(*wide_total, *mid_total)


def solution(mesh):
    return jax.shard_map(
        on_device,
        mesh=mesh,
        in_specs=(
            P(("cycle", "bin"), None),
            P(("cycle", "bin"), None),
            P(("cycle", "bin"), None),
            P(),
        ),
        out_specs=P("bin", "cycle", None),
        check_vma=False,
    )
```

time: 69.8 us -> 54.9 us (0.79)
  the two profiles are of different devices: /device:TPU:8 before, /device:TPU:0 now
where the time goes in v2:
time: 54.9 us; the launch traced here: 54.6 us
  waiting for transfers between devices  24 us (44%)
  starting transfers between devices  19.4 us (35%)
  Pallas kernels  7.16 us (13%)
  local copies, waits for them, and re-layouts  3.85 us (7%)
    ppermute x15, waiting for transfers between devices, swap(): return lax.ppermute(value, 'cycle', [(i, i ^ bit) for i in range(n)])  18.7 us
    ppermute x15, starting transfers between devices, swap(): return lax.ppermute(value, 'cycle', [(i, i ^ bit) for i in range(n)])  11.3 us
    ppermute x6, starting transfers between devices, to_owners(): lax.ppermute(parts[k], 'bin', [(i, i ^ k) for i in range(n_bin)])  8.16 us
    ppermute x6, waiting for transfers between devices, to_owners(): lax.ppermute(parts[k], 'bin', [(i, i ^ k) for i in range(n_bin)])  5.3 us
    unnamed x8, local copies, waits for them, and re-layouts  3.85 us
    pallas_call x1, Pallas kernels, on_device(): pl.pallas_call(functools.partial(place_mid_kernel, n_bin, per_owner, slot...  3.11 us
    pallas_call x2, Pallas kernels, moments(): pl.pallas_call(functools.partial(moment_kernel, lanes, rows_c, n_cycle, n...  1.97 us
  transfers between devices with their start and end apart: 21, of which 13 were waited for; matrix products, arithmetic and copies ran while one was open for 0% of the time, Pallas kernels for 6%

profile of v2, /device:TPU:0, one launch (start us, length us, event | category | flops | bytes accessed | tf_op | source)
XLA Modules:
  0.0 54.6 jit_solution(966607356724239357)
XLA Ops:
  0.0 3.1 %shard_map.46 = (bf16[88,1024]{1,0:T(8,128)(2,1)}, bf16[88,1024]{1,0:T(8,128)(2,1)}, bf16[88,1024]{1,0:T(8,128)(2,1)}, bf16[88,1024]{1,0:T(8,128)(2,1)}, s32[16,...) custom-call(s32[12]{0:T(128)} %order_hbm.1, s32[1,512]{1,0:T(1,128)} %bitcast.1, ...), custom_call_target="tpu_custom_call" | custom-call | tf_op jit(solution)/shard_map/pallas_call | solution.py:191
  3.1 4.0 %collective-permute-start.9 = (bf16[88,1024]{1,0:T(8,128)(2,1)}, bf16[88,1024]{1,0:T(8,128)(2,1)S(1)}, u32[]{:S(2)}, u32[]{:S(2)}) collective-permute-start(bf16[88,1024]{1,0:T(8,128)(2,1)} %get-tuple-element.52), channel_id=1, source_target_pairs={{0,3},{1,2},{2,1},{3,0},{4,7},{5,6},{6,5},{7,4},{8,11},{9,10},{10,... | collective-permute-start | bytes 540680 | tf_op jit(solution)/shard_map/ppermute | solution.py:161
  7.1 0.5 collective-permute-start.10
  7.7 1.1 %copy-done = bf16[512,640]{1,0:T(8,128)(2,1)S(1)} copy-done((bf16[512,640]{1,0:T(8,128)(2,1)S(1)}, bf16[512,640]{1,0:T(8,128)(2,1)}, u32[]{:S(2)}) %copy-start) | copy-done | bytes 655384
  8.8 1.1 %copy-done.1 = bf16[512,640]{1,0:T(8,128)(2,1)S(1)} copy-done((bf16[512,640]{1,0:T(8,128)(2,1)S(1)}, bf16[512,640]{1,0:T(8,128)(2,1)}, u32[]{:S(2)}) %copy-start.1) | copy-done | bytes 655384
  9.9 0.9 %copy-done.2 = bf16[88,1024]{1,0:T(8,128)(2,1)S(1)} copy-done((bf16[88,1024]{1,0:T(8,128)(2,1)S(1)}, bf16[88,1024]{1,0:T(8,128)(2,1)}, u32[]{:S(2)}) %copy-start.2) | copy-done | bytes 180248
  10.8 0.8 %copy-done.3 = s32[16,512]{1,0:T(8,128)S(1)} copy-done((s32[16,512]{1,0:T(8,128)S(1)}, s32[16,512]{1,0:T(8,128)}, u32[]{:S(2)}) %copy-start.3) | copy-done | bytes 32792
  11.6 0.7 %shard_map.47 = (bf16[88,1280]{1,0:T(8,128)(2,1)S(1)}, bf16[88,1280]{1,0:T(8,128)(2,1)S(1)}, bf16[88,1280]{1,0:T(8,128)(2,1)S(1)}, bf16[88,1280]{1,0:T(8,128)(2,1)S(1)}, bf16[88,1024]{1,0:T(8,128)(2,1)S(1)}) custom-call(s32[16,512]{1,0:T(8,128)S(1)} %copy-done.3, bf16[512,640]{1,0:T(8,128)(2,1)S(1)} %copy-done, bf16[512,640]{1,0:T(8,128)(2,1)S(1)} %copy-done.1, ...), custom_call_target="tpu_custom_call" | custom-call | tf_op jit(solution)/shard_map/pallas_call | solution.py:205
  12.3 2.9 %collective-permute-start = (bf16[88,1280]{1,0:T(8,128)(2,1)S(1)}, bf16[88,1280]{1,0:T(8,128)(2,1)S(1)}, u32[]{:S(2)}, u32[]{:S(2)}) collective-permute-start(bf16[88,1280]{1,0:T(8,128)(2,1)S(1)} %get-tuple-element.39), channel_id=1, source_target_pairs={{0,3},{1,2},{2,1},{3,0},{4,7},{5,6},{6,5},{7,4},{8,11},{9,10},{10,... | collective-permute-start | bytes 675848 | tf_op jit(solution)/shard_map/ppermute | solution.py:161
  15.2 0.5 collective-permute-start.1
  16.2 0.4 collective-permute-done.11.refs_3_
  16.6 0.8 %shard_map.53 = (f32[88,512]{1,0:T(8,128)S(1)}, f32[88,512]{1,0:T(8,128)S(1)}, f32[88,512]{1,0:T(8,128)S(1)}, f32[88,512]{1,0:T(8,128)S(1)}, f32[88,512]{1,0:T(8...) custom-call(bf16[88,1024]{1,0:T(8,128)(2,1)S(1)} %get-tuple-element.51.refs_0_, ...), custom_call_target="tpu_custom_call" | custom-call | tf_op jit(solution)/shard_map/pallas_call | solution.py:218
  17.5 0.5 collective-permute-start.14
  18.0 0.9 %collective-permute-done.12.refs_0_ = f32[88,512]{1,0:T(8,128)S(1)} collective-permute-done((f32[88,512]{1,0:T(8,128)S(1)}, f32[88,512]{1,0:T(8,128)S(1)}, u32[]{:S(2)}, u32[]{:S(2)}) %collective-permute-start.12) | collective-permute-done | bytes 180256 | tf_op jit(solution)/shard_map/ppermute | solution.py:166
  18.9 1.6 %collective-permute-start.13 = (f32[88,512]{1,0:T(8,128)S(1)}, f32[88,512]{1,0:T(8,128)S(1)}, u32[]{:S(2)}, u32[]{:S(2)}) collective-permute-start(f32[88,512]{1,0:T(8,128)S(1)} %shard_map.54), channel_id=1, source_target_pairs={{0,8},{4,12},{8,0},{12,4},{16,24},{20,28},{24,16},{28,20},{1,9},{5... | collective-permute-start | bytes 540680 | tf_op jit(solution)/shard_map/ppermute | solution.py:166
  20.6 0.5 collective-permute-start.15
  21.1 0.7 %collective-permute-done.refs_1_ = bf16[88,1280]{1,0:T(8,128)(2,1)S(1)} collective-permute-done((bf16[88,1280]{1,0:T(8,128)(2,1)S(1)}, bf16[88,1280]{1,0:T(8,128)(2,1)S(1)}, u32[]{:S(2)}, u32[]{:S(2)}) %collective-permute-start) | collective-permute-done | bytes 225312 | tf_op jit(solution)/shard_map/ppermute | solution.py:161
  21.8 3.6 %collective-permute-done.1.refs_2_ = bf16[88,1280]{1,0:T(8,128)(2,1)S(1)} collective-permute-done((bf16[88,1280]{1,0:T(8,128)(2,1)S(1)}, bf16[88,1280]{1,0:T(8,128)(2,1)S(1)}, u32[]{:S(2)}, u32[]{:S(2)}) %collective-permute-start.1) | collective-permute-done | bytes 225312 | tf_op jit(solution)/shard_map/ppermute | solution.py:161
  25.4 0.3 collective-permute-done.2.refs_3_
  25.7 1.2 %shard_map.48 = (f32[64,640]{1,0:T(8,128)S(1)}, f32[24,640]{1,0:T(8,128)S(1)}, f32[88,640]{1,0:T(8,128)S(1)}, f32[88,640]{1,0:T(8,128)S(1)}, f32[88,640]{1,0:T(8...) custom-call(bf16[88,1280]{1,0:T(8,128)(2,1)S(1)} %get-tuple-element.38, ...), custom_call_target="tpu_custom_call" | custom-call | tf_op jit(solution)/shard_map/pallas_call | solution.py:218
  26.9 0.5 collective-permute-start.17
  27.5 1.2 %collective-permute-done.8.refs_1_ = f32[24,640]{1,0:T(8,128)S(1)} collective-permute-done((f32[24,640]{1,0:T(8,128)S(1)}, f32[24,640]{1,0:T(8,128)S(1)}, u32[]{:S(2)}, u32[]{:S(2)}) %collective-permute-start.8) | collective-permute-done | bytes 61472 | tf_op jit(solution)/shard_map/ppermute | solution.py:166
  29.5 1.6 %collective-permute-start.16 = (f32[88,640]{1,0:T(8,128)S(1)}, f32[88,640]{1,0:T(8,128)S(1)}, u32[]{:S(2)}, u32[]{:S(2)}) collective-permute-start(f32[88,640]{1,0:T(8,128)S(1)} %shard_map.56), channel_id=1, source_target_pairs={{0,8},{4,12},{8,0},{12,4},{16,24},{20,28},{24,16},{28,20},{1,9},{5... | collective-permute-start | bytes 675848 | tf_op jit(solution)/shard_map/ppermute | solution.py:166
  31.2 2.7 %collective-permute-start.18 = (f32[88,512]{1,0:T(8,128)S(1)}, f32[88,512]{1,0:T(8,128)S(1)}, u32[]{:S(2)}, u32[]{:S(2)}) collective-permute-start(f32[88,512]{1,0:T(8,128)S(1)} %shard_map.58), channel_id=1, source_target_pairs={{0,16},{4,20},{8,24},{12,28},{16,0},{20,4},{24,8},{28,12},{1,17},{... | collective-permute-start | bytes 540680 | tf_op jit(solution)/shard_map/ppermute | solution.py:166
  33.9 0.5 collective-permute-start.5
  34.4 6.5 %collective-permute-done.18.refs_1_.mid_b_ref = f32[88,512]{1,0:T(8,128)S(1)} collective-permute-done((f32[88,512]{1,0:T(8,128)S(1)}, f32[88,512]{1,0:T(8,128)S(1)}, u32[]{:S(2)}, u32[]{:S(2)}) %collective-permute-start.18) | collective-permute-done | bytes 180256 | tf_op jit(solution)/shard_map/ppermute | solution.py:166
  40.9 0.9 %collective-permute-done.16.refs_0_ = f32[88,640]{1,0:T(8,128)S(1)} collective-permute-done((f32[88,640]{1,0:T(8,128)S(1)}, f32[88,640]{1,0:T(8,128)S(1)}, u32[]{:S(2)}, u32[]{:S(2)}) %collective-permute-start.16) | collective-permute-done | bytes 225312 | tf_op jit(solution)/shard_map/ppermute | solution.py:166
  41.8 2.6 %collective-permute-start.19 = (f32[88,640]{1,0:T(8,128)S(1)}, f32[88,640]{1,0:T(8,128)S(1)}, u32[]{:S(2)}, u32[]{:S(2)}) collective-permute-start(f32[88,640]{1,0:T(8,128)S(1)} %shard_map.59), channel_id=1, source_target_pairs={{0,16},{4,20},{8,24},{12,28},{16,0},{20,4},{24,8},{28,12},{1,17},{... | collective-permute-start | bytes 675848 | tf_op jit(solution)/shard_map/ppermute | solution.py:166
  44.4 1.4 %collective-permute-done.20.refs_0_ = f32[88,512]{1,0:T(8,128)S(1)} collective-permute-done((f32[88,512]{1,0:T(8,128)S(1)}, f32[88,512]{1,0:T(8,128)S(1)}, u32[]{:S(2)}, u32[]{:S(2)}) %collective-permute-start.20) | collective-permute-done | bytes 180256 | tf_op jit(solution)/shard_map/ppermute | solution.py:166
  45.9 3.6 %collective-permute-done.5.refs_0_ = f32[88,640]{1,0:T(8,128)S(1)} collective-permute-done((f32[88,640]{1,0:T(8,128)S(1)}, f32[88,640]{1,0:T(8,128)S(1)}, u32[]{:S(2)}, u32[]{:S(2)}) %collective-permute-start.5) | collective-permute-done | bytes 225312 | tf_op jit(solution)/shard_map/ppermute | solution.py:166
  49.6 4.0 %collective-permute-done.19.wide_b_ref = f32[88,640]{1,0:T(8,128)S(1)} collective-permute-done((f32[88,640]{1,0:T(8,128)S(1)}, f32[88,640]{1,0:T(8,128)S(1)}, u32[]{:S(2)}, u32[]{:S(2)}) %collective-permute-start.19) | collective-permute-done | bytes 225312 | tf_op jit(solution)/shard_map/ppermute | solution.py:166
  53.6 1.0 %shard_map.62 = f32[3,80,640]{2,1,0:T(8,128)} custom-call(f32[88,640]{1,0:T(8,128)S(1)} %shard_map.51.wide_a_ref, f32[88,640]{1,0:T(8,128)S(1)} %collective-permute-done.19.wide_b_ref, f32[88,512]{1,0:T(8,128)S(1)} %shard_map.61.mid_a_ref, f32[88,512]{1,0:T(8,128)S(1)} %collective-permute-done.18.refs_1_.mid_b_ref), custom_call_target="tpu_custom_call" | custom-call | tf_op jit(solution)/shard_map/pallas_call | solution.py:266
  (35 shorter events, 1.9 us)
Async XLA Ops:
  3.1 12.6 %collective-permute-start.9 = (bf16[88,1024]{1,0:T(8,128)(2,1)}, bf16[88,1024]{1,0:T(8,128)(2,1)S(1)}, u32[]{:S(2)}, u32[]{:S(2)}) collective-permute-start(bf16[88,1024]{1,0:T(8,128)(2,1)} %get-tuple-element.52), channel_id=1, source_target_pairs={{0,3},{1,2},{2,1},{3,0},{4,7},{5,6},{6,5},{7,4},{8,11},{9,10},{10,... | collective-permute-start | bytes 540680 | tf_op jit(solution)/shard_map/ppermute | solution.py:161
  7.1 9.1 %collective-permute-start.10 = (bf16[88,1024]{1,0:T(8,128)(2,1)}, bf16[88,1024]{1,0:T(8,128)(2,1)S(1)}, u32[]{:S(2)}, u32[]{:S(2)}) collective-permute-start(bf16[88,1024]{1,0:T(8,128)(2,1)} %get-tuple-element.53), channel_id=1, source_target_pairs={{0,2},{1,3},{2,0},{3,1},{4,6},{5,7},{6,4},{7,5},{8,10},{9,11},{10,... | collective-permute-start | bytes 540680 | tf_op jit(solution)/shard_map/ppermute | solution.py:161
  7.6 9.0 %collective-permute-start.11 = (bf16[88,1024]{1,0:T(8,128)(2,1)}, bf16[88,1024]{1,0:T(8,128)(2,1)S(1)}, u32[]{:S(2)}, u32[]{:S(2)}) collective-permute-start(bf16[88,1024]{1,0:T(8,128)(2,1)} %get-tuple-element.54), channel_id=1, source_target_pairs={{0,1},{1,0},{2,3},{3,2},{4,5},{5,4},{6,7},{7,6},{8,9},{9,8},{10,11... | collective-permute-start | bytes 540680 | tf_op jit(solution)/shard_map/ppermute | solution.py:161
  7.7 1.1 %copy-start = (bf16[512,640]{1,0:T(8,128)(2,1)S(1)}, bf16[512,640]{1,0:T(8,128)(2,1)}, u32[]{:S(2)}) copy-start(bf16[512,640]{1,0:T(8,128)(2,1)} %get-tuple-element.35.bg_ref) | copy-start | bytes 1966084
  8.8 1.1 %copy-start.1 = (bf16[512,640]{1,0:T(8,128)(2,1)S(1)}, bf16[512,640]{1,0:T(8,128)(2,1)}, u32[]{:S(2)}) copy-start(bf16[512,640]{1,0:T(8,128)(2,1)} %get-tuple-element.36.an_ref) | copy-start | bytes 1966084
  9.9 0.9 %copy-start.2 = (bf16[88,1024]{1,0:T(8,128)(2,1)S(1)}, bf16[88,1024]{1,0:T(8,128)(2,1)}, u32[]{:S(2)}) copy-start(bf16[88,1024]{1,0:T(8,128)(2,1)} %get-tuple-element.37.own_ref) | copy-start | bytes 540676
  10.8 0.8 %copy-start.3 = (s32[16,512]{1,0:T(8,128)S(1)}, s32[16,512]{1,0:T(8,128)}, u32[]{:S(2)}) copy-start(s32[16,512]{1,0:T(8,128)} %get-tuple-element.34.keys_ref) | copy-start | bytes 98308
  12.3 9.5 %collective-permute-start = (bf16[88,1280]{1,0:T(8,128)(2,1)S(1)}, bf16[88,1280]{1,0:T(8,128)(2,1)S(1)}, u32[]{:S(2)}, u32[]{:S(2)}) collective-permute-start(bf16[88,1280]{1,0:T(8,128)(2,1)S(1)} %get-tuple-element.39), channel_id=1, source_target_pairs={{0,3},{1,2},{2,1},{3,0},{4,7},{5,6},{6,5},{7,4},{8,11},{9,10},{10,... | collective-permute-start | bytes 675848 | tf_op jit(solution)/shard_map/ppermute | solution.py:161
  15.2 10.1 %collective-permute-start.1 = (bf16[88,1280]{1,0:T(8,128)(2,1)S(1)}, bf16[88,1280]{1,0:T(8,128)(2,1)S(1)}, u32[]{:S(2)}, u32[]{:S(2)}) collective-permute-start(bf16[88,1280]{1,0:T(8,128)(2,1)S(1)} %get-tuple-element.40), channel_id=1, source_target_pairs={{0,2},{1,3},{2,0},{3,1},{4,6},{5,7},{6,4},{7,5},{8,10},{9,11},{10,... | collective-permute-start | bytes 675848 | tf_op jit(solution)/shard_map/ppermute | solution.py:161
  15.7 10.0 %collective-permute-start.2 = (bf16[88,1280]{1,0:T(8,128)(2,1)S(1)}, bf16[88,1280]{1,0:T(8,128)(2,1)S(1)}, u32[]{:S(2)}, u32[]{:S(2)}) collective-permute-start(bf16[88,1280]{1,0:T(8,128)(2,1)S(1)} %get-tuple-element.41), channel_id=1, source_target_pairs={{0,1},{1,0},{2,3},{3,2},{4,5},{5,4},{6,7},{7,6},{8,9},{9,8},{10,11... | collective-permute-start | bytes 675848 | tf_op jit(solution)/shard_map/ppermute | solution.py:161
  17.4 1.5 %collective-permute-start.12 = (f32[88,512]{1,0:T(8,128)S(1)}, f32[88,512]{1,0:T(8,128)S(1)}, u32[]{:S(2)}, u32[]{:S(2)}) collective-permute-start(f32[88,512]{1,0:T(8,128)S(1)} %get-tuple-element.56), channel_id=1, source_target_pairs={{0,4},{4,0},{8,12},{12,8},{16,20},{20,16},{24,28},{28,24},{1,5},{5... | collective-permute-start | bytes 540680 | tf_op jit(solution)/shard_map/ppermute | solution.py:166
  17.5 3.1 %collective-permute-start.14 = (f32[88,512]{1,0:T(8,128)S(1)}, f32[88,512]{1,0:T(8,128)S(1)}, u32[]{:S(2)}, u32[]{:S(2)}) collective-permute-start(f32[88,512]{1,0:T(8,128)S(1)} %get-tuple-element.58), channel_id=1, source_target_pairs={{0,4},{4,0},{8,12},{12,8},{16,20},{20,16},{24,28},{28,24},{1,5},{5... | collective-permute-start | bytes 540680 | tf_op jit(solution)/shard_map/ppermute | solution.py:166
  18.9 10.3 %collective-permute-start.13 = (f32[88,512]{1,0:T(8,128)S(1)}, f32[88,512]{1,0:T(8,128)S(1)}, u32[]{:S(2)}, u32[]{:S(2)}) collective-permute-start(f32[88,512]{1,0:T(8,128)S(1)} %shard_map.54), channel_id=1, source_target_pairs={{0,8},{4,12},{8,0},{12,4},{16,24},{20,28},{24,16},{28,20},{1,9},{5... | collective-permute-start | bytes 540680 | tf_op jit(solution)/shard_map/ppermute | solution.py:166
  20.6 8.9 %collective-permute-start.15 = (f32[88,512]{1,0:T(8,128)S(1)}, f32[88,512]{1,0:T(8,128)S(1)}, u32[]{:S(2)}, u32[]{:S(2)}) collective-permute-start(f32[88,512]{1,0:T(8,128)S(1)} %shard_map.55), channel_id=1, source_target_pairs={{0,8},{4,12},{8,0},{12,4},{16,24},{20,28},{24,16},{28,20},{1,9},{5... | collective-permute-start | bytes 540680 | tf_op jit(solution)/shard_map/ppermute | solution.py:166
  26.9 2.1 %collective-permute-start.7 = (f32[64,640]{1,0:T(8,128)S(1)}, f32[64,640]{1,0:T(8,128)S(1)}, u32[]{:S(2)}, u32[]{:S(2)}) collective-permute-start(f32[64,640]{1,0:T(8,128)S(1)} %get-tuple-element.49), channel_id=1, source_target_pairs={{0,4},{4,0},{8,12},{12,8},{16,20},{20,16},{24,28},{28,24},{1,5},{5... | collective-permute-start | bytes 491528 | tf_op jit(solution)/shard_map/ppermute | solution.py:166
  26.9 4.2 %collective-permute-start.17 = (f32[88,512]{1,0:T(8,128)S(1)}, f32[88,512]{1,0:T(8,128)S(1)}, u32[]{:S(2)}, u32[]{:S(2)}) collective-permute-start(f32[88,512]{1,0:T(8,128)S(1)} %get-tuple-element.60), channel_id=1, source_target_pairs={{0,4},{4,0},{8,12},{12,8},{16,20},{20,16},{24,28},{28,24},{1,5},{5... | collective-permute-start | bytes 540680 | tf_op jit(solution)/shard_map/ppermute | solution.py:166
  27.4 1.2 %collective-permute-start.8 = (f32[24,640]{1,0:T(8,128)S(1)}, f32[24,640]{1,0:T(8,128)S(1)}, u32[]{:S(2)}, u32[]{:S(2)}) collective-permute-start(f32[24,640]{1,0:T(8,128)S(1)} %get-tuple-element.50), channel_id=1, source_target_pairs={{0,4},{4,0},{8,12},{12,8},{16,20},{20,16},{24,28},{28,24},{1,5},{5... | collective-permute-start | bytes 184328 | tf_op jit(solution)/shard_map/ppermute | solution.py:166
  28.7 5.2 %collective-permute-start.4 = (f32[88,640]{1,0:T(8,128)S(1)}, f32[88,640]{1,0:T(8,128)S(1)}, u32[]{:S(2)}, u32[]{:S(2)}) collective-permute-start(f32[88,640]{1,0:T(8,128)S(1)} %get-tuple-element.45), channel_id=1, source_target_pairs={{0,4},{4,0},{8,12},{12,8},{16,20},{20,16},{24,28},{28,24},{1,5},{5... | collective-permute-start | bytes 675848 | tf_op jit(solution)/shard_map/ppermute | solution.py:166
  28.9 5.4 %collective-permute-start.6 = (f32[88,640]{1,0:T(8,128)S(1)}, f32[88,640]{1,0:T(8,128)S(1)}, u32[]{:S(2)}, u32[]{:S(2)}) collective-permute-start(f32[88,640]{1,0:T(8,128)S(1)} %get-tuple-element.47), channel_id=1, source_target_pairs={{0,4},{4,0},{8,12},{12,8},{16,20},{20,16},{24,28},{28,24},{1,5},{5... | collective-permute-start | bytes 675848 | tf_op jit(solution)/shard_map/ppermute | solution.py:166
  29.5 12.3 %collective-permute-start.16 = (f32[88,640]{1,0:T(8,128)S(1)}, f32[88,640]{1,0:T(8,128)S(1)}, u32[]{:S(2)}, u32[]{:S(2)}) collective-permute-start(f32[88,640]{1,0:T(8,128)S(1)} %shard_map.56), channel_id=1, source_target_pairs={{0,8},{4,12},{8,0},{12,4},{16,24},{20,28},{24,16},{28,20},{1,9},{5... | collective-permute-start | bytes 675848 | tf_op jit(solution)/shard_map/ppermute | solution.py:166
  31.2 9.7 %collective-permute-start.18 = (f32[88,512]{1,0:T(8,128)S(1)}, f32[88,512]{1,0:T(8,128)S(1)}, u32[]{:S(2)}, u32[]{:S(2)}) collective-permute-start(f32[88,512]{1,0:T(8,128)S(1)} %shard_map.58), channel_id=1, source_target_pairs={{0,16},{4,20},{8,24},{12,28},{16,0},{20,4},{24,8},{28,12},{1,17},{... | collective-permute-start | bytes 540680 | tf_op jit(solution)/shard_map/ppermute | solution.py:166
  33.8 12.0 %collective-permute-start.3 = (f32[88,640]{1,0:T(8,128)S(1)}, f32[88,640]{1,0:T(8,128)S(1)}, u32[]{:S(2)}, u32[]{:S(2)}) collective-permute-start(f32[88,640]{1,0:T(8,128)S(1)} %get-tuple-element.43), channel_id=1, source_target_pairs={{0,4},{4,0},{8,12},{12,8},{16,20},{20,16},{24,28},{28,24},{1,5},{5... | collective-permute-start | bytes 675848 | tf_op jit(solution)/shard_map/ppermute | solution.py:166
  33.9 15.7 %collective-permute-start.5 = (f32[88,640]{1,0:T(8,128)S(1)}, f32[88,640]{1,0:T(8,128)S(1)}, u32[]{:S(2)}, u32[]{:S(2)}) collective-permute-start(f32[88,640]{1,0:T(8,128)S(1)} %shard_map.50), channel_id=1, source_target_pairs={{0,8},{4,12},{8,0},{12,4},{16,24},{20,28},{24,16},{28,20},{1,9},{5... | collective-permute-start | bytes 675848 | tf_op jit(solution)/shard_map/ppermute | solution.py:166
  41.8 11.8 %collective-permute-start.19 = (f32[88,640]{1,0:T(8,128)S(1)}, f32[88,640]{1,0:T(8,128)S(1)}, u32[]{:S(2)}, u32[]{:S(2)}) collective-permute-start(f32[88,640]{1,0:T(8,128)S(1)} %shard_map.59), channel_id=1, source_target_pairs={{0,16},{4,20},{8,24},{12,28},{16,0},{20,4},{24,8},{28,12},{1,17},{... | collective-permute-start | bytes 675848 | tf_op jit(solution)/shard_map/ppermute | solution.py:166
  44.4 1.4 %collective-permute-start.20 = (f32[88,512]{1,0:T(8,128)S(1)}, f32[88,512]{1,0:T(8,128)S(1)}, u32[]{:S(2)}, u32[]{:S(2)}) collective-permute-start(f32[88,512]{1,0:T(8,128)S(1)} %get-tuple-element.62), channel_id=1, source_target_pairs={{0,4},{4,0},{8,12},{12,8},{16,20},{20,16},{24,28},{28,24},{1,5},{5... | collective-permute-start | bytes 540680 | tf_op jit(solution)/shard_map/ppermute | solution.py:166

commit v3 on v2

v3 whole, which is shorter than its diff:
```python
import functools

import jax
import jax.numpy as jnp
from jax import lax
from jax.experimental import pallas as pl
from jax.experimental.pallas import tpu as pltpu
from jax.sharding import PartitionSpec as P

C_IASI = 616
C_CRIS = 431
C_ATMS = 22
WIDE = 640
ATMS_AT = 616
MID = 512
CRIS_ONE = 431
CRIS_AN = 432
CRIS_COLUMNS = 384
CRIS_SLOT = CRIS_COLUMNS + MID
SUMS = 8

VMEM = pl.BlockSpec(memory_space=pltpu.VMEM)
HBM = pl.BlockSpec(memory_space=pltpu.HBM)
ANY = pl.BlockSpec(memory_space=pl.ANY)
PARAMS = pltpu.CompilerParams(vmem_limit_bytes=48 * 1024 * 1024)


CFG = {'first': 'M', 'order': {'F': (3, 2, 1), 'S': (1, 3, 2)}, 'core': {'F': (48, 88, 168), 'S': (64, 128, 144, 168, 208, 216)}, 'z1': {'F': (88, 128), 'S': (88,)}, 'z2': {'F': (), 'S': (40,)}, 'after': {('z1', 'S', 0): (('z1', 'F', 0),), ('z1', 'F', 2): (('z2', 'F', 0),), ('keep', 'F'): (('z1', 'F', 0),)}}


def row_keys(order_ref, tile_ref, me, n_bin, per_owner):
    rows = tile_ref.shape[1]
    tiles = n_bin * per_owner
    padded = -(-tiles // 16) * 16
    place = lax.broadcasted_iota(jnp.int32, (padded, rows), 0)
    wanted = jnp.full((padded, rows), -1, jnp.int32)
    for k in range(n_bin):
        for i in range(per_owner):
            wanted = jnp.where(place == k * per_owner + i, order_ref[(me ^ k) * per_owner + i], wanted)
    hits = wanted == tile_ref[...]
    before = lax.broadcasted_iota(jnp.int32, (rows, rows), 0) < lax.broadcasted_iota(jnp.int32, (rows, rows), 1)
    rank = jnp.dot(
        hits.astype(jnp.float32).astype(jnp.bfloat16),
        before.astype(jnp.float32).astype(jnp.bfloat16),
        preferred_element_type=jnp.float32,
    )
    return jnp.where(hits, rank, -1.0).astype(jnp.int32)


def placing(keys, instrument, n_bin, per_owner, slots):
    slot = lax.broadcasted_iota(jnp.int32, (slots, keys.shape[1]), 0)
    parts = [
        (slot == keys[k * per_owner + instrument : k * per_owner + instrument + 1, :]).astype(jnp.float32)
        for k in range(n_bin)
    ]
    return jnp.concatenate(parts, axis=0).astype(jnp.bfloat16)


def marked(values, limit, one_at):
    lane = lax.broadcasted_iota(jnp.int32, values.shape, 1)
    ones = jnp.where(lane == one_at, 1.0, 0.0)
    return jnp.where(lane < limit, values.astype(jnp.float32), ones).astype(jnp.bfloat16)


def place_wide(keys, out_refs, part, values, n_bin, per_owner, slots):
    iasi, atms = (placing(keys, instrument, n_bin, per_owner, slots) for instrument in (0, 2))
    placed = jnp.dot(iasi, marked(values, C_IASI, WIDE - 1), preferred_element_type=jnp.float32)
    aside = jnp.dot(atms, marked(values[:, :128], C_ATMS, C_ATMS), preferred_element_type=jnp.float32)
    last = placed[:, WIDE - 128 :] + pltpu.roll(aside, ATMS_AT % 128, 1)
    first, middle, end = part * WIDE, (part + 1) * WIDE - 128, (part + 1) * WIDE
    for k in range(n_bin):
        at = slice(k * slots, (k + 1) * slots)
        out_refs[k][:, first:middle] = placed[at, : WIDE - 128].astype(jnp.bfloat16)
        out_refs[k][:, middle:end] = last[at].astype(jnp.bfloat16)


def place_mid(keys, out_refs, part, values, n_bin, per_owner, slots):
    cris = placing(keys, 1, n_bin, per_owner, slots)
    placed = jnp.dot(cris, marked(values[:, :MID], C_CRIS, CRIS_ONE), preferred_element_type=jnp.float32)
    if part == 1:
        placed = pltpu.roll(placed, CRIS_AN - CRIS_COLUMNS, 1)
    for k in range(n_bin):
        rows = placed[k * slots : (k + 1) * slots]
        if part == 0:
            out_refs[k][:, :MID] = rows.astype(jnp.bfloat16)
        else:
            shared = out_refs[k][:, CRIS_COLUMNS:MID].astype(jnp.float32) + rows[:, : MID - CRIS_COLUMNS]
            out_refs[k][:, CRIS_COLUMNS:MID] = shared.astype(jnp.bfloat16)
            out_refs[k][:, MID:] = rows[:, MID - CRIS_COLUMNS :].astype(jnp.bfloat16)


def first_place_kernel(place, sizes, order_hbm, tile_hbm, bg_hbm, an_hbm, *refs):
    n_bin = sizes[0]
    out_refs, (keys_ref, bg_ref, an_ref, order_ref, tile_ref, sem) = refs[:n_bin], refs[n_bin:]
    copies = [
        pltpu.make_async_copy(source, target, sem.at[i])
        for i, (source, target) in enumerate(
            ((order_hbm, order_ref), (tile_hbm, tile_ref), (bg_hbm, bg_ref), (an_hbm, an_ref))
        )
    ]
    for copy in copies:
        copy.start()
    copies[0].wait()
    copies[1].wait()
    keys = row_keys(order_ref, tile_ref, lax.axis_index("bin"), *sizes[:2])
    keys_ref[...] = keys
    for part, ref in enumerate((bg_ref, an_ref)):
        copies[2 + part].wait()
        place(keys, out_refs, part, ref[...], *sizes)


def second_place_kernel(place, sizes, keys_ref, bg_ref, an_ref, *out_refs):
    for part, ref in enumerate((bg_ref, an_ref)):
        place(keys_ref[...], out_refs, part, ref[...], *sizes)


def offset_of(place, n):
    bits = n.bit_length() - 1
    return sum(1 << i for i in range(bits) if not place >> (bits - 1 - i) & 1)


def moment_kernel(lanes, rows_c, n_cycle, n_in, n_after, *refs):
    in_refs, out_refs, cross_ref = refs[:n_in], refs[n_in + n_after : -1], refs[-1]
    columns, sums_end = (WIDE, WIDE) if lanes == WIDE else (CRIS_COLUMNS, CRIS_ONE + 1)
    cross = jnp.zeros((lanes, lanes), jnp.float32)
    for ref in in_refs:
        cross = cross + lax.dot_general(
            ref[:, :lanes],
            ref[:, columns : columns + lanes],
            (((0,), (0,)), ((), ())),
            preferred_element_type=jnp.float32,
        )
    cross_ref[:lanes, :] = cross
    if lanes == WIDE:
        lane = lax.broadcasted_iota(jnp.int32, (WIDE - ATMS_AT, 128), 1) + (WIDE - 128)
        cross_ref[: WIDE - ATMS_AT, WIDE - 128 :] = jnp.where(
            (lane >= ATMS_AT) & (lane < WIDE - 1),
            cross_ref[ATMS_AT:, WIDE - 128 :],
            cross_ref[: WIDE - ATMS_AT, WIDE - 128 :],
        )
    else:
        cross_ref[lanes:, :] = jnp.zeros((cross_ref.shape[0] - lanes, lanes), jnp.float32)
    sums = cross_ref[sums_end - SUMS : sums_end, :]
    me = lax.axis_index("cycle")
    segments, end = [], 0
    for place in range(n_cycle):
        segments.append((place, end, end + rows_c))
        end += rows_c
        if place % (n_cycle // 4) == n_cycle // 8 - 1:
            segments.append((None, end, end + SUMS))
            end += SUMS
    start = 0
    for out_ref in out_refs:
        end = start + out_ref.shape[0]
        for place, first, last in segments:
            low, high = max(start, first), min(end, last)
            if low < high:
                if place is None:
                    rows = sums[low - first : high - first]
                else:
                    row = (me ^ offset_of(place, n_cycle)) * rows_c + (low - first)
                    rows = cross_ref[pl.ds(pl.multiple_of(row, 8), high - low), :]
                out_ref[low - start : high - start, :] = rows
        start = end


def finish_kernel(rows_c, n_wide, n_mid, *refs):
    wide_keep_ref, wide_send_ref, *wide_got = refs[: 2 + n_wide]
    mid_keep_ref, mid_send_ref, *mid_got = refs[2 + n_wide : -1]
    out_ref = refs[-1]
    wide_got = jnp.concatenate([ref[...] for ref in wide_got])
    mid_got = jnp.concatenate([ref[...] for ref in mid_got])
    row = lax.broadcasted_iota(jnp.int32, (rows_c, WIDE), 0) + lax.axis_index("cycle") * rows_c
    lane = lax.broadcasted_iota(jnp.int32, (rows_c, WIDE), 1)
    total = wide_keep_ref[...] + wide_got[:rows_c]
    sums = wide_send_ref[wide_send_ref.shape[0] - SUMS :] + wide_got[rows_c:]

    def covariance(total, one, sums):
        n = sums[:, one : one + 1]
        return total / n - (total[:, one : one + 1] / n) * (sums / n)

    cov = covariance(total, WIDE - 1, sums[SUMS - 1 :])
    out_ref[0] = jnp.where((lane < C_IASI) & (row < C_IASI), cov, 0.0)
    cov = covariance(total[:, WIDE - 128 :], 126, sums[SUMS - 2 : SUMS - 1, WIDE - 128 :])
    cov = pltpu.roll(cov, 128 - ATMS_AT % 128, 1)
    out_ref[2, :, :128] = jnp.where((lane[:, :128] < C_ATMS) & (row[:, :128] < C_ATMS), cov, 0.0)
    out_ref[2, :, 128:] = jnp.zeros((rows_c, WIDE - 128), jnp.float32)

    total = mid_keep_ref[...] + mid_got[:rows_c]
    sums = mid_send_ref[mid_send_ref.shape[0] - SUMS :] + mid_got[rows_c:]
    cov = covariance(total, CRIS_AN - CRIS_COLUMNS + CRIS_ONE, sums[SUMS - 1 :])
    cov = pltpu.roll(cov, MID - (CRIS_AN - CRIS_COLUMNS), 1)
    out_ref[1, :, :MID] = jnp.where((lane[:, :MID] < C_CRIS) & (row[:, :MID] < C_CRIS), cov, 0.0)
    out_ref[1, :, MID:] = jnp.zeros((rows_c, WIDE - MID), jnp.float32)


def to_owners(parts, order):
    n_bin = len(parts)
    return [parts[0]] + [
        lax.ppermute(parts[k], "bin", [(i, i ^ k) for i in range(n_bin)])
        for k in (order if n_bin == 4 else range(n_bin - 1, 0, -1))
    ]


def swap(value, bit, n):
    return lax.ppermute(value, "cycle", [(i, i ^ bit) for i in range(n)])


def sum_kernel(first, spans, n_after, near_ref, *refs):
    out_ref = refs[-1]
    rows = out_ref.shape[0]
    out_ref[...] = near_ref[first : first + rows]
    for ref, start in zip(refs[: len(spans)], spans):
        low, high = max(first, start), min(first + rows, start + ref.shape[0])
        out_ref[low - first : high - first] += ref[low - start : high - start]


def on_device(obs_minus_bg, obs_minus_an, tile_of_row, owner_order):
    n_bin = lax.axis_size("bin")
    n_cycle = lax.axis_size("cycle")
    rows, width = obs_minus_bg.shape
    tiles = owner_order.shape[0]
    per_owner = tiles // n_bin
    slots = -(-(2 * rows // tiles) // 8) * 8
    rows_c = width // n_cycle
    tile = tile_of_row.reshape(1, rows)
    padded = -(-tiles // 16) * 16
    sizes = (n_bin, per_owner, slots)
    cfg = CFG
    lanes = {"F": MID, "S": WIDE} if cfg["first"] == "M" else {"F": WIDE, "S": MID}
    places = {MID: place_mid, WIDE: place_wide}

    def slot_shapes(p):
        return [jax.ShapeDtypeStruct((slots, 2 * WIDE if lanes[p] == WIDE else CRIS_SLOT), jnp.bfloat16)] * n_bin

    *first, keys, bg, an = pl.pallas_call(
        functools.partial(first_place_kernel, places[lanes["F"]], sizes),
        out_shape=slot_shapes("F")
        + [jax.ShapeDtypeStruct((padded, rows), jnp.int32)]
        + [jax.ShapeDtypeStruct((rows, width), jnp.bfloat16)] * 2,
        in_specs=[HBM] * 4,
        out_specs=[VMEM] * (n_bin + 3),
        scratch_shapes=[
            pltpu.SMEM((tiles,), jnp.int32),
            pltpu.VMEM((1, rows), jnp.int32),
            pltpu.SemaphoreType.DMA((4,)),
        ],
        compiler_params=PARAMS,
    )(*(pltpu.with_memory_space_constraint(x, pltpu.HBM) for x in (owner_order, tile, obs_minus_bg, obs_minus_an)))
    second = pl.pallas_call(
        functools.partial(second_place_kernel, places[lanes["S"]], sizes),
        out_shape=slot_shapes("S"),
        in_specs=[VMEM] * 3,
        out_specs=[VMEM] * n_bin,
        compiler_params=PARAMS,
    )(keys, bg, an)
    owned = {"F": to_owners(first, cfg["order"]["F"]), "S": to_owners(second, cfg["order"]["S"])}

    kept = n_cycle // 8 * rows_c
    sent = kept + SUMS
    half = 2 * (sent + kept)

    def bounds(cuts, end):
        return list(zip([0, *cuts], [*cuts, end]))

    core_spans = {p: bounds(cfg["core"][p], half) for p in "FS"}
    z1_spans = {p: bounds(cfg["z1"][p], sent + kept) for p in "FS"}
    z2_spans = {p: bounds(cfg["z2"][p], sent) for p in "FS"}
    memo, busy = {}, set()

    def get(name):
        if name not in memo:
            assert name not in busy
            busy.add(name)
            memo[name] = make(*name)
            busy.discard(name)
        return memo[name]

    def after(*name):
        return [get(n) for n in cfg["after"].get(name, ())]

    def overlapping(kind, p, spans, low, high, shift=0):
        hits = [(i, start + shift) for i, (start, end) in enumerate(spans) if start + shift < high and low < end + shift]
        return [get((kind, p, i)) for i, _ in hits], [start for _, start in hits]

    def summed(p, low, high, z1, waits):
        terms, starts = overlapping("core", p, core_spans[p], low, high)
        if z1:
            more, more_starts = overlapping("z1", p, z1_spans[p], low, high, sent + kept)
            terms, starts = terms + more, starts + more_starts
        return pl.pallas_call(
            functools.partial(sum_kernel, low, starts, len(waits)),
            out_shape=jax.ShapeDtypeStruct((high - low, lanes[p]), jnp.float32),
            in_specs=[VMEM] * (1 + len(terms)) + [ANY] * len(waits),
            out_specs=VMEM,
            compiler_params=PARAMS,
        )(get(("moments", p))[-1], *terms, *waits)

    def make(kind, p, i=None):
        if kind == "moments":
            waits = after(kind, p)
            shapes = [end - start for start, end in core_spans[p]] + [half]
            return pl.pallas_call(
                functools.partial(moment_kernel, lanes[p], rows_c, n_cycle, n_bin, len(waits)),
                out_shape=[jax.ShapeDtypeStruct((size, lanes[p]), jnp.float32) for size in shapes],
                in_specs=[VMEM] * n_bin + [ANY] * len(waits),
                out_specs=[VMEM] * len(shapes),
                scratch_shapes=[pltpu.VMEM((WIDE, lanes[p]), jnp.float32)],
                compiler_params=PARAMS,
            )(*owned[p], *waits)
        if kind == "got":
            return owned[p][i]
        if kind == "core":
            return swap(get(("moments", p))[i], 1, n_cycle)
        if kind == "z1":
            low, high = z1_spans[p][i]
            return swap(summed(p, low, high, False, after(kind, p, i)), 2, n_cycle)
        if kind == "send":
            low, high = z2_spans[p][i]
            return summed(p, low + sent + kept, high + sent + kept, True, after(kind, p, i))
        if kind == "z2":
            return swap(get(("send", p, i)), 4, n_cycle)
        if kind == "keep":
            return summed(p, half - kept, half, True, after(kind, p))

    def ends(p):
        n = len(z2_spans[p])
        keep, send, got = get(("keep", p)), get(("send", p, n - 1)), [get(("z2", p, i)) for i in range(n)]
        bit = 8
        while bit < n_cycle:
            got = jnp.concatenate(got)
            part = keep.shape[0] // 2
            send = jnp.concatenate([keep[:part] + got[:part], send[-SUMS:] + got[-SUMS:]])
            keep, got = keep[part:] + got[part:-SUMS], [swap(send, bit, n_cycle)]
            bit *= 2
        return [keep, send, *got]

    wide, mid = (ends(p) for p in sorted("FS", key=lambda p: -lanes[p]))
    return pl.pallas_call(
        functools.partial(finish_kernel, rows_c, len(wide) - 2, len(mid) - 2),
        out_shape=jax.ShapeDtypeStruct((per_owner, rows_c, width), jnp.float32),
        in_specs=[VMEM] * (len(wide) + len(mid)),
        out_specs=VMEM,
        compiler_params=PARAMS,
    )(*wide, *mid)


def solution(mesh):
    return jax.shard_map(
        on_device,
        mesh=mesh,
        in_specs=(
            P(("cycle", "bin"), None),
            P(("cycle", "bin"), None),
            P(("cycle", "bin"), None),
            P(),
        ),
        out_specs=P("bin", "cycle", None),
        check_vma=False,
    )
```

time: 54.9 us -> 51.6 us (0.940)
  starting transfers between devices: 19.4 us -> 24.1 us
  local copies, waits for them, and re-layouts: 3.85 us -> 0 us
  waiting for transfers between devices: 24 us -> 21 us
  Pallas kernels: 7.16 us -> 6.25 us
    ppermute x15 -> x19, waiting for transfers between devices: 18.7 us -> 14.9 us  [swap(): return lax.ppermute(value, 'cycle', [(i, i ^ bit) for i in range(n)])]
    unnamed x8 -> x0, local copies, waits for them, and re-layouts: 3.85 us -> none
    ppermute x15 -> x19, starting transfers between devices: 11.3 us -> 14.2 us  [swap(): return lax.ppermute(value, 'cycle', [(i, i ^ bit) for i in range(n)])]
    ppermute x6, starting transfers between devices: 8.16 us -> 9.93 us  [to_owners(): lax.ppermute(parts[k], 'bin', [(i, i ^ k) for i in range(n_bin)])]
    pallas_call x17 -> x15, Pallas kernels: 7.16 us -> 6.25 us  [the longest x1 1.97 us: on_device(): pl.pallas_call(functools.partial(first_place_kernel, places[lanes['F']],...]
    ppermute x6, waiting for transfers between devices: 5.3 us -> 6.11 us  [to_owners(): lax.ppermute(parts[k], 'bin', [(i, i ^ k) for i in range(n_bin)])]
  transfers between devices with their start and end apart: 21 -> 25, of which waited for: 13 -> 13; matrix products, arithmetic and copies ran while one was open for 0% -> 0% of each run, Pallas kernels for 6% -> 6%
where the time goes in v3:
time: 51.6 us; the launch traced here: 51.5 us
  starting transfers between devices  24.1 us (47%)
  waiting for transfers between devices  21 us (41%)
  Pallas kernels  6.25 us (12%)
    ppermute x19, waiting for transfers between devices, swap(): return lax.ppermute(value, 'cycle', [(i, i ^ bit) for i in range(n)])  14.9 us
    ppermute x19, starting transfers between devices, swap(): return lax.ppermute(value, 'cycle', [(i, i ^ bit) for i in range(n)])  14.2 us
    ppermute x6, starting transfers between devices, to_owners(): lax.ppermute(parts[k], 'bin', [(i, i ^ k) for i in range(n_bin)])  9.93 us
    ppermute x6, waiting for transfers between devices, to_owners(): lax.ppermute(parts[k], 'bin', [(i, i ^ k) for i in range(n_bin)])  6.11 us
    pallas_call x1, Pallas kernels, on_device(): pl.pallas_call(functools.partial(first_place_kernel, places[lanes['F']],...  1.97 us
    pallas_call x2, Pallas kernels, make(): pl.pallas_call(functools.partial(moment_kernel, lanes[p], rows_c, n_cycle...  1.96 us
    pallas_call x1, Pallas kernels, on_device(): pl.pallas_call(functools.partial(finish_kernel, rows_c, len(wide) - 2, le...  1.08 us
  transfers between devices with their start and end apart: 25, of which 13 were waited for; matrix products, arithmetic and copies ran while one was open for 0% of the time, Pallas kernels for 6%

profile of v3, /device:TPU:0, one launch (start us, length us, event | category | flops | bytes accessed | tf_op | source)
XLA Modules:
  0.0 51.5 jit_solution(4310402785126039195)
XLA Ops:
  0.0 2.0 %shard_map.46 = (bf16[88,896]{1,0:T(8,128)(2,1)S(1)}, bf16[88,896]{1,0:T(8,128)(2,1)S(1)}, bf16[88,896]{1,0:T(8,128)(2,1)S(1)}, bf16[88,896]{1,0:T(8,128)(2,1)S(...) custom-call(s32[12]{0:T(128)} %order_hbm.1, s32[1,512]{1,0:T(1,128)} %bitcast.1, ...), custom_call_target="tpu_custom_call" | custom-call | tf_op jit(solution)/shard_map/pallas_call | solution.py:236
  2.0 4.0 %collective-permute-start.10 = (bf16[88,896]{1,0:T(8,128)(2,1)S(1)}, bf16[88,896]{1,0:T(8,128)(2,1)S(1)}, u32[]{:S(2)}, u32[]{:S(2)}) collective-permute-start(bf16[88,896]{1,0:T(8,128)(2,1)S(1)} %get-tuple-element.44), channel_id=1, source_target_pairs={{0,3},{1,2},{2,1},{3,0},{4,7},{5,6},{6,5},{7,4},{8,11},{9,10},{10,... | collective-permute-start | bytes 473096 | tf_op jit(solution)/shard_map/ppermute | solution.py:200
  5.9 0.5 collective-permute-start.11
  6.6 1.0 %shard_map.47 = (bf16[88,1280]{1,0:T(8,128)(2,1)S(1)}, bf16[88,1280]{1,0:T(8,128)(2,1)S(1)}, bf16[88,1280]{1,0:T(8,128)(2,1)S(1)}, bf16[88,1280]{1,0:T(8,128)(2,1)S(1)}) custom-call(s32[16,512]{1,0:T(8,128)S(1)} %get-tuple-element.29.keys_ref, bf16[512,640]{1,0:T(8,128)(2,1)S(1)} %get-tuple-element.30.bg_ref, bf16[512,640]{1,0:T(8,128)(2,1)S(1)} %get-tuple-element.31.an_ref), custom_call_target="tpu_custom_call" | custom-call | tf_op jit(solution)/shard_map/pallas_call | solution.py:250
  7.6 2.0 %collective-permute-start = (bf16[88,1280]{1,0:T(8,128)(2,1)S(1)}, bf16[88,1280]{1,0:T(8,128)(2,1)S(1)}, u32[]{:S(2)}, u32[]{:S(2)}) collective-permute-start(bf16[88,1280]{1,0:T(8,128)(2,1)S(1)} %get-tuple-element.33), channel_id=1, source_target_pairs={{0,1},{1,0},{2,3},{3,2},{4,5},{5,4},{6,7},{7,6},{8,9},{9,8},{10,11... | collective-permute-start | bytes 675848 | tf_op jit(solution)/shard_map/ppermute | solution.py:200
  9.5 1.5 %collective-permute-start.1 = (bf16[88,1280]{1,0:T(8,128)(2,1)S(1)}, bf16[88,1280]{1,0:T(8,128)(2,1)S(1)}, u32[]{:S(2)}, u32[]{:S(2)}) collective-permute-start(bf16[88,1280]{1,0:T(8,128)(2,1)S(1)} %get-tuple-element.34), channel_id=1, source_target_pairs={{0,3},{1,2},{2,1},{3,0},{4,7},{5,6},{6,5},{7,4},{8,11},{9,10},{10,... | collective-permute-start | bytes 675848 | tf_op jit(solution)/shard_map/ppermute | solution.py:200
  11.0 1.9 %collective-permute-start.2 = (bf16[88,1280]{1,0:T(8,128)(2,1)S(1)}, bf16[88,1280]{1,0:T(8,128)(2,1)S(1)}, u32[]{:S(2)}, u32[]{:S(2)}) collective-permute-start(bf16[88,1280]{1,0:T(8,128)(2,1)S(1)} %get-tuple-element.35), channel_id=1, source_target_pairs={{0,2},{1,3},{2,0},{3,1},{4,6},{5,7},{6,4},{7,5},{8,10},{9,11},{10,... | collective-permute-start | bytes 675848 | tf_op jit(solution)/shard_map/ppermute | solution.py:200
  12.9 0.6 %collective-permute-done.11.refs_2_ = bf16[88,896]{1,0:T(8,128)(2,1)S(1)} collective-permute-done((bf16[88,896]{1,0:T(8,128)(2,1)S(1)}, bf16[88,896]{1,0:T(8,128)(2,1)S(1)}, u32[]{:S(2)}, u32[]{:S(2)}) %collective-permute-start.11) | collective-permute-done | bytes 157728 | tf_op jit(solution)/shard_map/ppermute | solution.py:200
  13.5 1.3 %collective-permute-done.12.refs_3_ = bf16[88,896]{1,0:T(8,128)(2,1)S(1)} collective-permute-done((bf16[88,896]{1,0:T(8,128)(2,1)S(1)}, bf16[88,896]{1,0:T(8,128)(2,1)S(1)}, u32[]{:S(2)}, u32[]{:S(2)}) %collective-permute-start.12) | collective-permute-done | bytes 157728 | tf_op jit(solution)/shard_map/ppermute | solution.py:200
  14.8 0.8 %shard_map.51 = (f32[48,512]{1,0:T(8,128)S(1)}, f32[40,512]{1,0:T(8,128)S(1)}, f32[80,512]{1,0:T(8,128)S(1)}, f32[168,512]{1,0:T(8,128)S(1)}, f32[336,512]{1,0:T(8,128)S(1)}) custom-call(bf16[88,896]{1,0:T(8,128)(2,1)S(1)} %get-tuple-element.43.refs_0_, bf16[88,896]{1,0:T(8,128)(2,1)S(1)} %collective-permute-done.10.refs_1_, ...), custom_call_target="tpu_custom_call" | custom-call | tf_op jit(solution)/shard_map/pallas_call | solution.py:303
  15.7 0.5 collective-permute-start.13
  16.2 0.8 %collective-permute-done.14.refs_1_ = f32[40,512]{1,0:T(8,128)S(1)} collective-permute-done((f32[40,512]{1,0:T(8,128)S(1)}, f32[40,512]{1,0:T(8,128)S(1)}, u32[]{:S(2)}, u32[]{:S(2)}) %collective-permute-start.14) | collective-permute-done | bytes 81952 | tf_op jit(solution)/shard_map/ppermute | solution.py:206
  17.2 1.7 %collective-permute-start.15 = (f32[88,512]{1,0:T(8,128)S(1)}, f32[88,512]{1,0:T(8,128)S(1)}, u32[]{:S(2)}, u32[]{:S(2)}) collective-permute-start(f32[88,512]{1,0:T(8,128)S(1)} %shard_map.52), channel_id=1, source_target_pairs={{0,8},{4,12},{8,0},{12,4},{16,24},{20,28},{24,16},{28,20},{1,9},{5... | collective-permute-start | bytes 540680 | tf_op jit(solution)/shard_map/ppermute | solution.py:206
  18.8 0.8 %collective-permute-done.refs_1_ = bf16[88,1280]{1,0:T(8,128)(2,1)S(1)} collective-permute-done((bf16[88,1280]{1,0:T(8,128)(2,1)S(1)}, bf16[88,1280]{1,0:T(8,128)(2,1)S(1)}, u32[]{:S(2)}, u32[]{:S(2)}) %collective-permute-start) | collective-permute-done | bytes 225312 | tf_op jit(solution)/shard_map/ppermute | solution.py:200
  19.7 3.4 %collective-permute-done.1.refs_2_ = bf16[88,1280]{1,0:T(8,128)(2,1)S(1)} collective-permute-done((bf16[88,1280]{1,0:T(8,128)(2,1)S(1)}, bf16[88,1280]{1,0:T(8,128)(2,1)S(1)}, u32[]{:S(2)}, u32[]{:S(2)}) %collective-permute-start.1) | collective-permute-done | bytes 225312 | tf_op jit(solution)/shard_map/ppermute | solution.py:200
  23.0 1.2 %shard_map.48 = (f32[64,640]{1,0:T(8,128)S(1)}, f32[64,640]{1,0:T(8,128)S(1)}, f32[16,640]{1,0:T(8,128)S(1)}, f32[24,640]{1,0:T(8,128)S(1)}, f32[40,640]{1,0:T(8...) custom-call(bf16[88,1280]{1,0:T(8,128)(2,1)S(1)} %get-tuple-element.32.refs_0_, ...), custom_call_target="tpu_custom_call" | custom-call | tf_op jit(solution)/shard_map/pallas_call | solution.py:303
  24.9 0.8 %collective-permute-done.4.refs_0_.refs_1_ = f32[64,640]{1,0:T(8,128)S(1)} collective-permute-done((f32[64,640]{1,0:T(8,128)S(1)}, f32[64,640]{1,0:T(8,128)S(1)}, u32[]{:S(2)}, u32[]{:S(2)}) %collective-permute-start.4) | collective-permute-done | bytes 163872 | tf_op jit(solution)/shard_map/ppermute | solution.py:206
  25.9 1.8 %collective-permute-start.16 = (f32[88,640]{1,0:T(8,128)S(1)}, f32[88,640]{1,0:T(8,128)S(1)}, u32[]{:S(2)}, u32[]{:S(2)}) collective-permute-start(f32[88,640]{1,0:T(8,128)S(1)} %shard_map.53), channel_id=1, source_target_pairs={{0,8},{4,12},{8,0},{12,4},{16,24},{20,28},{24,16},{28,20},{1,9},{5... | collective-permute-start | bytes 675848 | tf_op jit(solution)/shard_map/ppermute | solution.py:206
  27.8 0.5 collective-permute-start.6
  28.3 2.7 %collective-permute-start.23 = (f32[88,512]{1,0:T(8,128)S(1)}, f32[88,512]{1,0:T(8,128)S(1)}, u32[]{:S(2)}, u32[]{:S(2)}) collective-permute-start(f32[88,512]{1,0:T(8,128)S(1)} %shard_map.57.refs_5_), channel_id=1, source_target_pairs={{0,16},{4,20},{8,24},{12,28},{16,0},{20,4},{24,8},{28,12},{1,17},{... | collective-permute-start | bytes 540680 | tf_op jit(solution)/shard_map/ppermute | solution.py:206
  31.0 0.5 collective-permute-start.8
  31.5 0.9 %collective-permute-done.8.refs_0_ = f32[8,640]{1,0:T(8,128)S(1)} collective-permute-done((f32[8,640]{1,0:T(8,128)S(1)}, f32[8,640]{1,0:T(8,128)S(1)}, u32[]{:S(2)}, u32[]{:S(2)}) %collective-permute-start.8) | collective-permute-done | bytes 20512 | tf_op jit(solution)/shard_map/ppermute | solution.py:206
  32.9 5.3 %collective-permute-done.16.refs_2_.refs_1_ = f32[88,640]{1,0:T(8,128)S(1)} collective-permute-done((f32[88,640]{1,0:T(8,128)S(1)}, f32[88,640]{1,0:T(8,128)S(1)}, u32[]{:S(2)}, u32[]{:S(2)}) %collective-permute-start.16) | collective-permute-done | bytes 225312 | tf_op jit(solution)/shard_map/ppermute | solution.py:206
  38.2 1.0 %collective-permute-start.19 = (f32[48,640]{1,0:T(8,128)S(1)}, f32[48,640]{1,0:T(8,128)S(1)}, u32[]{:S(2)}, u32[]{:S(2)}) collective-permute-start(f32[48,640]{1,0:T(8,128)S(1)} %shard_map.54.refs_1_), channel_id=1, source_target_pairs={{0,16},{4,20},{8,24},{12,28},{16,0},{20,4},{24,8},{28,12},{1,17},{... | collective-permute-start | bytes 368648 | tf_op jit(solution)/shard_map/ppermute | solution.py:206
  39.3 2.0 %collective-permute-start.18 = (f32[40,640]{1,0:T(8,128)S(1)}, f32[40,640]{1,0:T(8,128)S(1)}, u32[]{:S(2)}, u32[]{:S(2)}) collective-permute-start(f32[40,640]{1,0:T(8,128)S(1)} %shard_map.55), channel_id=1, source_target_pairs={{0,16},{4,20},{8,24},{12,28},{16,0},{20,4},{24,8},{28,12},{1,17},{... | collective-permute-start | bytes 307208 | tf_op jit(solution)/shard_map/ppermute | solution.py:206
  41.3 1.1 %collective-permute-start.22 = (f32[40,512]{1,0:T(8,128)S(1)}, f32[40,512]{1,0:T(8,128)S(1)}, u32[]{:S(2)}, u32[]{:S(2)}) collective-permute-start(f32[40,512]{1,0:T(8,128)S(1)} %shard_map.56), channel_id=1, source_target_pairs={{0,8},{4,12},{8,0},{12,4},{16,24},{20,28},{24,16},{28,20},{1,9},{5... | collective-permute-start | bytes 245768 | tf_op jit(solution)/shard_map/ppermute | solution.py:206
  42.5 1.0 %collective-permute-start.24 = (f32[40,512]{1,0:T(8,128)S(1)}, f32[40,512]{1,0:T(8,128)S(1)}, u32[]{:S(2)}, u32[]{:S(2)}) collective-permute-start(f32[40,512]{1,0:T(8,128)S(1)} %shard_map.58), channel_id=1, source_target_pairs={{0,8},{4,12},{8,0},{12,4},{16,24},{20,28},{24,16},{28,20},{1,9},{5... | collective-permute-start | bytes 245768 | tf_op jit(solution)/shard_map/ppermute | solution.py:206
  43.5 2.6 %collective-permute-done.7.refs_1_ = f32[80,640]{1,0:T(8,128)S(1)} collective-permute-done((f32[80,640]{1,0:T(8,128)S(1)}, f32[80,640]{1,0:T(8,128)S(1)}, u32[]{:S(2)}, u32[]{:S(2)}) %collective-permute-start.7) | collective-permute-done | bytes 204832 | tf_op jit(solution)/shard_map/ppermute | solution.py:206
  46.2 2.4 %collective-permute-done.22.refs_1_ = f32[40,512]{1,0:T(8,128)S(1)} collective-permute-done((f32[40,512]{1,0:T(8,128)S(1)}, f32[40,512]{1,0:T(8,128)S(1)}, u32[]{:S(2)}, u32[]{:S(2)}) %collective-permute-start.22) | collective-permute-done | bytes 81952 | tf_op jit(solution)/shard_map/ppermute | solution.py:206
  48.6 1.1 %collective-permute-done.24.refs_2_ = f32[40,512]{1,0:T(8,128)S(1)} collective-permute-done((f32[40,512]{1,0:T(8,128)S(1)}, f32[40,512]{1,0:T(8,128)S(1)}, u32[]{:S(2)}, u32[]{:S(2)}) %collective-permute-start.24) | collective-permute-done | bytes 81952 | tf_op jit(solution)/shard_map/ppermute | solution.py:206
  49.7 0.7 %collective-permute-done.18.refs_2_ = f32[40,640]{1,0:T(8,128)S(1)} collective-permute-done((f32[40,640]{1,0:T(8,128)S(1)}, f32[40,640]{1,0:T(8,128)S(1)}, u32[]{:S(2)}, u32[]{:S(2)}) %collective-permute-start.18) | collective-permute-done | bytes 102432 | tf_op jit(solution)/shard_map/ppermute | solution.py:206
  50.4 1.1 %shard_map.60 = f32[3,80,640]{2,1,0:T(8,128)} custom-call(f32[80,640]{1,0:T(8,128)S(1)} %shard_map.50.refs_0_, f32[48,640]{1,0:T(8,128)S(1)} %shard_map.54.refs_1_, f32[40,640]{1,0:T(8,128)S(1)} %collective-permute-done.18.refs_2_, f32[48,640]{1,0:T(8,128)S(1)} %collective-permute-done.19.refs_3_, f32[80,512]{1,0:T(8,128)S(1)} %shard_map.59.refs_4_, ...), custom_call_target="tpu_custom_call" | custom-call | tf_op jit(solution)/shard_map/pallas_call | solution.py:339
  (33 shorter events, 2.0 us)
Async XLA Ops:
  2.0 9.0 %collective-permute-start.10 = (bf16[88,896]{1,0:T(8,128)(2,1)S(1)}, bf16[88,896]{1,0:T(8,128)(2,1)S(1)}, u32[]{:S(2)}, u32[]{:S(2)}) collective-permute-start(bf16[88,896]{1,0:T(8,128)(2,1)S(1)} %get-tuple-element.44), channel_id=1, source_target_pairs={{0,3},{1,2},{2,1},{3,0},{4,7},{5,6},{6,5},{7,4},{8,11},{9,10},{10,... | collective-permute-start | bytes 473096 | tf_op jit(solution)/shard_map/ppermute | solution.py:200
  5.9 7.5 %collective-permute-start.11 = (bf16[88,896]{1,0:T(8,128)(2,1)S(1)}, bf16[88,896]{1,0:T(8,128)(2,1)S(1)}, u32[]{:S(2)}, u32[]{:S(2)}) collective-permute-start(bf16[88,896]{1,0:T(8,128)(2,1)S(1)} %get-tuple-element.45), channel_id=1, source_target_pairs={{0,2},{1,3},{2,0},{3,1},{4,6},{5,7},{6,4},{7,5},{8,10},{9,11},{10,... | collective-permute-start | bytes 473096 | tf_op jit(solution)/shard_map/ppermute | solution.py:200
  6.4 8.4 %collective-permute-start.12 = (bf16[88,896]{1,0:T(8,128)(2,1)S(1)}, bf16[88,896]{1,0:T(8,128)(2,1)S(1)}, u32[]{:S(2)}, u32[]{:S(2)}) collective-permute-start(bf16[88,896]{1,0:T(8,128)(2,1)S(1)} %get-tuple-element.46), channel_id=1, source_target_pairs={{0,1},{1,0},{2,3},{3,2},{4,5},{5,4},{6,7},{7,6},{8,9},{9,8},{10,11... | collective-permute-start | bytes 473096 | tf_op jit(solution)/shard_map/ppermute | solution.py:200
  7.6 12.1 %collective-permute-start = (bf16[88,1280]{1,0:T(8,128)(2,1)S(1)}, bf16[88,1280]{1,0:T(8,128)(2,1)S(1)}, u32[]{:S(2)}, u32[]{:S(2)}) collective-permute-start(bf16[88,1280]{1,0:T(8,128)(2,1)S(1)} %get-tuple-element.33), channel_id=1, source_target_pairs={{0,1},{1,0},{2,3},{3,2},{4,5},{5,4},{6,7},{7,6},{8,9},{9,8},{10,11... | collective-permute-start | bytes 675848 | tf_op jit(solution)/shard_map/ppermute | solution.py:200
  9.5 13.5 %collective-permute-start.1 = (bf16[88,1280]{1,0:T(8,128)(2,1)S(1)}, bf16[88,1280]{1,0:T(8,128)(2,1)S(1)}, u32[]{:S(2)}, u32[]{:S(2)}) collective-permute-start(bf16[88,1280]{1,0:T(8,128)(2,1)S(1)} %get-tuple-element.34), channel_id=1, source_target_pairs={{0,3},{1,2},{2,1},{3,0},{4,7},{5,6},{6,5},{7,4},{8,11},{9,10},{10,... | collective-permute-start | bytes 675848 | tf_op jit(solution)/shard_map/ppermute | solution.py:200
  11.0 12.0 %collective-permute-start.2 = (bf16[88,1280]{1,0:T(8,128)(2,1)S(1)}, bf16[88,1280]{1,0:T(8,128)(2,1)S(1)}, u32[]{:S(2)}, u32[]{:S(2)}) collective-permute-start(bf16[88,1280]{1,0:T(8,128)(2,1)S(1)} %get-tuple-element.35), channel_id=1, source_target_pairs={{0,2},{1,3},{2,0},{3,1},{4,6},{5,7},{6,4},{7,5},{8,10},{9,11},{10,... | collective-permute-start | bytes 675848 | tf_op jit(solution)/shard_map/ppermute | solution.py:200
  15.6 1.3 %collective-permute-start.14 = (f32[40,512]{1,0:T(8,128)S(1)}, f32[40,512]{1,0:T(8,128)S(1)}, u32[]{:S(2)}, u32[]{:S(2)}) collective-permute-start(f32[40,512]{1,0:T(8,128)S(1)} %get-tuple-element.49), channel_id=1, source_target_pairs={{0,4},{4,0},{8,12},{12,8},{16,20},{20,16},{24,28},{28,24},{1,5},{5... | collective-permute-start | bytes 245768 | tf_op jit(solution)/shard_map/ppermute | solution.py:206
  15.7 1.4 %collective-permute-start.13 = (f32[48,512]{1,0:T(8,128)S(1)}, f32[48,512]{1,0:T(8,128)S(1)}, u32[]{:S(2)}, u32[]{:S(2)}) collective-permute-start(f32[48,512]{1,0:T(8,128)S(1)} %get-tuple-element.48), channel_id=1, source_target_pairs={{0,4},{4,0},{8,12},{12,8},{16,20},{20,16},{24,28},{28,24},{1,5},{5... | collective-permute-start | bytes 294920 | tf_op jit(solution)/shard_map/ppermute | solution.py:206
  17.0 11.3 %collective-permute-start.20 = (f32[168,512]{1,0:T(8,128)S(1)}, f32[168,512]{1,0:T(8,128)S(1)}, u32[]{:S(2)}, u32[]{:S(2)}) collective-permute-start(f32[168,512]{1,0:T(8,128)S(1)} %get-tuple-element.51), channel_id=1, source_target_pairs={{0,4},{4,0},{8,12},{12,8},{16,20},{20,16},{24,28},{28,24},{1,5},{5... | collective-permute-start | bytes 1032200 | tf_op jit(solution)/shard_map/ppermute | solution.py:206
  17.2 8.7 %collective-permute-start.15 = (f32[88,512]{1,0:T(8,128)S(1)}, f32[88,512]{1,0:T(8,128)S(1)}, u32[]{:S(2)}, u32[]{:S(2)}) collective-permute-start(f32[88,512]{1,0:T(8,128)S(1)} %shard_map.52), channel_id=1, source_target_pairs={{0,8},{4,12},{8,0},{12,4},{16,24},{20,28},{24,16},{28,20},{1,9},{5... | collective-permute-start | bytes 540680 | tf_op jit(solution)/shard_map/ppermute | solution.py:206
  24.2 1.5 %collective-permute-start.4 = (f32[64,640]{1,0:T(8,128)S(1)}, f32[64,640]{1,0:T(8,128)S(1)}, u32[]{:S(2)}, u32[]{:S(2)}) collective-permute-start(f32[64,640]{1,0:T(8,128)S(1)} %get-tuple-element.38), channel_id=1, source_target_pairs={{0,4},{4,0},{8,12},{12,8},{16,20},{20,16},{24,28},{28,24},{1,5},{5... | collective-permute-start | bytes 491528 | tf_op jit(solution)/shard_map/ppermute | solution.py:206
  24.3 1.6 %collective-permute-start.9 = (f32[64,640]{1,0:T(8,128)S(1)}, f32[64,640]{1,0:T(8,128)S(1)}, u32[]{:S(2)}, u32[]{:S(2)}) collective-permute-start(f32[64,640]{1,0:T(8,128)S(1)} %get-tuple-element.42), channel_id=1, source_target_pairs={{0,4},{4,0},{8,12},{12,8},{16,20},{20,16},{24,28},{28,24},{1,5},{5... | collective-permute-start | bytes 491528 | tf_op jit(solution)/shard_map/ppermute | solution.py:206
  24.8 8.1 %collective-permute-start.3 = (f32[120,640]{1,0:T(8,128)S(1)}, f32[120,640]{1,0:T(8,128)S(1)}, u32[]{:S(2)}, u32[]{:S(2)}) collective-permute-start(f32[120,640]{1,0:T(8,128)S(1)} %get-tuple-element.37), channel_id=1, source_target_pairs={{0,4},{4,0},{8,12},{12,8},{16,20},{20,16},{24,28},{28,24},{1,5},{5... | collective-permute-start | bytes 921608 | tf_op jit(solution)/shard_map/ppermute | solution.py:206
  25.9 12.3 %collective-permute-start.16 = (f32[88,640]{1,0:T(8,128)S(1)}, f32[88,640]{1,0:T(8,128)S(1)}, u32[]{:S(2)}, u32[]{:S(2)}) collective-permute-start(f32[88,640]{1,0:T(8,128)S(1)} %shard_map.53), channel_id=1, source_target_pairs={{0,8},{4,12},{8,0},{12,4},{16,24},{20,28},{24,16},{28,20},{1,9},{5... | collective-permute-start | bytes 675848 | tf_op jit(solution)/shard_map/ppermute | solution.py:206
  27.8 3.2 %collective-permute-start.5 = (f32[16,640]{1,0:T(8,128)S(1)}, f32[16,640]{1,0:T(8,128)S(1)}, u32[]{:S(2)}, u32[]{:S(2)}) collective-permute-start(f32[16,640]{1,0:T(8,128)S(1)} %get-tuple-element.39), channel_id=1, source_target_pairs={{0,4},{4,0},{8,12},{12,8},{16,20},{20,16},{24,28},{28,24},{1,5},{5... | collective-permute-start | bytes 122888 | tf_op jit(solution)/shard_map/ppermute | solution.py:206
  27.8 3.2 %collective-permute-start.6 = (f32[24,640]{1,0:T(8,128)S(1)}, f32[24,640]{1,0:T(8,128)S(1)}, u32[]{:S(2)}, u32[]{:S(2)}) collective-permute-start(f32[24,640]{1,0:T(8,128)S(1)} %get-tuple-element.40), channel_id=1, source_target_pairs={{0,4},{4,0},{8,12},{12,8},{16,20},{20,16},{24,28},{28,24},{1,5},{5... | collective-permute-start | bytes 184328 | tf_op jit(solution)/shard_map/ppermute | solution.py:206
  28.3 14.1 %collective-permute-start.23 = (f32[88,512]{1,0:T(8,128)S(1)}, f32[88,512]{1,0:T(8,128)S(1)}, u32[]{:S(2)}, u32[]{:S(2)}) collective-permute-start(f32[88,512]{1,0:T(8,128)S(1)} %shard_map.57.refs_5_), channel_id=1, source_target_pairs={{0,16},{4,20},{8,24},{12,28},{16,0},{20,4},{24,8},{28,12},{1,17},{... | collective-permute-start | bytes 540680 | tf_op jit(solution)/shard_map/ppermute | solution.py:206
  31.0 10.3 %collective-permute-start.21 = (f32[80,512]{1,0:T(8,128)S(1)}, f32[80,512]{1,0:T(8,128)S(1)}, u32[]{:S(2)}, u32[]{:S(2)}) collective-permute-start(f32[80,512]{1,0:T(8,128)S(1)} %get-tuple-element.52), channel_id=1, source_target_pairs={{0,4},{4,0},{8,12},{12,8},{16,20},{20,16},{24,28},{28,24},{1,5},{5... | collective-permute-start | bytes 491528 | tf_op jit(solution)/shard_map/ppermute | solution.py:206
  31.0 1.4 %collective-permute-start.8 = (f32[8,640]{1,0:T(8,128)S(1)}, f32[8,640]{1,0:T(8,128)S(1)}, u32[]{:S(2)}, u32[]{:S(2)}) collective-permute-start(f32[8,640]{1,0:T(8,128)S(1)} %get-tuple-element.41), channel_id=1, source_target_pairs={{0,4},{4,0},{8,12},{12,8},{16,20},{20,16},{24,28},{28,24},{1,5},{5... | collective-permute-start | bytes 61448 | tf_op jit(solution)/shard_map/ppermute | solution.py:206
  32.4 13.7 %collective-permute-start.7 = (f32[80,640]{1,0:T(8,128)S(1)}, f32[80,640]{1,0:T(8,128)S(1)}, u32[]{:S(2)}, u32[]{:S(2)}) collective-permute-start(f32[80,640]{1,0:T(8,128)S(1)} %shard_map.49), channel_id=1, source_target_pairs={{0,8},{4,12},{8,0},{12,4},{16,24},{20,28},{24,16},{28,20},{1,9},{5... | collective-permute-start | bytes 614408 | tf_op jit(solution)/shard_map/ppermute | solution.py:206
  32.9 6.4 %collective-permute-start.17 = (f32[40,640]{1,0:T(8,128)S(1)}, f32[40,640]{1,0:T(8,128)S(1)}, u32[]{:S(2)}, u32[]{:S(2)}) collective-permute-start(f32[40,640]{1,0:T(8,128)S(1)} %get-tuple-element.50), channel_id=1, source_target_pairs={{0,4},{4,0},{8,12},{12,8},{16,20},{20,16},{24,28},{28,24},{1,5},{5... | collective-permute-start | bytes 307208 | tf_op jit(solution)/shard_map/ppermute | solution.py:206
  38.2 12.2 %collective-permute-start.19 = (f32[48,640]{1,0:T(8,128)S(1)}, f32[48,640]{1,0:T(8,128)S(1)}, u32[]{:S(2)}, u32[]{:S(2)}) collective-permute-start(f32[48,640]{1,0:T(8,128)S(1)} %shard_map.54.refs_1_), channel_id=1, source_target_pairs={{0,16},{4,20},{8,24},{12,28},{16,0},{20,4},{24,8},{28,12},{1,17},{... | collective-permute-start | bytes 368648 | tf_op jit(solution)/shard_map/ppermute | solution.py:206
  39.3 11.1 %collective-permute-start.18 = (f32[40,640]{1,0:T(8,128)S(1)}, f32[40,640]{1,0:T(8,128)S(1)}, u32[]{:S(2)}, u32[]{:S(2)}) collective-permute-start(f32[40,640]{1,0:T(8,128)S(1)} %shard_map.55), channel_id=1, source_target_pairs={{0,16},{4,20},{8,24},{12,28},{16,0},{20,4},{24,8},{28,12},{1,17},{... | collective-permute-start | bytes 307208 | tf_op jit(solution)/shard_map/ppermute | solution.py:206
  41.3 7.2 %collective-permute-start.22 = (f32[40,512]{1,0:T(8,128)S(1)}, f32[40,512]{1,0:T(8,128)S(1)}, u32[]{:S(2)}, u32[]{:S(2)}) collective-permute-start(f32[40,512]{1,0:T(8,128)S(1)} %shard_map.56), channel_id=1, source_target_pairs={{0,8},{4,12},{8,0},{12,4},{16,24},{20,28},{24,16},{28,20},{1,9},{5... | collective-permute-start | bytes 245768 | tf_op jit(solution)/shard_map/ppermute | solution.py:206
  42.5 7.2 %collective-permute-start.24 = (f32[40,512]{1,0:T(8,128)S(1)}, f32[40,512]{1,0:T(8,128)S(1)}, u32[]{:S(2)}, u32[]{:S(2)}) collective-permute-start(f32[40,512]{1,0:T(8,128)S(1)} %shard_map.58), channel_id=1, source_target_pairs={{0,8},{4,12},{8,0},{12,4},{16,24},{20,28},{24,16},{28,20},{1,9},{5... | collective-permute-start | bytes 245768 | tf_op jit(solution)/shard_map/ppermute | solution.py:206

commit v4 on v3

--- a/solution.py
+++ b/solution.py
@@ -25,7 +25,17 @@
 PARAMS = pltpu.CompilerParams(vmem_limit_bytes=48 * 1024 * 1024)
 
 
-CFG = {'first': 'M', 'order': {'F': (3, 2, 1), 'S': (1, 3, 2)}, 'core': {'F': (48, 88, 168), 'S': (64, 128, 144, 168, 208, 216)}, 'z1': {'F': (88, 128), 'S': (88,)}, 'z2': {'F': (), 'S': (40,)}, 'after': {('z1', 'S', 0): (('z1', 'F', 0),), ('z1', 'F', 2): (('z2', 'F', 0),), ('keep', 'F'): (('z1', 'F', 0),)}}
+CFG = {
+    "first": "M",
+    "order": {"F": (3, 2, 1), "S": (2, 1, 3)},
+    "core": {"F": (88, 168), "S": (40, 136, 144, 168, 256)},
+    "z1": {"F": (), "S": (88,)},
+    "z2": {"F": (), "S": (48,)},
+    "after": {
+        ("send", "S", 1): (("z2", "F", 0), ("z1", "S", 0)),
+        ("z1", "S", 1): (("got", "S", 2),),
+    },
+}
 
 
 def row_keys(order_ref, tile_ref, me, n_bin, per_owner):
@@ -38,12 +48,16 @@
         for i in range(per_owner):
             wanted = jnp.where(place == k * per_owner + i, order_ref[(me ^ k) * per_owner + i], wanted)
     hits = wanted == tile_ref[...]
-    before = lax.broadcasted_iota(jnp.int32, (rows, rows), 0) < lax.broadcasted_iota(jnp.int32, (rows, rows), 1)
-    rank = jnp.dot(
-        hits.astype(jnp.float32).astype(jnp.bfloat16),
-        before.astype(jnp.float32).astype(jnp.bfloat16),
-        preferred_element_type=jnp.float32,
-    )
+    block = 128
+    before = lax.broadcasted_iota(jnp.int32, (block, block), 0) < lax.broadcasted_iota(jnp.int32, (block, block), 1)
+    before = before.astype(jnp.float32).astype(jnp.bfloat16)
+    ones = hits.astype(jnp.float32)
+    ranks, seen = [], jnp.zeros((padded, 1), jnp.float32)
+    for at in range(0, rows, block):
+        here = ones[:, at : at + block]
+        ranks.append(seen + jnp.dot(here.astype(jnp.bfloat16), before, preferred_element_type=jnp.float32))
+        seen = seen + jnp.sum(here, axis=1, keepdims=True)
+    rank = jnp.concatenate(ranks, axis=1)
     return jnp.where(hits, rank, -1.0).astype(jnp.int32)
 
 
@@ -122,14 +136,17 @@
 def moment_kernel(lanes, rows_c, n_cycle, n_in, n_after, *refs):
     in_refs, out_refs, cross_ref = refs[:n_in], refs[n_in + n_after : -1], refs[-1]
     columns, sums_end = (WIDE, WIDE) if lanes == WIDE else (CRIS_COLUMNS, CRIS_ONE + 1)
-    cross = jnp.zeros((lanes, lanes), jnp.float32)
-    for ref in in_refs:
-        cross = cross + lax.dot_general(
-            ref[:, :lanes],
-            ref[:, columns : columns + lanes],
-            (((0,), (0,)), ((), ())),
-            preferred_element_type=jnp.float32,
+    whole = in_refs[0].shape[0] // 16 * 16
+
+    def stacked(at):
+        ends = [ref[whole:, at : at + lanes].astype(jnp.float32) for ref in in_refs]
+        return jnp.concatenate(
+            [ref[:whole, at : at + lanes] for ref in in_refs] + [jnp.concatenate(ends).astype(jnp.bfloat16)]
         )
+
+    cross = lax.dot_general(
+        stacked(0), stacked(columns), (((0,), (0,)), ((), ())), preferred_element_type=jnp.float32
+    )
     cross_ref[:lanes, :] = cross
     if lanes == WIDE:
         lane = lax.broadcasted_iota(jnp.int32, (WIDE - ATMS_AT, 128), 1) + (WIDE - 128)
@@ -164,34 +181,45 @@
         start = end
 
 
-def finish_kernel(rows_c, n_wide, n_mid, *refs):
-    wide_keep_ref, wide_send_ref, *wide_got = refs[: 2 + n_wide]
-    mid_keep_ref, mid_send_ref, *mid_got = refs[2 + n_wide : -1]
+def covariance(total, one, sums):
+    scale = 1.0 / sums[:, one : one + 1]
+    return total * scale - (total[:, one : one + 1] * scale) * (sums * scale)
+
+
+def finish_mid_kernel(rows_c, keep_ref, send_ref, *refs):
     out_ref = refs[-1]
-    wide_got = jnp.concatenate([ref[...] for ref in wide_got])
-    mid_got = jnp.concatenate([ref[...] for ref in mid_got])
+    got = jnp.concatenate([ref[...] for ref in refs[:-1]])
+    row = lax.broadcasted_iota(jnp.int32, (rows_c, MID), 0) + lax.axis_index("cycle") * rows_c
+    lane = lax.broadcasted_iota(jnp.int32, (rows_c, MID), 1)
+    sums = send_ref[send_ref.shape[0] - SUMS :] + got[rows_c:]
+    cov = covariance(keep_ref[...] + got[:rows_c], CRIS_AN - CRIS_COLUMNS + CRIS_ONE, sums[SUMS - 1 :])
+    cov = pltpu.roll(cov, MID - (CRIS_AN - CRIS_COLUMNS), 1)
+    out_ref[:, :MID] = jnp.where((lane < C_CRIS) & (row < C_CRIS), cov, 0.0)
+    out_ref[:, MID:] = jnp.zeros((rows_c, WIDE - MID), jnp.float32)
+
+
+def finish_kernel(rows_c, keep_ref, send_ref, *refs):
+    *got_refs, mid_ref, out_ref, wide_ref, atms_ref, sem = refs
+    mid_copy = pltpu.make_async_copy(mid_ref, out_ref.at[1], sem.at[1])
+    mid_copy.start()
+    got = jnp.concatenate([ref[...] for ref in got_refs])
     row = lax.broadcasted_iota(jnp.int32, (rows_c, WIDE), 0) + lax.axis_index("cycle") * rows_c
     lane = lax.broadcasted_iota(jnp.int32, (rows_c, WIDE), 1)
-    total = wide_keep_ref[...] + wide_got[:rows_c]
-    sums = wide_send_ref[wide_send_ref.shape[0] - SUMS :] + wide_got[rows_c:]
-
-    def covariance(total, one, sums):
-        n = sums[:, one : one + 1]
-        return total / n - (total[:, one : one + 1] / n) * (sums / n)
-
+    total = keep_ref[...] + got[:rows_c]
+    sums = send_ref[send_ref.shape[0] - SUMS :] + got[rows_c:]
     cov = covariance(total, WIDE - 1, sums[SUMS - 1 :])
-    out_ref[0] = jnp.where((lane < C_IASI) & (row < C_IASI), cov, 0.0)
+    wide_ref[...] = jnp.where((lane < C_IASI) & (row < C_IASI), cov, 0.0)
+    wide_copy = pltpu.make_async_copy(wide_ref, out_ref.at[0], sem.at[0])
+    wide_copy.start()
     cov = covariance(total[:, WIDE - 128 :], 126, sums[SUMS - 2 : SUMS - 1, WIDE - 128 :])
     cov = pltpu.roll(cov, 128 - ATMS_AT % 128, 1)
-    out_ref[2, :, :128] = jnp.where((lane[:, :128] < C_ATMS) & (row[:, :128] < C_ATMS), cov, 0.0)
-    out_ref[2, :, 128:] = jnp.zeros((rows_c, WIDE - 128), jnp.float32)
-
-    total = mid_keep_ref[...] + mid_got[:rows_c]
-    sums = mid_send_ref[mid_send_ref.shape[0] - SUMS :] + mid_got[rows_c:]
-    cov = covariance(total, CRIS_AN - CRIS_COLUMNS + CRIS_ONE, sums[SUMS - 1 :])
-    cov = pltpu.roll(cov, MID - (CRIS_AN - CRIS_COLUMNS), 1)
-    out_ref[1, :, :MID] = jnp.where((lane[:, :MID] < C_CRIS) & (row[:, :MID] < C_CRIS), cov, 0.0)
-    out_ref[1, :, MID:] = jnp.zeros((rows_c, WIDE - MID), jnp.float32)
+    atms_ref[:, :128] = jnp.where((lane[:, :128] < C_ATMS) & (row[:, :128] < C_ATMS), cov, 0.0)
+    atms_ref[:, 128:] = jnp.zeros((rows_c, WIDE - 128), jnp.float32)
+    atms_copy = pltpu.make_async_copy(atms_ref, out_ref.at[2], sem.at[2])
+    atms_copy.start()
+    mid_copy.wait()
+    wide_copy.wait()
+    atms_copy.wait()
 
 
 def to_owners(parts, order):
@@ -336,13 +364,25 @@
         return [keep, send, *got]
 
     wide, mid = (ends(p) for p in sorted("FS", key=lambda p: -lanes[p]))
-    return pl.pallas_call(
-        functools.partial(finish_kernel, rows_c, len(wide) - 2, len(mid) - 2),
-        out_shape=jax.ShapeDtypeStruct((per_owner, rows_c, width), jnp.float32),
-        in_specs=[VMEM] * (len(wide) + len(mid)),
+    mid = pl.pallas_call(
+        functools.partial(finish_mid_kernel, rows_c),
+        out_shape=jax.ShapeDtypeStruct((rows_c, width), jnp.float32),
+        in_specs=[VMEM] * len(mid),
         out_specs=VMEM,
         compiler_params=PARAMS,
-    )(*wide, *mid)
+    )(*mid)
+    return pl.pallas_call(
+        functools.partial(finish_kernel, rows_c),
+        out_shape=jax.ShapeDtypeStruct((per_owner, rows_c, width), jnp.float32),
+        in_specs=[VMEM] * (len(wide) + 1),
+        out_specs=HBM,
+        scratch_shapes=[
+            pltpu.VMEM((rows_c, width), jnp.float32),
+            pltpu.VMEM((rows_c, width), jnp.float32),
+            pltpu.SemaphoreType.DMA((3,)),
+        ],
+        compiler_params=PARAMS,
+    )(*wide, mid)
 
 
 def solution(mesh):

time: 51.6 us -> 50.9 us (0.986)
  Pallas kernels: 6.25 us -> 5.66 us
    ppermute x6, waiting for transfers between devices: 6.11 us -> 5.03 us  [to_owners(): lax.ppermute(parts[k], 'bin', [(i, i ^ k) for i in range(n_bin)])]
    ppermute x19 -> x15, waiting for transfers between devices: 14.9 us -> 15.9 us  [swap(): return lax.ppermute(value, 'cycle', [(i, i ^ bit) for i in range(n)])]
    ppermute x19 -> x15, starting transfers between devices: 14.2 us -> 13.2 us  [swap(): return lax.ppermute(value, 'cycle', [(i, i ^ bit) for i in range(n)])]
    ppermute x6, starting transfers between devices: 9.93 us -> 10.8 us  [to_owners(): lax.ppermute(parts[k], 'bin', [(i, i ^ k) for i in range(n_bin)])]
    pallas_call x2, Pallas kernels: 1.96 us -> 1.34 us  [make(): pl.pallas_call(functools.partial(moment_kernel, lanes[p], rows_c, n_cycle...]
    pallas_call x1 -> x2, Pallas kernels: 1.08 us -> 1.14 us  [the longest x1 0.92 us: on_device(): pl.pallas_call(functools.partial(finish_kernel, rows_c), out_shape=jax.Sh...]
  transfers between devices with their start and end apart: 25 -> 21, of which waited for: 13 -> 12; matrix products, arithmetic and copies ran while one was open for 0% -> 0% of each run, Pallas kernels for 6% -> 5%
where the time goes in v4:
time: 50.9 us; the launch traced here: 50.7 us
  starting transfers between devices  24 us (47%)
  waiting for transfers between devices  21 us (41%)
  Pallas kernels  5.66 us (11%)
    ppermute x15, waiting for transfers between devices, swap(): return lax.ppermute(value, 'cycle', [(i, i ^ bit) for i in range(n)])  15.9 us
    ppermute x15, starting transfers between devices, swap(): return lax.ppermute(value, 'cycle', [(i, i ^ bit) for i in range(n)])  13.2 us
    ppermute x6, starting transfers between devices, to_owners(): lax.ppermute(parts[k], 'bin', [(i, i ^ k) for i in range(n_bin)])  10.8 us
    ppermute x6, waiting for transfers between devices, to_owners(): lax.ppermute(parts[k], 'bin', [(i, i ^ k) for i in range(n_bin)])  5.03 us
    pallas_call x1, Pallas kernels, on_device(): pl.pallas_call(functools.partial(first_place_kernel, places[lanes['F']],...  1.97 us
    pallas_call x2, Pallas kernels, make(): pl.pallas_call(functools.partial(moment_kernel, lanes[p], rows_c, n_cycle...  1.34 us
  transfers between devices with their start and end apart: 21, of which 12 were waited for; matrix products, arithmetic and copies ran while one was open for 0% of the time, Pallas kernels for 5%

profile of v4, /device:TPU:0, one launch (start us, length us, event | category | flops | bytes accessed | tf_op | source)
XLA Modules:
  0.0 50.7 jit_solution(16567985724653173005)
XLA Ops:
  0.0 2.0 %shard_map.46 = (bf16[88,896]{1,0:T(8,128)(2,1)S(1)}, bf16[88,896]{1,0:T(8,128)(2,1)S(1)}, bf16[88,896]{1,0:T(8,128)(2,1)S(1)}, bf16[88,896]{1,0:T(8,128)(2,1)S(...) custom-call(s32[12]{0:T(128)} %order_hbm.1, s32[1,512]{1,0:T(1,128)} %bitcast.1, ...), custom_call_target="tpu_custom_call" | custom-call | tf_op jit(solution)/shard_map/pallas_call | solution.py:264
  2.0 4.0 %collective-permute-start.11 = (bf16[88,896]{1,0:T(8,128)(2,1)S(1)}, bf16[88,896]{1,0:T(8,128)(2,1)S(1)}, u32[]{:S(2)}, u32[]{:S(2)}) collective-permute-start(bf16[88,896]{1,0:T(8,128)(2,1)S(1)} %get-tuple-element.42), channel_id=1, source_target_pairs={{0,3},{1,2},{2,1},{3,0},{4,7},{5,6},{6,5},{7,4},{8,11},{9,10},{10,... | collective-permute-start | bytes 473096 | tf_op jit(solution)/shard_map/ppermute | solution.py:228
  5.9 0.5 collective-permute-start.12
  6.6 1.0 %shard_map.47 = (bf16[88,1280]{1,0:T(8,128)(2,1)S(1)}, bf16[88,1280]{1,0:T(8,128)(2,1)S(1)}, bf16[88,1280]{1,0:T(8,128)(2,1)S(1)}, bf16[88,1280]{1,0:T(8,128)(2,1)S(1)}) custom-call(s32[16,512]{1,0:T(8,128)S(1)} %get-tuple-element.27.keys_ref, bf16[512,640]{1,0:T(8,128)(2,1)S(1)} %get-tuple-element.28.bg_ref, bf16[512,640]{1,0:T(8,128)(2,1)S(1)} %get-tuple-element.29.an_ref), custom_call_target="tpu_custom_call" | custom-call | tf_op jit(solution)/shard_map/pallas_call | solution.py:278
  7.6 2.0 %collective-permute-start = (bf16[88,1280]{1,0:T(8,128)(2,1)S(1)}, bf16[88,1280]{1,0:T(8,128)(2,1)S(1)}, u32[]{:S(2)}, u32[]{:S(2)}) collective-permute-start(bf16[88,1280]{1,0:T(8,128)(2,1)S(1)} %get-tuple-element.31), channel_id=1, source_target_pairs={{0,2},{1,3},{2,0},{3,1},{4,6},{5,7},{6,4},{7,5},{8,10},{9,11},{10,... | collective-permute-start | bytes 675848 | tf_op jit(solution)/shard_map/ppermute | solution.py:228
  9.6 1.5 %collective-permute-start.1 = (bf16[88,1280]{1,0:T(8,128)(2,1)S(1)}, bf16[88,1280]{1,0:T(8,128)(2,1)S(1)}, u32[]{:S(2)}, u32[]{:S(2)}) collective-permute-start(bf16[88,1280]{1,0:T(8,128)(2,1)S(1)} %get-tuple-element.32), channel_id=1, source_target_pairs={{0,1},{1,0},{2,3},{3,2},{4,5},{5,4},{6,7},{7,6},{8,9},{9,8},{10,11... | collective-permute-start | bytes 675848 | tf_op jit(solution)/shard_map/ppermute | solution.py:228
  11.0 2.7 %collective-permute-start.2 = (bf16[88,1280]{1,0:T(8,128)(2,1)S(1)}, bf16[88,1280]{1,0:T(8,128)(2,1)S(1)}, u32[]{:S(2)}, u32[]{:S(2)}) collective-permute-start(bf16[88,1280]{1,0:T(8,128)(2,1)S(1)} %get-tuple-element.33), channel_id=1, source_target_pairs={{0,3},{1,2},{2,1},{3,0},{4,7},{5,6},{6,5},{7,4},{8,11},{9,10},{10,... | collective-permute-start | bytes 675848 | tf_op jit(solution)/shard_map/ppermute | solution.py:228
  13.8 1.0 %collective-permute-done.13.refs_3_ = bf16[88,896]{1,0:T(8,128)(2,1)S(1)} collective-permute-done((bf16[88,896]{1,0:T(8,128)(2,1)S(1)}, bf16[88,896]{1,0:T(8,128)(2,1)S(1)}, u32[]{:S(2)}, u32[]{:S(2)}) %collective-permute-start.13) | collective-permute-done | bytes 157728 | tf_op jit(solution)/shard_map/ppermute | solution.py:228
  14.8 0.5 %shard_map.52 = (f32[88,512]{1,0:T(8,128)S(1)}, f32[80,512]{1,0:T(8,128)S(1)}, f32[168,512]{1,0:T(8,128)S(1)}, f32[336,512]{1,0:T(8,128)S(1)}) custom-call(bf16[88,896]{1,0:T(8,128)(2,1)S(1)} %get-tuple-element.41.refs_0_, bf16[88,896]{1,0:T(8,128)(2,1)S(1)} %collective-permute-done.11.refs_1_, bf16[88,896]{1,0:T(8,128)(2,1)S(1)} %collective-permute-done.12.refs_2_, ...), custom_call_target="tpu_custom_call" | custom-call | tf_op jit(solution)/shard_map/pallas_call | solution.py:331
  15.5 0.5 collective-permute-start.16
  16.0 1.1 %collective-permute-done.16.refs_1_ = f32[80,512]{1,0:T(8,128)S(1)} collective-permute-done((f32[80,512]{1,0:T(8,128)S(1)}, f32[80,512]{1,0:T(8,128)S(1)}, u32[]{:S(2)}, u32[]{:S(2)}) %collective-permute-start.16) | collective-permute-done | bytes 163872 | tf_op jit(solution)/shard_map/ppermute | solution.py:234
  17.1 0.3 collective-permute-start.14
  17.4 1.6 %collective-permute-start.17 = (f32[168,512]{1,0:T(8,128)S(1)}, f32[168,512]{1,0:T(8,128)S(1)}, u32[]{:S(2)}, u32[]{:S(2)}) collective-permute-start(f32[168,512]{1,0:T(8,128)S(1)} %shard_map.53), channel_id=1, source_target_pairs={{0,8},{4,12},{8,0},{12,4},{16,24},{20,28},{24,16},{28,20},{1,9},{5... | collective-permute-start | bytes 1032200 | tf_op jit(solution)/shard_map/ppermute | solution.py:234
  19.2 0.4 collective-permute-done.1.refs_2_.refs_3_
  19.6 3.4 %collective-permute-done.2.refs_3_ = bf16[88,1280]{1,0:T(8,128)(2,1)S(1)} collective-permute-done((bf16[88,1280]{1,0:T(8,128)(2,1)S(1)}, bf16[88,1280]{1,0:T(8,128)(2,1)S(1)}, u32[]{:S(2)}, u32[]{:S(2)}) %collective-permute-start.2) | collective-permute-done | bytes 225312 | tf_op jit(solution)/shard_map/ppermute | solution.py:228
  23.0 0.8 %shard_map.48 = (f32[40,640]{1,0:T(8,128)S(1)}, f32[96,640]{1,0:T(8,128)S(1)}, f32[8,640]{1,0:T(8,128)S(1)}, f32[24,640]{1,0:T(8,128)S(1)}, f32[88,640]{1,0:T(8,...) custom-call(bf16[88,1280]{1,0:T(8,128)(2,1)S(1)} %get-tuple-element.30.refs_0_, ...), custom_call_target="tpu_custom_call" | custom-call | tf_op jit(solution)/shard_map/pallas_call | solution.py:331
  23.9 0.5 collective-permute-start.9
  24.5 1.1 %collective-permute-done.9.refs_0_ = f32[40,640]{1,0:T(8,128)S(1)} collective-permute-done((f32[40,640]{1,0:T(8,128)S(1)}, f32[40,640]{1,0:T(8,128)S(1)}, u32[]{:S(2)}, u32[]{:S(2)}) %collective-permute-start.9) | collective-permute-done | bytes 102432 | tf_op jit(solution)/shard_map/ppermute | solution.py:234
  25.6 1.8 %collective-permute-start.10 = (f32[88,640]{1,0:T(8,128)S(1)}, f32[88,640]{1,0:T(8,128)S(1)}, u32[]{:S(2)}, u32[]{:S(2)}) collective-permute-start(f32[88,640]{1,0:T(8,128)S(1)} %shard_map.51), channel_id=1, source_target_pairs={{0,8},{4,12},{8,0},{12,4},{16,24},{20,28},{24,16},{28,20},{1,9},{5... | collective-permute-start | bytes 675848 | tf_op jit(solution)/shard_map/ppermute | solution.py:234
  27.4 0.2 collective-permute-done.17.refs_1_
  27.7 2.7 %collective-permute-start.18 = (f32[88,512]{1,0:T(8,128)S(1)}, f32[88,512]{1,0:T(8,128)S(1)}, u32[]{:S(2)}, u32[]{:S(2)}) collective-permute-start(f32[88,512]{1,0:T(8,128)S(1)} %shard_map.54.send_ref), channel_id=1, source_target_pairs={{0,16},{4,20},{8,24},{12,28},{16,0},{20,4},{24,8},{28,12},{1,17},{... | collective-permute-start | bytes 540680 | tf_op jit(solution)/shard_map/ppermute | solution.py:234
  30.4 0.5 %collective-permute-start.5 = (f32[8,640]{1,0:T(8,128)S(1)}, f32[8,640]{1,0:T(8,128)S(1)}, u32[]{:S(2)}, u32[]{:S(2)}) collective-permute-start(f32[8,640]{1,0:T(8,128)S(1)} %get-tuple-element.37), channel_id=1, source_target_pairs={{0,4},{4,0},{8,12},{12,8},{16,20},{20,16},{24,28},{28,24},{1,5},{5... | collective-permute-start | bytes 61448 | tf_op jit(solution)/shard_map/ppermute | solution.py:234
  30.9 0.8 %collective-permute-done.5.refs_1_ = f32[8,640]{1,0:T(8,128)S(1)} collective-permute-done((f32[8,640]{1,0:T(8,128)S(1)}, f32[8,640]{1,0:T(8,128)S(1)}, u32[]{:S(2)}, u32[]{:S(2)}) %collective-permute-start.5) | collective-permute-done | bytes 20512 | tf_op jit(solution)/shard_map/ppermute | solution.py:234
  31.7 0.3 collective-permute-start.3
  32.1 1.6 %collective-permute-start.7 = (f32[80,640]{1,0:T(8,128)S(1)}, f32[80,640]{1,0:T(8,128)S(1)}, u32[]{:S(2)}, u32[]{:S(2)}) collective-permute-start(f32[80,640]{1,0:T(8,128)S(1)} %shard_map.49), channel_id=1, source_target_pairs={{0,8},{4,12},{8,0},{12,4},{16,24},{20,28},{24,16},{28,20},{1,9},{5... | collective-permute-start | bytes 614408 | tf_op jit(solution)/shard_map/ppermute | solution.py:234
  33.8 4.1 %collective-permute-done.10.refs_1_.refs_3_ = f32[88,640]{1,0:T(8,128)S(1)} collective-permute-done((f32[88,640]{1,0:T(8,128)S(1)}, f32[88,640]{1,0:T(8,128)S(1)}, u32[]{:S(2)}, u32[]{:S(2)}) %collective-permute-start.10) | collective-permute-done | bytes 225312 | tf_op jit(solution)/shard_map/ppermute | solution.py:234
  37.9 0.5 %collective-permute-start.19 = (f32[48,640]{1,0:T(8,128)S(1)}, f32[48,640]{1,0:T(8,128)S(1)}, u32[]{:S(2)}, u32[]{:S(2)}) collective-permute-start(f32[48,640]{1,0:T(8,128)S(1)} %shard_map.56), channel_id=1, source_target_pairs={{0,16},{4,20},{8,24},{12,28},{16,0},{20,4},{24,8},{28,12},{1,17},{... | collective-permute-start | bytes 368648 | tf_op jit(solution)/shard_map/ppermute | solution.py:234
  38.5 2.5 %collective-permute-start.20 = (f32[40,640]{1,0:T(8,128)S(1)}, f32[40,640]{1,0:T(8,128)S(1)}, u32[]{:S(2)}, u32[]{:S(2)}) collective-permute-start(f32[40,640]{1,0:T(8,128)S(1)} %shard_map.55.send_ref), channel_id=1, source_target_pairs={{0,16},{4,20},{8,24},{12,28},{16,0},{20,4},{24,8},{28,12},{1,17},{... | collective-permute-start | bytes 307208 | tf_op jit(solution)/shard_map/ppermute | solution.py:234
  41.0 4.2 %collective-permute-done.7.refs_1_ = f32[80,640]{1,0:T(8,128)S(1)} collective-permute-done((f32[80,640]{1,0:T(8,128)S(1)}, f32[80,640]{1,0:T(8,128)S(1)}, u32[]{:S(2)}, u32[]{:S(2)}) %collective-permute-start.7) | collective-permute-done | bytes 204832 | tf_op jit(solution)/shard_map/ppermute | solution.py:234
  45.5 3.2 %collective-permute-done.19.refs_0_ = f32[48,640]{1,0:T(8,128)S(1)} collective-permute-done((f32[48,640]{1,0:T(8,128)S(1)}, f32[48,640]{1,0:T(8,128)S(1)}, u32[]{:S(2)}, u32[]{:S(2)}) %collective-permute-start.19) | collective-permute-done | bytes 122912 | tf_op jit(solution)/shard_map/ppermute | solution.py:234
  48.7 1.1 %collective-permute-done.20.refs_1_ = f32[40,640]{1,0:T(8,128)S(1)} collective-permute-done((f32[40,640]{1,0:T(8,128)S(1)}, f32[40,640]{1,0:T(8,128)S(1)}, u32[]{:S(2)}, u32[]{:S(2)}) %collective-permute-start.20) | collective-permute-done | bytes 102432 | tf_op jit(solution)/shard_map/ppermute | solution.py:234
  49.8 0.9 %shard_map.59 = f32[3,80,640]{2,1,0:T(8,128)} custom-call(f32[80,640]{1,0:T(8,128)S(1)} %shard_map.50.keep_ref, f32[40,640]{1,0:T(8,128)S(1)} %shard_map.55.send_ref, f32[48,640]{1,0:T(8,128)S(1)} %collective-permute-done.19.refs_0_, f32[40,640]{1,0:T(8,128)S(1)} %collective-permute-done.20.refs_1_, f32[80,640]{1,0:T(8,128)S(1)} %shard_map.58.refs_2_), custom_call_target="tpu_custom_call" | custom-call | tf_op jit(solution)/shard_map/pallas_call | solution.py:374
  (24 shorter events, 1.0 us)
Async XLA Ops:
  2.0 9.1 %collective-permute-start.11 = (bf16[88,896]{1,0:T(8,128)(2,1)S(1)}, bf16[88,896]{1,0:T(8,128)(2,1)S(1)}, u32[]{:S(2)}, u32[]{:S(2)}) collective-permute-start(bf16[88,896]{1,0:T(8,128)(2,1)S(1)} %get-tuple-element.42), channel_id=1, source_target_pairs={{0,3},{1,2},{2,1},{3,0},{4,7},{5,6},{6,5},{7,4},{8,11},{9,10},{10,... | collective-permute-start | bytes 473096 | tf_op jit(solution)/shard_map/ppermute | solution.py:228
  5.9 7.9 %collective-permute-start.12 = (bf16[88,896]{1,0:T(8,128)(2,1)S(1)}, bf16[88,896]{1,0:T(8,128)(2,1)S(1)}, u32[]{:S(2)}, u32[]{:S(2)}) collective-permute-start(bf16[88,896]{1,0:T(8,128)(2,1)S(1)} %get-tuple-element.43), channel_id=1, source_target_pairs={{0,2},{1,3},{2,0},{3,1},{4,6},{5,7},{6,4},{7,5},{8,10},{9,11},{10,... | collective-permute-start | bytes 473096 | tf_op jit(solution)/shard_map/ppermute | solution.py:228
  6.4 8.4 %collective-permute-start.13 = (bf16[88,896]{1,0:T(8,128)(2,1)S(1)}, bf16[88,896]{1,0:T(8,128)(2,1)S(1)}, u32[]{:S(2)}, u32[]{:S(2)}) collective-permute-start(bf16[88,896]{1,0:T(8,128)(2,1)S(1)} %get-tuple-element.44), channel_id=1, source_target_pairs={{0,1},{1,0},{2,3},{3,2},{4,5},{5,4},{6,7},{7,6},{8,9},{9,8},{10,11... | collective-permute-start | bytes 473096 | tf_op jit(solution)/shard_map/ppermute | solution.py:228
  7.6 11.7 %collective-permute-start = (bf16[88,1280]{1,0:T(8,128)(2,1)S(1)}, bf16[88,1280]{1,0:T(8,128)(2,1)S(1)}, u32[]{:S(2)}, u32[]{:S(2)}) collective-permute-start(bf16[88,1280]{1,0:T(8,128)(2,1)S(1)} %get-tuple-element.31), channel_id=1, source_target_pairs={{0,2},{1,3},{2,0},{3,1},{4,6},{5,7},{6,4},{7,5},{8,10},{9,11},{10,... | collective-permute-start | bytes 675848 | tf_op jit(solution)/shard_map/ppermute | solution.py:228
  9.6 10.1 %collective-permute-start.1 = (bf16[88,1280]{1,0:T(8,128)(2,1)S(1)}, bf16[88,1280]{1,0:T(8,128)(2,1)S(1)}, u32[]{:S(2)}, u32[]{:S(2)}) collective-permute-start(bf16[88,1280]{1,0:T(8,128)(2,1)S(1)} %get-tuple-element.32), channel_id=1, source_target_pairs={{0,1},{1,0},{2,3},{3,2},{4,5},{5,4},{6,7},{7,6},{8,9},{9,8},{10,11... | collective-permute-start | bytes 675848 | tf_op jit(solution)/shard_map/ppermute | solution.py:228
  11.0 12.0 %collective-permute-start.2 = (bf16[88,1280]{1,0:T(8,128)(2,1)S(1)}, bf16[88,1280]{1,0:T(8,128)(2,1)S(1)}, u32[]{:S(2)}, u32[]{:S(2)}) collective-permute-start(bf16[88,1280]{1,0:T(8,128)(2,1)S(1)} %get-tuple-element.33), channel_id=1, source_target_pairs={{0,3},{1,2},{2,1},{3,0},{4,7},{5,6},{6,5},{7,4},{8,11},{9,10},{10,... | collective-permute-start | bytes 675848 | tf_op jit(solution)/shard_map/ppermute | solution.py:228
  15.4 2.0 %collective-permute-start.15 = (f32[88,512]{1,0:T(8,128)S(1)}, f32[88,512]{1,0:T(8,128)S(1)}, u32[]{:S(2)}, u32[]{:S(2)}) collective-permute-start(f32[88,512]{1,0:T(8,128)S(1)} %get-tuple-element.47), channel_id=1, source_target_pairs={{0,4},{4,0},{8,12},{12,8},{16,20},{20,16},{24,28},{28,24},{1,5},{5... | collective-permute-start | bytes 540680 | tf_op jit(solution)/shard_map/ppermute | solution.py:234
  15.5 1.6 %collective-permute-start.16 = (f32[80,512]{1,0:T(8,128)S(1)}, f32[80,512]{1,0:T(8,128)S(1)}, u32[]{:S(2)}, u32[]{:S(2)}) collective-permute-start(f32[80,512]{1,0:T(8,128)S(1)} %get-tuple-element.48), channel_id=1, source_target_pairs={{0,4},{4,0},{8,12},{12,8},{16,20},{20,16},{24,28},{28,24},{1,5},{5... | collective-permute-start | bytes 491528 | tf_op jit(solution)/shard_map/ppermute | solution.py:234
  17.1 10.3 %collective-permute-start.14 = (f32[168,512]{1,0:T(8,128)S(1)}, f32[168,512]{1,0:T(8,128)S(1)}, u32[]{:S(2)}, u32[]{:S(2)}) collective-permute-start(f32[168,512]{1,0:T(8,128)S(1)} %get-tuple-element.46), channel_id=1, source_target_pairs={{0,4},{4,0},{8,12},{12,8},{16,20},{20,16},{24,28},{28,24},{1,5},{5... | collective-permute-start | bytes 1032200 | tf_op jit(solution)/shard_map/ppermute | solution.py:234
  17.4 10.3 %collective-permute-start.17 = (f32[168,512]{1,0:T(8,128)S(1)}, f32[168,512]{1,0:T(8,128)S(1)}, u32[]{:S(2)}, u32[]{:S(2)}) collective-permute-start(f32[168,512]{1,0:T(8,128)S(1)} %shard_map.53), channel_id=1, source_target_pairs={{0,8},{4,12},{8,0},{12,4},{16,24},{20,28},{24,16},{28,20},{1,9},{5... | collective-permute-start | bytes 1032200 | tf_op jit(solution)/shard_map/ppermute | solution.py:234
  23.8 1.7 %collective-permute-start.4 = (f32[96,640]{1,0:T(8,128)S(1)}, f32[96,640]{1,0:T(8,128)S(1)}, u32[]{:S(2)}, u32[]{:S(2)}) collective-permute-start(f32[96,640]{1,0:T(8,128)S(1)} %get-tuple-element.36), channel_id=1, source_target_pairs={{0,4},{4,0},{8,12},{12,8},{16,20},{20,16},{24,28},{28,24},{1,5},{5... | collective-permute-start | bytes 737288 | tf_op jit(solution)/shard_map/ppermute | solution.py:234
  23.9 1.6 %collective-permute-start.9 = (f32[40,640]{1,0:T(8,128)S(1)}, f32[40,640]{1,0:T(8,128)S(1)}, u32[]{:S(2)}, u32[]{:S(2)}) collective-permute-start(f32[40,640]{1,0:T(8,128)S(1)} %get-tuple-element.40), channel_id=1, source_target_pairs={{0,4},{4,0},{8,12},{12,8},{16,20},{20,16},{24,28},{28,24},{1,5},{5... | collective-permute-start | bytes 307208 | tf_op jit(solution)/shard_map/ppermute | solution.py:234
  24.4 9.3 %collective-permute-start.8 = (f32[88,640]{1,0:T(8,128)S(1)}, f32[88,640]{1,0:T(8,128)S(1)}, u32[]{:S(2)}, u32[]{:S(2)}) collective-permute-start(f32[88,640]{1,0:T(8,128)S(1)} %get-tuple-element.39), channel_id=1, source_target_pairs={{0,4},{4,0},{8,12},{12,8},{16,20},{20,16},{24,28},{28,24},{1,5},{5... | collective-permute-start | bytes 675848 | tf_op jit(solution)/shard_map/ppermute | solution.py:234
  25.6 12.3 %collective-permute-start.10 = (f32[88,640]{1,0:T(8,128)S(1)}, f32[88,640]{1,0:T(8,128)S(1)}, u32[]{:S(2)}, u32[]{:S(2)}) collective-permute-start(f32[88,640]{1,0:T(8,128)S(1)} %shard_map.51), channel_id=1, source_target_pairs={{0,8},{4,12},{8,0},{12,4},{16,24},{20,28},{24,16},{28,20},{1,9},{5... | collective-permute-start | bytes 675848 | tf_op jit(solution)/shard_map/ppermute | solution.py:234
  27.7 10.7 %collective-permute-start.18 = (f32[88,512]{1,0:T(8,128)S(1)}, f32[88,512]{1,0:T(8,128)S(1)}, u32[]{:S(2)}, u32[]{:S(2)}) collective-permute-start(f32[88,512]{1,0:T(8,128)S(1)} %shard_map.54.send_ref), channel_id=1, source_target_pairs={{0,16},{4,20},{8,24},{12,28},{16,0},{20,4},{24,8},{28,12},{1,17},{... | collective-permute-start | bytes 540680 | tf_op jit(solution)/shard_map/ppermute | solution.py:234
  30.4 1.7 %collective-permute-start.6 = (f32[24,640]{1,0:T(8,128)S(1)}, f32[24,640]{1,0:T(8,128)S(1)}, u32[]{:S(2)}, u32[]{:S(2)}) collective-permute-start(f32[24,640]{1,0:T(8,128)S(1)} %get-tuple-element.38), channel_id=1, source_target_pairs={{0,4},{4,0},{8,12},{12,8},{16,20},{20,16},{24,28},{28,24},{1,5},{5... | collective-permute-start | bytes 184328 | tf_op jit(solution)/shard_map/ppermute | solution.py:234
  30.4 1.4 %collective-permute-start.5 = (f32[8,640]{1,0:T(8,128)S(1)}, f32[8,640]{1,0:T(8,128)S(1)}, u32[]{:S(2)}, u32[]{:S(2)}) collective-permute-start(f32[8,640]{1,0:T(8,128)S(1)} %get-tuple-element.37), channel_id=1, source_target_pairs={{0,4},{4,0},{8,12},{12,8},{16,20},{20,16},{24,28},{28,24},{1,5},{5... | collective-permute-start | bytes 61448 | tf_op jit(solution)/shard_map/ppermute | solution.py:234
  31.7 9.3 %collective-permute-start.3 = (f32[80,640]{1,0:T(8,128)S(1)}, f32[80,640]{1,0:T(8,128)S(1)}, u32[]{:S(2)}, u32[]{:S(2)}) collective-permute-start(f32[80,640]{1,0:T(8,128)S(1)} %get-tuple-element.35), channel_id=1, source_target_pairs={{0,4},{4,0},{8,12},{12,8},{16,20},{20,16},{24,28},{28,24},{1,5},{5... | collective-permute-start | bytes 614408 | tf_op jit(solution)/shard_map/ppermute | solution.py:234
  32.1 13.1 %collective-permute-start.7 = (f32[80,640]{1,0:T(8,128)S(1)}, f32[80,640]{1,0:T(8,128)S(1)}, u32[]{:S(2)}, u32[]{:S(2)}) collective-permute-start(f32[80,640]{1,0:T(8,128)S(1)} %shard_map.49), channel_id=1, source_target_pairs={{0,8},{4,12},{8,0},{12,4},{16,24},{20,28},{24,16},{28,20},{1,9},{5... | collective-permute-start | bytes 614408 | tf_op jit(solution)/shard_map/ppermute | solution.py:234
  37.9 10.8 %collective-permute-start.19 = (f32[48,640]{1,0:T(8,128)S(1)}, f32[48,640]{1,0:T(8,128)S(1)}, u32[]{:S(2)}, u32[]{:S(2)}) collective-permute-start(f32[48,640]{1,0:T(8,128)S(1)} %shard_map.56), channel_id=1, source_target_pairs={{0,16},{4,20},{8,24},{12,28},{16,0},{20,4},{24,8},{28,12},{1,17},{... | collective-permute-start | bytes 368648 | tf_op jit(solution)/shard_map/ppermute | solution.py:234
  38.5 11.3 %collective-permute-start.20 = (f32[40,640]{1,0:T(8,128)S(1)}, f32[40,640]{1,0:T(8,128)S(1)}, u32[]{:S(2)}, u32[]{:S(2)}) collective-permute-start(f32[40,640]{1,0:T(8,128)S(1)} %shard_map.55.send_ref), channel_id=1, source_target_pairs={{0,16},{4,20},{8,24},{12,28},{16,0},{20,4},{24,8},{28,12},{1,17},{... | collective-permute-start | bytes 307208 | tf_op jit(solution)/shard_map/ppermute | solution.py:234

commit v5 on v4

--- a/solution.py
+++ b/solution.py
@@ -29,11 +29,12 @@
     "first": "M",
     "order": {"F": (3, 2, 1), "S": (2, 1, 3)},
     "core": {"F": (88, 168), "S": (40, 136, 144, 168, 256)},
-    "z1": {"F": (), "S": (88,)},
+    "z1": {"F": (), "S": (88, 128)},
     "z2": {"F": (), "S": (48,)},
     "after": {
-        ("send", "S", 1): (("z2", "F", 0), ("z1", "S", 0)),
-        ("z1", "S", 1): (("got", "S", 2),),
+        ("send", "S", 1): (("z2", "F", 0),),
+        ("keep", "F"): (("z2", "F", 0),),
+        ("moments", "S"): (("core", "F", 0),),
     },
 }
 

time: 50.9 us -> 50.7 us (level)
    ppermute x15 -> x16, waiting for transfers between devices: 15.9 us -> 15.6 us  [swap(): return lax.ppermute(value, 'cycle', [(i, i ^ bit) for i in range(n)])]
    ppermute x15 -> x16, starting transfers between devices: 13.2 us -> 13.3 us  [swap(): return lax.ppermute(value, 'cycle', [(i, i ^ bit) for i in range(n)])]
  transfers between devices with their start and end apart: 21 -> 22, of which waited for: 12 -> 10; matrix products, arithmetic and copies ran while one was open for 0% -> 0% of each run, Pallas kernels for 5% -> 6%
where the time goes in v5:
time: 50.7 us; the launch traced here: 50.6 us
  starting transfers between devices  24.1 us (48%)
  waiting for transfers between devices  20.6 us (41%)
  Pallas kernels  5.68 us (11%)
    ppermute x16, waiting for transfers between devices, swap(): return lax.ppermute(value, 'cycle', [(i, i ^ bit) for i in range(n)])  15.6 us
    ppermute x16, starting transfers between devices, swap(): return lax.ppermute(value, 'cycle', [(i, i ^ bit) for i in range(n)])  13.3 us
    ppermute x6, starting transfers between devices, to_owners(): lax.ppermute(parts[k], 'bin', [(i, i ^ k) for i in range(n_bin)])  10.8 us
    ppermute x6, waiting for transfers between devices, to_owners(): lax.ppermute(parts[k], 'bin', [(i, i ^ k) for i in range(n_bin)])  5.03 us
    pallas_call x1, Pallas kernels, on_device(): pl.pallas_call(functools.partial(first_place_kernel, places[lanes['F']],...  1.97 us
    pallas_call x2, Pallas kernels, make(): pl.pallas_call(functools.partial(moment_kernel, lanes[p], rows_c, n_cycle...  1.34 us
  transfers between devices with their start and end apart: 22, of which 10 were waited for; matrix products, arithmetic and copies ran while one was open for 0% of the time, Pallas kernels for 6%

profile of v5, /device:TPU:0, one launch (start us, length us, event | category | flops | bytes accessed | tf_op | source)
XLA Modules:
  0.0 50.6 jit_solution(3850700482367621408)
XLA Ops:
  0.0 2.0 %shard_map.46 = (bf16[88,896]{1,0:T(8,128)(2,1)S(1)}, bf16[88,896]{1,0:T(8,128)(2,1)S(1)}, bf16[88,896]{1,0:T(8,128)(2,1)S(1)}, bf16[88,896]{1,0:T(8,128)(2,1)S(...) custom-call(s32[12]{0:T(128)} %order_hbm.1, s32[1,512]{1,0:T(1,128)} %bitcast.1, ...), custom_call_target="tpu_custom_call" | custom-call | tf_op jit(solution)/shard_map/pallas_call | solution.py:265
  2.0 4.0 %collective-permute-start.3 = (bf16[88,896]{1,0:T(8,128)(2,1)S(1)}, bf16[88,896]{1,0:T(8,128)(2,1)S(1)}, u32[]{:S(2)}, u32[]{:S(2)}) collective-permute-start(bf16[88,896]{1,0:T(8,128)(2,1)S(1)} %get-tuple-element.35), channel_id=1, source_target_pairs={{0,3},{1,2},{2,1},{3,0},{4,7},{5,6},{6,5},{7,4},{8,11},{9,10},{10,... | collective-permute-start | bytes 473096 | tf_op jit(solution)/shard_map/ppermute | solution.py:229
  5.9 0.5 %collective-permute-start.4 = (bf16[88,896]{1,0:T(8,128)(2,1)S(1)}, bf16[88,896]{1,0:T(8,128)(2,1)S(1)}, u32[]{:S(2)}, u32[]{:S(2)}) collective-permute-start(bf16[88,896]{1,0:T(8,128)(2,1)S(1)} %get-tuple-element.36), channel_id=1, source_target_pairs={{0,2},{1,3},{2,0},{3,1},{4,6},{5,7},{6,4},{7,5},{8,10},{9,11},{10,... | collective-permute-start | bytes 473096 | tf_op jit(solution)/shard_map/ppermute | solution.py:229
  6.4 0.1 collective-permute-start.5
  6.6 1.0 %shard_map.47 = (bf16[88,1280]{1,0:T(8,128)(2,1)S(1)}, bf16[88,1280]{1,0:T(8,128)(2,1)S(1)}, bf16[88,1280]{1,0:T(8,128)(2,1)S(1)}, bf16[88,1280]{1,0:T(8,128)(2,1)S(1)}) custom-call(s32[16,512]{1,0:T(8,128)S(1)} %get-tuple-element.27.keys_ref, bf16[512,640]{1,0:T(8,128)(2,1)S(1)} %get-tuple-element.28.bg_ref, bf16[512,640]{1,0:T(8,128)(2,1)S(1)} %get-tuple-element.29.an_ref), custom_call_target="tpu_custom_call" | custom-call | tf_op jit(solution)/shard_map/pallas_call | solution.py:279
  7.6 2.0 %collective-permute-start = (bf16[88,1280]{1,0:T(8,128)(2,1)S(1)}, bf16[88,1280]{1,0:T(8,128)(2,1)S(1)}, u32[]{:S(2)}, u32[]{:S(2)}) collective-permute-start(bf16[88,1280]{1,0:T(8,128)(2,1)S(1)} %get-tuple-element.31), channel_id=1, source_target_pairs={{0,2},{1,3},{2,0},{3,1},{4,6},{5,7},{6,4},{7,5},{8,10},{9,11},{10,... | collective-permute-start | bytes 675848 | tf_op jit(solution)/shard_map/ppermute | solution.py:229
  9.6 1.5 %collective-permute-start.1 = (bf16[88,1280]{1,0:T(8,128)(2,1)S(1)}, bf16[88,1280]{1,0:T(8,128)(2,1)S(1)}, u32[]{:S(2)}, u32[]{:S(2)}) collective-permute-start(bf16[88,1280]{1,0:T(8,128)(2,1)S(1)} %get-tuple-element.32), channel_id=1, source_target_pairs={{0,1},{1,0},{2,3},{3,2},{4,5},{5,4},{6,7},{7,6},{8,9},{9,8},{10,11... | collective-permute-start | bytes 675848 | tf_op jit(solution)/shard_map/ppermute | solution.py:229
  11.1 2.7 %collective-permute-start.2 = (bf16[88,1280]{1,0:T(8,128)(2,1)S(1)}, bf16[88,1280]{1,0:T(8,128)(2,1)S(1)}, u32[]{:S(2)}, u32[]{:S(2)}) collective-permute-start(bf16[88,1280]{1,0:T(8,128)(2,1)S(1)} %get-tuple-element.33), channel_id=1, source_target_pairs={{0,3},{1,2},{2,1},{3,0},{4,7},{5,6},{6,5},{7,4},{8,11},{9,10},{10,... | collective-permute-start | bytes 675848 | tf_op jit(solution)/shard_map/ppermute | solution.py:229
  13.8 1.0 %collective-permute-done.5.refs_3_ = bf16[88,896]{1,0:T(8,128)(2,1)S(1)} collective-permute-done((bf16[88,896]{1,0:T(8,128)(2,1)S(1)}, bf16[88,896]{1,0:T(8,128)(2,1)S(1)}, u32[]{:S(2)}, u32[]{:S(2)}) %collective-permute-start.5) | collective-permute-done | bytes 157728 | tf_op jit(solution)/shard_map/ppermute | solution.py:229
  14.8 0.5 %shard_map.48 = (f32[88,512]{1,0:T(8,128)S(1)}, f32[80,512]{1,0:T(8,128)S(1)}, f32[168,512]{1,0:T(8,128)S(1)}, f32[336,512]{1,0:T(8,128)S(1)}) custom-call(bf16[88,896]{1,0:T(8,128)(2,1)S(1)} %get-tuple-element.34.refs_0_, bf16[88,896]{1,0:T(8,128)(2,1)S(1)} %collective-permute-done.3.refs_1_, bf16[88,896]{1,0:T(8,128)(2,1)S(1)} %collective-permute-done.4.refs_2_, ...), custom_call_target="tpu_custom_call" | custom-call | tf_op jit(solution)/shard_map/pallas_call | solution.py:332
  15.5 0.5 collective-permute-start.17
  15.9 1.1 %collective-permute-done.17.refs_1_ = f32[80,512]{1,0:T(8,128)S(1)} collective-permute-done((f32[80,512]{1,0:T(8,128)S(1)}, f32[80,512]{1,0:T(8,128)S(1)}, u32[]{:S(2)}, u32[]{:S(2)}) %collective-permute-start.17) | collective-permute-done | bytes 163872 | tf_op jit(solution)/shard_map/ppermute | solution.py:235
  17.1 0.3 collective-permute-start.16
  17.4 1.6 %collective-permute-start.18 = (f32[168,512]{1,0:T(8,128)S(1)}, f32[168,512]{1,0:T(8,128)S(1)}, u32[]{:S(2)}, u32[]{:S(2)}) collective-permute-start(f32[168,512]{1,0:T(8,128)S(1)} %shard_map.54), channel_id=1, source_target_pairs={{0,8},{4,12},{8,0},{12,4},{16,24},{20,28},{24,16},{28,20},{1,9},{5... | collective-permute-start | bytes 1032200 | tf_op jit(solution)/shard_map/ppermute | solution.py:235
  19.0 0.2 collective-permute-done.refs_1_
  19.2 0.4 collective-permute-done.1.refs_2_
  19.6 3.4 %collective-permute-done.2.refs_3_ = bf16[88,1280]{1,0:T(8,128)(2,1)S(1)} collective-permute-done((bf16[88,1280]{1,0:T(8,128)(2,1)S(1)}, bf16[88,1280]{1,0:T(8,128)(2,1)S(1)}, u32[]{:S(2)}, u32[]{:S(2)}) %collective-permute-start.2) | collective-permute-done | bytes 225312 | tf_op jit(solution)/shard_map/ppermute | solution.py:229
  23.0 0.8 %shard_map.49 = (f32[40,640]{1,0:T(8,128)S(1)}, f32[96,640]{1,0:T(8,128)S(1)}, f32[8,640]{1,0:T(8,128)S(1)}, f32[24,640]{1,0:T(8,128)S(1)}, f32[88,640]{1,0:T(8,...) custom-call(bf16[88,1280]{1,0:T(8,128)(2,1)S(1)} %get-tuple-element.30.refs_0_, ...), custom_call_target="tpu_custom_call" | custom-call | tf_op jit(solution)/shard_map/pallas_call | solution.py:332
  23.9 0.5 collective-permute-start.14
  24.5 1.1 %collective-permute-done.14.refs_0_ = f32[40,640]{1,0:T(8,128)S(1)} collective-permute-done((f32[40,640]{1,0:T(8,128)S(1)}, f32[40,640]{1,0:T(8,128)S(1)}, u32[]{:S(2)}, u32[]{:S(2)}) %collective-permute-start.14) | collective-permute-done | bytes 102432 | tf_op jit(solution)/shard_map/ppermute | solution.py:235
  25.6 1.8 %collective-permute-start.15 = (f32[88,640]{1,0:T(8,128)S(1)}, f32[88,640]{1,0:T(8,128)S(1)}, u32[]{:S(2)}, u32[]{:S(2)}) collective-permute-start(f32[88,640]{1,0:T(8,128)S(1)} %shard_map.53), channel_id=1, source_target_pairs={{0,8},{4,12},{8,0},{12,4},{16,24},{20,28},{24,16},{28,20},{1,9},{5... | collective-permute-start | bytes 675848 | tf_op jit(solution)/shard_map/ppermute | solution.py:235
  27.4 0.2 collective-permute-done.18.refs_1_
  27.7 2.7 %collective-permute-start.19 = (f32[88,512]{1,0:T(8,128)S(1)}, f32[88,512]{1,0:T(8,128)S(1)}, u32[]{:S(2)}, u32[]{:S(2)}) collective-permute-start(f32[88,512]{1,0:T(8,128)S(1)} %shard_map.55.send_ref), channel_id=1, source_target_pairs={{0,16},{4,20},{8,24},{12,28},{16,0},{20,4},{24,8},{28,12},{1,17},{... | collective-permute-start | bytes 540680 | tf_op jit(solution)/shard_map/ppermute | solution.py:235
  30.4 0.5 %collective-permute-start.11 = (f32[24,640]{1,0:T(8,128)S(1)}, f32[24,640]{1,0:T(8,128)S(1)}, u32[]{:S(2)}, u32[]{:S(2)}) collective-permute-start(f32[24,640]{1,0:T(8,128)S(1)} %get-tuple-element.43), channel_id=1, source_target_pairs={{0,4},{4,0},{8,12},{12,8},{16,20},{20,16},{24,28},{28,24},{1,5},{5... | collective-permute-start | bytes 184328 | tf_op jit(solution)/shard_map/ppermute | solution.py:235
  30.9 6.2 %collective-permute-done.15.refs_1_ = f32[88,640]{1,0:T(8,128)S(1)} collective-permute-done((f32[88,640]{1,0:T(8,128)S(1)}, f32[88,640]{1,0:T(8,128)S(1)}, u32[]{:S(2)}, u32[]{:S(2)}) %collective-permute-start.15) | collective-permute-done | bytes 225312 | tf_op jit(solution)/shard_map/ppermute | solution.py:235
  37.2 0.6 %collective-permute-start.20 = (f32[48,640]{1,0:T(8,128)S(1)}, f32[48,640]{1,0:T(8,128)S(1)}, u32[]{:S(2)}, u32[]{:S(2)}) collective-permute-start(f32[48,640]{1,0:T(8,128)S(1)} %shard_map.57), channel_id=1, source_target_pairs={{0,16},{4,20},{8,24},{12,28},{16,0},{20,4},{24,8},{28,12},{1,17},{... | collective-permute-start | bytes 368648 | tf_op jit(solution)/shard_map/ppermute | solution.py:235
  37.8 2.5 %collective-permute-start.9 = (f32[40,640]{1,0:T(8,128)S(1)}, f32[40,640]{1,0:T(8,128)S(1)}, u32[]{:S(2)}, u32[]{:S(2)}) collective-permute-start(f32[40,640]{1,0:T(8,128)S(1)} %shard_map.50), channel_id=1, source_target_pairs={{0,8},{4,12},{8,0},{12,4},{16,24},{20,28},{24,16},{28,20},{1,9},{5... | collective-permute-start | bytes 307208 | tf_op jit(solution)/shard_map/ppermute | solution.py:235
  40.5 2.0 %collective-permute-start.21 = (f32[40,640]{1,0:T(8,128)S(1)}, f32[40,640]{1,0:T(8,128)S(1)}, u32[]{:S(2)}, u32[]{:S(2)}) collective-permute-start(f32[40,640]{1,0:T(8,128)S(1)} %shard_map.56.send_ref), channel_id=1, source_target_pairs={{0,16},{4,20},{8,24},{12,28},{16,0},{20,4},{24,8},{28,12},{1,17},{... | collective-permute-start | bytes 307208 | tf_op jit(solution)/shard_map/ppermute | solution.py:235
  42.5 5.8 %collective-permute-done.9.refs_1_ = f32[40,640]{1,0:T(8,128)S(1)} collective-permute-done((f32[40,640]{1,0:T(8,128)S(1)}, f32[40,640]{1,0:T(8,128)S(1)}, u32[]{:S(2)}, u32[]{:S(2)}) %collective-permute-start.9) | collective-permute-done | bytes 102432 | tf_op jit(solution)/shard_map/ppermute | solution.py:235
  48.2 1.1 %collective-permute-done.12.refs_2_ = f32[40,640]{1,0:T(8,128)S(1)} collective-permute-done((f32[40,640]{1,0:T(8,128)S(1)}, f32[40,640]{1,0:T(8,128)S(1)}, u32[]{:S(2)}, u32[]{:S(2)}) %collective-permute-start.12) | collective-permute-done | bytes 102432 | tf_op jit(solution)/shard_map/ppermute | solution.py:235
  49.4 0.2 shard_map.59.refs_2_
  49.7 0.9 %shard_map.60 = f32[3,80,640]{2,1,0:T(8,128)} custom-call(f32[80,640]{1,0:T(8,128)S(1)} %shard_map.52.keep_ref, f32[40,640]{1,0:T(8,128)S(1)} %shard_map.56.send_ref, f32[48,640]{1,0:T(8,128)S(1)} %collective-permute-done.20.refs_0_, f32[40,640]{1,0:T(8,128)S(1)} %collective-permute-done.21.refs_1_, f32[80,640]{1,0:T(8,128)S(1)} %shard_map.59.refs_2_), custom_call_target="tpu_custom_call" | custom-call | tf_op jit(solution)/shard_map/pallas_call | solution.py:375
  (27 shorter events, 0.6 us)
Async XLA Ops:
  2.0 9.1 %collective-permute-start.3 = (bf16[88,896]{1,0:T(8,128)(2,1)S(1)}, bf16[88,896]{1,0:T(8,128)(2,1)S(1)}, u32[]{:S(2)}, u32[]{:S(2)}) collective-permute-start(bf16[88,896]{1,0:T(8,128)(2,1)S(1)} %get-tuple-element.35), channel_id=1, source_target_pairs={{0,3},{1,2},{2,1},{3,0},{4,7},{5,6},{6,5},{7,4},{8,11},{9,10},{10,... | collective-permute-start | bytes 473096 | tf_op jit(solution)/shard_map/ppermute | solution.py:229
  5.9 7.9 %collective-permute-start.4 = (bf16[88,896]{1,0:T(8,128)(2,1)S(1)}, bf16[88,896]{1,0:T(8,128)(2,1)S(1)}, u32[]{:S(2)}, u32[]{:S(2)}) collective-permute-start(bf16[88,896]{1,0:T(8,128)(2,1)S(1)} %get-tuple-element.36), channel_id=1, source_target_pairs={{0,2},{1,3},{2,0},{3,1},{4,6},{5,7},{6,4},{7,5},{8,10},{9,11},{10,... | collective-permute-start | bytes 473096 | tf_op jit(solution)/shard_map/ppermute | solution.py:229
  6.4 8.4 %collective-permute-start.5 = (bf16[88,896]{1,0:T(8,128)(2,1)S(1)}, bf16[88,896]{1,0:T(8,128)(2,1)S(1)}, u32[]{:S(2)}, u32[]{:S(2)}) collective-permute-start(bf16[88,896]{1,0:T(8,128)(2,1)S(1)} %get-tuple-element.37), channel_id=1, source_target_pairs={{0,1},{1,0},{2,3},{3,2},{4,5},{5,4},{6,7},{7,6},{8,9},{9,8},{10,11... | collective-permute-start | bytes 473096 | tf_op jit(solution)/shard_map/ppermute | solution.py:229
  7.6 11.7 %collective-permute-start = (bf16[88,1280]{1,0:T(8,128)(2,1)S(1)}, bf16[88,1280]{1,0:T(8,128)(2,1)S(1)}, u32[]{:S(2)}, u32[]{:S(2)}) collective-permute-start(bf16[88,1280]{1,0:T(8,128)(2,1)S(1)} %get-tuple-element.31), channel_id=1, source_target_pairs={{0,2},{1,3},{2,0},{3,1},{4,6},{5,7},{6,4},{7,5},{8,10},{9,11},{10,... | collective-permute-start | bytes 675848 | tf_op jit(solution)/shard_map/ppermute | solution.py:229
  9.6 10.1 %collective-permute-start.1 = (bf16[88,1280]{1,0:T(8,128)(2,1)S(1)}, bf16[88,1280]{1,0:T(8,128)(2,1)S(1)}, u32[]{:S(2)}, u32[]{:S(2)}) collective-permute-start(bf16[88,1280]{1,0:T(8,128)(2,1)S(1)} %get-tuple-element.32), channel_id=1, source_target_pairs={{0,1},{1,0},{2,3},{3,2},{4,5},{5,4},{6,7},{7,6},{8,9},{9,8},{10,11... | collective-permute-start | bytes 675848 | tf_op jit(solution)/shard_map/ppermute | solution.py:229
  11.1 12.0 %collective-permute-start.2 = (bf16[88,1280]{1,0:T(8,128)(2,1)S(1)}, bf16[88,1280]{1,0:T(8,128)(2,1)S(1)}, u32[]{:S(2)}, u32[]{:S(2)}) collective-permute-start(bf16[88,1280]{1,0:T(8,128)(2,1)S(1)} %get-tuple-element.33), channel_id=1, source_target_pairs={{0,3},{1,2},{2,1},{3,0},{4,7},{5,6},{6,5},{7,4},{8,11},{9,10},{10,... | collective-permute-start | bytes 675848 | tf_op jit(solution)/shard_map/ppermute | solution.py:229
  15.4 2.0 %collective-permute-start.6 = (f32[88,512]{1,0:T(8,128)S(1)}, f32[88,512]{1,0:T(8,128)S(1)}, u32[]{:S(2)}, u32[]{:S(2)}) collective-permute-start(f32[88,512]{1,0:T(8,128)S(1)} %get-tuple-element.38), channel_id=1, source_target_pairs={{0,4},{4,0},{8,12},{12,8},{16,20},{20,16},{24,28},{28,24},{1,5},{5... | collective-permute-start | bytes 540680 | tf_op jit(solution)/shard_map/ppermute | solution.py:235
  15.5 1.6 %collective-permute-start.17 = (f32[80,512]{1,0:T(8,128)S(1)}, f32[80,512]{1,0:T(8,128)S(1)}, u32[]{:S(2)}, u32[]{:S(2)}) collective-permute-start(f32[80,512]{1,0:T(8,128)S(1)} %get-tuple-element.48), channel_id=1, source_target_pairs={{0,4},{4,0},{8,12},{12,8},{16,20},{20,16},{24,28},{28,24},{1,5},{5... | collective-permute-start | bytes 491528 | tf_op jit(solution)/shard_map/ppermute | solution.py:235
  17.1 10.3 %collective-permute-start.16 = (f32[168,512]{1,0:T(8,128)S(1)}, f32[168,512]{1,0:T(8,128)S(1)}, u32[]{:S(2)}, u32[]{:S(2)}) collective-permute-start(f32[168,512]{1,0:T(8,128)S(1)} %get-tuple-element.47), channel_id=1, source_target_pairs={{0,4},{4,0},{8,12},{12,8},{16,20},{20,16},{24,28},{28,24},{1,5},{5... | collective-permute-start | bytes 1032200 | tf_op jit(solution)/shard_map/ppermute | solution.py:235
  17.4 10.3 %collective-permute-start.18 = (f32[168,512]{1,0:T(8,128)S(1)}, f32[168,512]{1,0:T(8,128)S(1)}, u32[]{:S(2)}, u32[]{:S(2)}) collective-permute-start(f32[168,512]{1,0:T(8,128)S(1)} %shard_map.54), channel_id=1, source_target_pairs={{0,8},{4,12},{8,0},{12,4},{16,24},{20,28},{24,16},{28,20},{1,9},{5... | collective-permute-start | bytes 1032200 | tf_op jit(solution)/shard_map/ppermute | solution.py:235
  23.8 1.7 %collective-permute-start.8 = (f32[96,640]{1,0:T(8,128)S(1)}, f32[96,640]{1,0:T(8,128)S(1)}, u32[]{:S(2)}, u32[]{:S(2)}) collective-permute-start(f32[96,640]{1,0:T(8,128)S(1)} %get-tuple-element.41), channel_id=1, source_target_pairs={{0,4},{4,0},{8,12},{12,8},{16,20},{20,16},{24,28},{28,24},{1,5},{5... | collective-permute-start | bytes 737288 | tf_op jit(solution)/shard_map/ppermute | solution.py:235
  23.9 1.6 %collective-permute-start.14 = (f32[40,640]{1,0:T(8,128)S(1)}, f32[40,640]{1,0:T(8,128)S(1)}, u32[]{:S(2)}, u32[]{:S(2)}) collective-permute-start(f32[40,640]{1,0:T(8,128)S(1)} %get-tuple-element.45), channel_id=1, source_target_pairs={{0,4},{4,0},{8,12},{12,8},{16,20},{20,16},{24,28},{28,24},{1,5},{5... | collective-permute-start | bytes 307208 | tf_op jit(solution)/shard_map/ppermute | solution.py:235
  24.4 6.5 %collective-permute-start.13 = (f32[88,640]{1,0:T(8,128)S(1)}, f32[88,640]{1,0:T(8,128)S(1)}, u32[]{:S(2)}, u32[]{:S(2)}) collective-permute-start(f32[88,640]{1,0:T(8,128)S(1)} %get-tuple-element.44), channel_id=1, source_target_pairs={{0,4},{4,0},{8,12},{12,8},{16,20},{20,16},{24,28},{28,24},{1,5},{5... | collective-permute-start | bytes 675848 | tf_op jit(solution)/shard_map/ppermute | solution.py:235
  25.6 11.5 %collective-permute-start.15 = (f32[88,640]{1,0:T(8,128)S(1)}, f32[88,640]{1,0:T(8,128)S(1)}, u32[]{:S(2)}, u32[]{:S(2)}) collective-permute-start(f32[88,640]{1,0:T(8,128)S(1)} %shard_map.53), channel_id=1, source_target_pairs={{0,8},{4,12},{8,0},{12,4},{16,24},{20,28},{24,16},{28,20},{1,9},{5... | collective-permute-start | bytes 675848 | tf_op jit(solution)/shard_map/ppermute | solution.py:235
  27.7 12.7 %collective-permute-start.19 = (f32[88,512]{1,0:T(8,128)S(1)}, f32[88,512]{1,0:T(8,128)S(1)}, u32[]{:S(2)}, u32[]{:S(2)}) collective-permute-start(f32[88,512]{1,0:T(8,128)S(1)} %shard_map.55.send_ref), channel_id=1, source_target_pairs={{0,16},{4,20},{8,24},{12,28},{16,0},{20,4},{24,8},{28,12},{1,17},{... | collective-permute-start | bytes 540680 | tf_op jit(solution)/shard_map/ppermute | solution.py:235
  30.4 12.1 %collective-permute-start.7 = (f32[80,640]{1,0:T(8,128)S(1)}, f32[80,640]{1,0:T(8,128)S(1)}, u32[]{:S(2)}, u32[]{:S(2)}) collective-permute-start(f32[80,640]{1,0:T(8,128)S(1)} %get-tuple-element.40), channel_id=1, source_target_pairs={{0,4},{4,0},{8,12},{12,8},{16,20},{20,16},{24,28},{28,24},{1,5},{5... | collective-permute-start | bytes 614408 | tf_op jit(solution)/shard_map/ppermute | solution.py:235
  30.4 10.0 %collective-permute-start.11 = (f32[24,640]{1,0:T(8,128)S(1)}, f32[24,640]{1,0:T(8,128)S(1)}, u32[]{:S(2)}, u32[]{:S(2)}) collective-permute-start(f32[24,640]{1,0:T(8,128)S(1)} %get-tuple-element.43), channel_id=1, source_target_pairs={{0,4},{4,0},{8,12},{12,8},{16,20},{20,16},{24,28},{28,24},{1,5},{5... | collective-permute-start | bytes 184328 | tf_op jit(solution)/shard_map/ppermute | solution.py:235
  30.9 6.9 %collective-permute-start.10 = (f32[8,640]{1,0:T(8,128)S(1)}, f32[8,640]{1,0:T(8,128)S(1)}, u32[]{:S(2)}, u32[]{:S(2)}) collective-permute-start(f32[8,640]{1,0:T(8,128)S(1)} %get-tuple-element.42), channel_id=1, source_target_pairs={{0,4},{4,0},{8,12},{12,8},{16,20},{20,16},{24,28},{28,24},{1,5},{5... | collective-permute-start | bytes 61448 | tf_op jit(solution)/shard_map/ppermute | solution.py:235
  37.2 12.5 %collective-permute-start.20 = (f32[48,640]{1,0:T(8,128)S(1)}, f32[48,640]{1,0:T(8,128)S(1)}, u32[]{:S(2)}, u32[]{:S(2)}) collective-permute-start(f32[48,640]{1,0:T(8,128)S(1)} %shard_map.57), channel_id=1, source_target_pairs={{0,16},{4,20},{8,24},{12,28},{16,0},{20,4},{24,8},{28,12},{1,17},{... | collective-permute-start | bytes 368648 | tf_op jit(solution)/shard_map/ppermute | solution.py:235
  37.8 10.4 %collective-permute-start.9 = (f32[40,640]{1,0:T(8,128)S(1)}, f32[40,640]{1,0:T(8,128)S(1)}, u32[]{:S(2)}, u32[]{:S(2)}) collective-permute-start(f32[40,640]{1,0:T(8,128)S(1)} %shard_map.50), channel_id=1, source_target_pairs={{0,8},{4,12},{8,0},{12,4},{16,24},{20,28},{24,16},{28,20},{1,9},{5... | collective-permute-start | bytes 307208 | tf_op jit(solution)/shard_map/ppermute | solution.py:235
  40.4 9.0 %collective-permute-start.12 = (f32[40,640]{1,0:T(8,128)S(1)}, f32[40,640]{1,0:T(8,128)S(1)}, u32[]{:S(2)}, u32[]{:S(2)}) collective-permute-start(f32[40,640]{1,0:T(8,128)S(1)} %shard_map.51), channel_id=1, source_target_pairs={{0,8},{4,12},{8,0},{12,4},{16,24},{20,28},{24,16},{28,20},{1,9},{5... | collective-permute-start | bytes 307208 | tf_op jit(solution)/shard_map/ppermute | solution.py:235
  40.5 9.2 %collective-permute-start.21 = (f32[40,640]{1,0:T(8,128)S(1)}, f32[40,640]{1,0:T(8,128)S(1)}, u32[]{:S(2)}, u32[]{:S(2)}) collective-permute-start(f32[40,640]{1,0:T(8,128)S(1)} %shard_map.56.send_ref), channel_id=1, source_target_pairs={{0,16},{4,20},{8,24},{12,28},{16,0},{20,4},{24,8},{28,12},{1,17},{... | collective-permute-start | bytes 307208 | tf_op jit(solution)/shard_map/ppermute | solution.py:235

commit v6 on v5

--- a/solution.py
+++ b/solution.py
@@ -72,9 +72,11 @@
 
 
 def marked(values, limit, one_at):
-    lane = lax.broadcasted_iota(jnp.int32, values.shape, 1)
-    ones = jnp.where(lane == one_at, 1.0, 0.0)
-    return jnp.where(lane < limit, values.astype(jnp.float32), ones).astype(jnp.bfloat16)
+    first = limit // 128 * 128
+    last = values[:, first : first + 128]
+    lane = lax.broadcasted_iota(jnp.int32, last.shape, 1) + first
+    last = jnp.where(lane < limit, last.astype(jnp.float32), jnp.where(lane == one_at, 1.0, 0.0)).astype(jnp.bfloat16)
+    return jnp.concatenate([values[:, :first], last], axis=1) if first else last
 
 
 def place_wide(keys, out_refs, part, values, n_bin, per_owner, slots):

time: 50.7 us -> 50.7 us (level)
  no operation moved by 1% of the time
where the time goes in v6:
time: 50.7 us; the launch traced here: 50.6 us
  starting transfers between devices  24.1 us (48%)
  waiting for transfers between devices  20.6 us (41%)
  Pallas kernels  5.68 us (11%)
    ppermute x16, waiting for transfers between devices, swap(): return lax.ppermute(value, 'cycle', [(i, i ^ bit) for i in range(n)])  15.6 us
    ppermute x16, starting transfers between devices, swap(): return lax.ppermute(value, 'cycle', [(i, i ^ bit) for i in range(n)])  13.3 us
    ppermute x6, starting transfers between devices, to_owners(): lax.ppermute(parts[k], 'bin', [(i, i ^ k) for i in range(n_bin)])  10.8 us
    ppermute x6, waiting for transfers between devices, to_owners(): lax.ppermute(parts[k], 'bin', [(i, i ^ k) for i in range(n_bin)])  5.03 us
    pallas_call x1, Pallas kernels, on_device(): pl.pallas_call(functools.partial(first_place_kernel, places[lanes['F']],...  1.97 us
    pallas_call x2, Pallas kernels, make(): pl.pallas_call(functools.partial(moment_kernel, lanes[p], rows_c, n_cycle...  1.34 us
  transfers between devices with their start and end apart: 22, of which 10 were waited for; matrix products, arithmetic and copies ran while one was open for 0% of the time, Pallas kernels for 6%

profile of v6, /device:TPU:0, one launch (start us, length us, event | category | flops | bytes accessed | tf_op | source)
XLA Modules:
  0.0 50.6 jit_solution(4835998844536067725)
XLA Ops:
  0.0 2.0 %shard_map.46 = (bf16[88,896]{1,0:T(8,128)(2,1)S(1)}, bf16[88,896]{1,0:T(8,128)(2,1)S(1)}, bf16[88,896]{1,0:T(8,128)(2,1)S(1)}, bf16[88,896]{1,0:T(8,128)(2,1)S(...) custom-call(s32[12]{0:T(128)} %order_hbm.1, s32[1,512]{1,0:T(1,128)} %bitcast.1, ...), custom_call_target="tpu_custom_call" | custom-call | tf_op jit(solution)/shard_map/pallas_call | solution.py:267
  2.0 4.0 %collective-permute-start.3 = (bf16[88,896]{1,0:T(8,128)(2,1)S(1)}, bf16[88,896]{1,0:T(8,128)(2,1)S(1)}, u32[]{:S(2)}, u32[]{:S(2)}) collective-permute-start(bf16[88,896]{1,0:T(8,128)(2,1)S(1)} %get-tuple-element.35), channel_id=1, source_target_pairs={{0,3},{1,2},{2,1},{3,0},{4,7},{5,6},{6,5},{7,4},{8,11},{9,10},{10,... | collective-permute-start | bytes 473096 | tf_op jit(solution)/shard_map/ppermute | solution.py:231
  5.9 0.5 %collective-permute-start.4 = (bf16[88,896]{1,0:T(8,128)(2,1)S(1)}, bf16[88,896]{1,0:T(8,128)(2,1)S(1)}, u32[]{:S(2)}, u32[]{:S(2)}) collective-permute-start(bf16[88,896]{1,0:T(8,128)(2,1)S(1)} %get-tuple-element.36), channel_id=1, source_target_pairs={{0,2},{1,3},{2,0},{3,1},{4,6},{5,7},{6,4},{7,5},{8,10},{9,11},{10,... | collective-permute-start | bytes 473096 | tf_op jit(solution)/shard_map/ppermute | solution.py:231
  6.4 0.1 collective-permute-start.5
  6.6 1.0 %shard_map.47 = (bf16[88,1280]{1,0:T(8,128)(2,1)S(1)}, bf16[88,1280]{1,0:T(8,128)(2,1)S(1)}, bf16[88,1280]{1,0:T(8,128)(2,1)S(1)}, bf16[88,1280]{1,0:T(8,128)(2,1)S(1)}) custom-call(s32[16,512]{1,0:T(8,128)S(1)} %get-tuple-element.27.keys_ref, bf16[512,640]{1,0:T(8,128)(2,1)S(1)} %get-tuple-element.28.bg_ref, bf16[512,640]{1,0:T(8,128)(2,1)S(1)} %get-tuple-element.29.an_ref), custom_call_target="tpu_custom_call" | custom-call | tf_op jit(solution)/shard_map/pallas_call | solution.py:281
  7.6 2.0 %collective-permute-start = (bf16[88,1280]{1,0:T(8,128)(2,1)S(1)}, bf16[88,1280]{1,0:T(8,128)(2,1)S(1)}, u32[]{:S(2)}, u32[]{:S(2)}) collective-permute-start(bf16[88,1280]{1,0:T(8,128)(2,1)S(1)} %get-tuple-element.31), channel_id=1, source_target_pairs={{0,2},{1,3},{2,0},{3,1},{4,6},{5,7},{6,4},{7,5},{8,10},{9,11},{10,... | collective-permute-start | bytes 675848 | tf_op jit(solution)/shard_map/ppermute | solution.py:231
  9.6 1.5 %collective-permute-start.1 = (bf16[88,1280]{1,0:T(8,128)(2,1)S(1)}, bf16[88,1280]{1,0:T(8,128)(2,1)S(1)}, u32[]{:S(2)}, u32[]{:S(2)}) collective-permute-start(bf16[88,1280]{1,0:T(8,128)(2,1)S(1)} %get-tuple-element.32), channel_id=1, source_target_pairs={{0,1},{1,0},{2,3},{3,2},{4,5},{5,4},{6,7},{7,6},{8,9},{9,8},{10,11... | collective-permute-start | bytes 675848 | tf_op jit(solution)/shard_map/ppermute | solution.py:231
  11.1 2.7 %collective-permute-start.2 = (bf16[88,1280]{1,0:T(8,128)(2,1)S(1)}, bf16[88,1280]{1,0:T(8,128)(2,1)S(1)}, u32[]{:S(2)}, u32[]{:S(2)}) collective-permute-start(bf16[88,1280]{1,0:T(8,128)(2,1)S(1)} %get-tuple-element.33), channel_id=1, source_target_pairs={{0,3},{1,2},{2,1},{3,0},{4,7},{5,6},{6,5},{7,4},{8,11},{9,10},{10,... | collective-permute-start | bytes 675848 | tf_op jit(solution)/shard_map/ppermute | solution.py:231
  13.8 1.0 %collective-permute-done.5.refs_3_ = bf16[88,896]{1,0:T(8,128)(2,1)S(1)} collective-permute-done((bf16[88,896]{1,0:T(8,128)(2,1)S(1)}, bf16[88,896]{1,0:T(8,128)(2,1)S(1)}, u32[]{:S(2)}, u32[]{:S(2)}) %collective-permute-start.5) | collective-permute-done | bytes 157728 | tf_op jit(solution)/shard_map/ppermute | solution.py:231
  14.8 0.5 %shard_map.48 = (f32[88,512]{1,0:T(8,128)S(1)}, f32[80,512]{1,0:T(8,128)S(1)}, f32[168,512]{1,0:T(8,128)S(1)}, f32[336,512]{1,0:T(8,128)S(1)}) custom-call(bf16[88,896]{1,0:T(8,128)(2,1)S(1)} %get-tuple-element.34.refs_0_, bf16[88,896]{1,0:T(8,128)(2,1)S(1)} %collective-permute-done.3.refs_1_, bf16[88,896]{1,0:T(8,128)(2,1)S(1)} %collective-permute-done.4.refs_2_, ...), custom_call_target="tpu_custom_call" | custom-call | tf_op jit(solution)/shard_map/pallas_call | solution.py:334
  15.5 0.5 collective-permute-start.17
  15.9 1.1 %collective-permute-done.17.refs_1_ = f32[80,512]{1,0:T(8,128)S(1)} collective-permute-done((f32[80,512]{1,0:T(8,128)S(1)}, f32[80,512]{1,0:T(8,128)S(1)}, u32[]{:S(2)}, u32[]{:S(2)}) %collective-permute-start.17) | collective-permute-done | bytes 163872 | tf_op jit(solution)/shard_map/ppermute | solution.py:237
  17.1 0.3 collective-permute-start.16
  17.4 1.6 %collective-permute-start.18 = (f32[168,512]{1,0:T(8,128)S(1)}, f32[168,512]{1,0:T(8,128)S(1)}, u32[]{:S(2)}, u32[]{:S(2)}) collective-permute-start(f32[168,512]{1,0:T(8,128)S(1)} %shard_map.54), channel_id=1, source_target_pairs={{0,8},{4,12},{8,0},{12,4},{16,24},{20,28},{24,16},{28,20},{1,9},{5... | collective-permute-start | bytes 1032200 | tf_op jit(solution)/shard_map/ppermute | solution.py:237
  19.0 0.2 collective-permute-done.refs_1_
  19.2 0.4 collective-permute-done.1.refs_2_
  19.6 3.4 %collective-permute-done.2.refs_3_ = bf16[88,1280]{1,0:T(8,128)(2,1)S(1)} collective-permute-done((bf16[88,1280]{1,0:T(8,128)(2,1)S(1)}, bf16[88,1280]{1,0:T(8,128)(2,1)S(1)}, u32[]{:S(2)}, u32[]{:S(2)}) %collective-permute-start.2) | collective-permute-done | bytes 225312 | tf_op jit(solution)/shard_map/ppermute | solution.py:231
  23.0 0.8 %shard_map.49 = (f32[40,640]{1,0:T(8,128)S(1)}, f32[96,640]{1,0:T(8,128)S(1)}, f32[8,640]{1,0:T(8,128)S(1)}, f32[24,640]{1,0:T(8,128)S(1)}, f32[88,640]{1,0:T(8,...) custom-call(bf16[88,1280]{1,0:T(8,128)(2,1)S(1)} %get-tuple-element.30.refs_0_, ...), custom_call_target="tpu_custom_call" | custom-call | tf_op jit(solution)/shard_map/pallas_call | solution.py:334
  23.9 0.5 collective-permute-start.14
  24.5 1.1 %collective-permute-done.14.refs_0_ = f32[40,640]{1,0:T(8,128)S(1)} collective-permute-done((f32[40,640]{1,0:T(8,128)S(1)}, f32[40,640]{1,0:T(8,128)S(1)}, u32[]{:S(2)}, u32[]{:S(2)}) %collective-permute-start.14) | collective-permute-done | bytes 102432 | tf_op jit(solution)/shard_map/ppermute | solution.py:237
  25.6 1.8 %collective-permute-start.15 = (f32[88,640]{1,0:T(8,128)S(1)}, f32[88,640]{1,0:T(8,128)S(1)}, u32[]{:S(2)}, u32[]{:S(2)}) collective-permute-start(f32[88,640]{1,0:T(8,128)S(1)} %shard_map.53), channel_id=1, source_target_pairs={{0,8},{4,12},{8,0},{12,4},{16,24},{20,28},{24,16},{28,20},{1,9},{5... | collective-permute-start | bytes 675848 | tf_op jit(solution)/shard_map/ppermute | solution.py:237
  27.4 0.2 collective-permute-done.18.refs_1_
  27.7 2.7 %collective-permute-start.19 = (f32[88,512]{1,0:T(8,128)S(1)}, f32[88,512]{1,0:T(8,128)S(1)}, u32[]{:S(2)}, u32[]{:S(2)}) collective-permute-start(f32[88,512]{1,0:T(8,128)S(1)} %shard_map.55.send_ref), channel_id=1, source_target_pairs={{0,16},{4,20},{8,24},{12,28},{16,0},{20,4},{24,8},{28,12},{1,17},{... | collective-permute-start | bytes 540680 | tf_op jit(solution)/shard_map/ppermute | solution.py:237
  30.4 0.5 %collective-permute-start.11 = (f32[24,640]{1,0:T(8,128)S(1)}, f32[24,640]{1,0:T(8,128)S(1)}, u32[]{:S(2)}, u32[]{:S(2)}) collective-permute-start(f32[24,640]{1,0:T(8,128)S(1)} %get-tuple-element.43), channel_id=1, source_target_pairs={{0,4},{4,0},{8,12},{12,8},{16,20},{20,16},{24,28},{28,24},{1,5},{5... | collective-permute-start | bytes 184328 | tf_op jit(solution)/shard_map/ppermute | solution.py:237
  30.9 6.2 %collective-permute-done.15.refs_1_ = f32[88,640]{1,0:T(8,128)S(1)} collective-permute-done((f32[88,640]{1,0:T(8,128)S(1)}, f32[88,640]{1,0:T(8,128)S(1)}, u32[]{:S(2)}, u32[]{:S(2)}) %collective-permute-start.15) | collective-permute-done | bytes 225312 | tf_op jit(solution)/shard_map/ppermute | solution.py:237
  37.2 0.6 %collective-permute-start.20 = (f32[48,640]{1,0:T(8,128)S(1)}, f32[48,640]{1,0:T(8,128)S(1)}, u32[]{:S(2)}, u32[]{:S(2)}) collective-permute-start(f32[48,640]{1,0:T(8,128)S(1)} %shard_map.57), channel_id=1, source_target_pairs={{0,16},{4,20},{8,24},{12,28},{16,0},{20,4},{24,8},{28,12},{1,17},{... | collective-permute-start | bytes 368648 | tf_op jit(solution)/shard_map/ppermute | solution.py:237
  37.8 2.5 %collective-permute-start.9 = (f32[40,640]{1,0:T(8,128)S(1)}, f32[40,640]{1,0:T(8,128)S(1)}, u32[]{:S(2)}, u32[]{:S(2)}) collective-permute-start(f32[40,640]{1,0:T(8,128)S(1)} %shard_map.50), channel_id=1, source_target_pairs={{0,8},{4,12},{8,0},{12,4},{16,24},{20,28},{24,16},{28,20},{1,9},{5... | collective-permute-start | bytes 307208 | tf_op jit(solution)/shard_map/ppermute | solution.py:237
  40.5 2.0 %collective-permute-start.21 = (f32[40,640]{1,0:T(8,128)S(1)}, f32[40,640]{1,0:T(8,128)S(1)}, u32[]{:S(2)}, u32[]{:S(2)}) collective-permute-start(f32[40,640]{1,0:T(8,128)S(1)} %shard_map.56.send_ref), channel_id=1, source_target_pairs={{0,16},{4,20},{8,24},{12,28},{16,0},{20,4},{24,8},{28,12},{1,17},{... | collective-permute-start | bytes 307208 | tf_op jit(solution)/shard_map/ppermute | solution.py:237
  42.5 5.8 %collective-permute-done.9.refs_1_ = f32[40,640]{1,0:T(8,128)S(1)} collective-permute-done((f32[40,640]{1,0:T(8,128)S(1)}, f32[40,640]{1,0:T(8,128)S(1)}, u32[]{:S(2)}, u32[]{:S(2)}) %collective-permute-start.9) | collective-permute-done | bytes 102432 | tf_op jit(solution)/shard_map/ppermute | solution.py:237
  48.2 1.1 %collective-permute-done.12.refs_2_ = f32[40,640]{1,0:T(8,128)S(1)} collective-permute-done((f32[40,640]{1,0:T(8,128)S(1)}, f32[40,640]{1,0:T(8,128)S(1)}, u32[]{:S(2)}, u32[]{:S(2)}) %collective-permute-start.12) | collective-permute-done | bytes 102432 | tf_op jit(solution)/shard_map/ppermute | solution.py:237
  49.4 0.2 shard_map.59.refs_2_
  49.7 0.9 %shard_map.60 = f32[3,80,640]{2,1,0:T(8,128)} custom-call(f32[80,640]{1,0:T(8,128)S(1)} %shard_map.52.keep_ref, f32[40,640]{1,0:T(8,128)S(1)} %shard_map.56.send_ref, f32[48,640]{1,0:T(8,128)S(1)} %collective-permute-done.20.refs_0_, f32[40,640]{1,0:T(8,128)S(1)} %collective-permute-done.21.refs_1_, f32[80,640]{1,0:T(8,128)S(1)} %shard_map.59.refs_2_), custom_call_target="tpu_custom_call" | custom-call | tf_op jit(solution)/shard_map/pallas_call | solution.py:377
  (27 shorter events, 0.6 us)
Async XLA Ops:
  2.0 9.1 %collective-permute-start.3 = (bf16[88,896]{1,0:T(8,128)(2,1)S(1)}, bf16[88,896]{1,0:T(8,128)(2,1)S(1)}, u32[]{:S(2)}, u32[]{:S(2)}) collective-permute-start(bf16[88,896]{1,0:T(8,128)(2,1)S(1)} %get-tuple-element.35), channel_id=1, source_target_pairs={{0,3},{1,2},{2,1},{3,0},{4,7},{5,6},{6,5},{7,4},{8,11},{9,10},{10,... | collective-permute-start | bytes 473096 | tf_op jit(solution)/shard_map/ppermute | solution.py:231
  5.9 7.9 %collective-permute-start.4 = (bf16[88,896]{1,0:T(8,128)(2,1)S(1)}, bf16[88,896]{1,0:T(8,128)(2,1)S(1)}, u32[]{:S(2)}, u32[]{:S(2)}) collective-permute-start(bf16[88,896]{1,0:T(8,128)(2,1)S(1)} %get-tuple-element.36), channel_id=1, source_target_pairs={{0,2},{1,3},{2,0},{3,1},{4,6},{5,7},{6,4},{7,5},{8,10},{9,11},{10,... | collective-permute-start | bytes 473096 | tf_op jit(solution)/shard_map/ppermute | solution.py:231
  6.4 8.4 %collective-permute-start.5 = (bf16[88,896]{1,0:T(8,128)(2,1)S(1)}, bf16[88,896]{1,0:T(8,128)(2,1)S(1)}, u32[]{:S(2)}, u32[]{:S(2)}) collective-permute-start(bf16[88,896]{1,0:T(8,128)(2,1)S(1)} %get-tuple-element.37), channel_id=1, source_target_pairs={{0,1},{1,0},{2,3},{3,2},{4,5},{5,4},{6,7},{7,6},{8,9},{9,8},{10,11... | collective-permute-start | bytes 473096 | tf_op jit(solution)/shard_map/ppermute | solution.py:231
  7.6 11.7 %collective-permute-start = (bf16[88,1280]{1,0:T(8,128)(2,1)S(1)}, bf16[88,1280]{1,0:T(8,128)(2,1)S(1)}, u32[]{:S(2)}, u32[]{:S(2)}) collective-permute-start(bf16[88,1280]{1,0:T(8,128)(2,1)S(1)} %get-tuple-element.31), channel_id=1, source_target_pairs={{0,2},{1,3},{2,0},{3,1},{4,6},{5,7},{6,4},{7,5},{8,10},{9,11},{10,... | collective-permute-start | bytes 675848 | tf_op jit(solution)/shard_map/ppermute | solution.py:231
  9.6 10.1 %collective-permute-start.1 = (bf16[88,1280]{1,0:T(8,128)(2,1)S(1)}, bf16[88,1280]{1,0:T(8,128)(2,1)S(1)}, u32[]{:S(2)}, u32[]{:S(2)}) collective-permute-start(bf16[88,1280]{1,0:T(8,128)(2,1)S(1)} %get-tuple-element.32), channel_id=1, source_target_pairs={{0,1},{1,0},{2,3},{3,2},{4,5},{5,4},{6,7},{7,6},{8,9},{9,8},{10,11... | collective-permute-start | bytes 675848 | tf_op jit(solution)/shard_map/ppermute | solution.py:231
  11.1 12.0 %collective-permute-start.2 = (bf16[88,1280]{1,0:T(8,128)(2,1)S(1)}, bf16[88,1280]{1,0:T(8,128)(2,1)S(1)}, u32[]{:S(2)}, u32[]{:S(2)}) collective-permute-start(bf16[88,1280]{1,0:T(8,128)(2,1)S(1)} %get-tuple-element.33), channel_id=1, source_target_pairs={{0,3},{1,2},{2,1},{3,0},{4,7},{5,6},{6,5},{7,4},{8,11},{9,10},{10,... | collective-permute-start | bytes 675848 | tf_op jit(solution)/shard_map/ppermute | solution.py:231
  15.4 2.0 %collective-permute-start.6 = (f32[88,512]{1,0:T(8,128)S(1)}, f32[88,512]{1,0:T(8,128)S(1)}, u32[]{:S(2)}, u32[]{:S(2)}) collective-permute-start(f32[88,512]{1,0:T(8,128)S(1)} %get-tuple-element.38), channel_id=1, source_target_pairs={{0,4},{4,0},{8,12},{12,8},{16,20},{20,16},{24,28},{28,24},{1,5},{5... | collective-permute-start | bytes 540680 | tf_op jit(solution)/shard_map/ppermute | solution.py:237
  15.5 1.6 %collective-permute-start.17 = (f32[80,512]{1,0:T(8,128)S(1)}, f32[80,512]{1,0:T(8,128)S(1)}, u32[]{:S(2)}, u32[]{:S(2)}) collective-permute-start(f32[80,512]{1,0:T(8,128)S(1)} %get-tuple-element.48), channel_id=1, source_target_pairs={{0,4},{4,0},{8,12},{12,8},{16,20},{20,16},{24,28},{28,24},{1,5},{5... | collective-permute-start | bytes 491528 | tf_op jit(solution)/shard_map/ppermute | solution.py:237
  17.1 10.3 %collective-permute-start.16 = (f32[168,512]{1,0:T(8,128)S(1)}, f32[168,512]{1,0:T(8,128)S(1)}, u32[]{:S(2)}, u32[]{:S(2)}) collective-permute-start(f32[168,512]{1,0:T(8,128)S(1)} %get-tuple-element.47), channel_id=1, source_target_pairs={{0,4},{4,0},{8,12},{12,8},{16,20},{20,16},{24,28},{28,24},{1,5},{5... | collective-permute-start | bytes 1032200 | tf_op jit(solution)/shard_map/ppermute | solution.py:237
  17.4 10.3 %collective-permute-start.18 = (f32[168,512]{1,0:T(8,128)S(1)}, f32[168,512]{1,0:T(8,128)S(1)}, u32[]{:S(2)}, u32[]{:S(2)}) collective-permute-start(f32[168,512]{1,0:T(8,128)S(1)} %shard_map.54), channel_id=1, source_target_pairs={{0,8},{4,12},{8,0},{12,4},{16,24},{20,28},{24,16},{28,20},{1,9},{5... | collective-permute-start | bytes 1032200 | tf_op jit(solution)/shard_map/ppermute | solution.py:237
  23.8 1.7 %collective-permute-start.8 = (f32[96,640]{1,0:T(8,128)S(1)}, f32[96,640]{1,0:T(8,128)S(1)}, u32[]{:S(2)}, u32[]{:S(2)}) collective-permute-start(f32[96,640]{1,0:T(8,128)S(1)} %get-tuple-element.41), channel_id=1, source_target_pairs={{0,4},{4,0},{8,12},{12,8},{16,20},{20,16},{24,28},{28,24},{1,5},{5... | collective-permute-start | bytes 737288 | tf_op jit(solution)/shard_map/ppermute | solution.py:237
  23.9 1.6 %collective-permute-start.14 = (f32[40,640]{1,0:T(8,128)S(1)}, f32[40,640]{1,0:T(8,128)S(1)}, u32[]{:S(2)}, u32[]{:S(2)}) collective-permute-start(f32[40,640]{1,0:T(8,128)S(1)} %get-tuple-element.45), channel_id=1, source_target_pairs={{0,4},{4,0},{8,12},{12,8},{16,20},{20,16},{24,28},{28,24},{1,5},{5... | collective-permute-start | bytes 307208 | tf_op jit(solution)/shard_map/ppermute | solution.py:237
  24.4 6.5 %collective-permute-start.13 = (f32[88,640]{1,0:T(8,128)S(1)}, f32[88,640]{1,0:T(8,128)S(1)}, u32[]{:S(2)}, u32[]{:S(2)}) collective-permute-start(f32[88,640]{1,0:T(8,128)S(1)} %get-tuple-element.44), channel_id=1, source_target_pairs={{0,4},{4,0},{8,12},{12,8},{16,20},{20,16},{24,28},{28,24},{1,5},{5... | collective-permute-start | bytes 675848 | tf_op jit(solution)/shard_map/ppermute | solution.py:237
  25.6 11.5 %collective-permute-start.15 = (f32[88,640]{1,0:T(8,128)S(1)}, f32[88,640]{1,0:T(8,128)S(1)}, u32[]{:S(2)}, u32[]{:S(2)}) collective-permute-start(f32[88,640]{1,0:T(8,128)S(1)} %shard_map.53), channel_id=1, source_target_pairs={{0,8},{4,12},{8,0},{12,4},{16,24},{20,28},{24,16},{28,20},{1,9},{5... | collective-permute-start | bytes 675848 | tf_op jit(solution)/shard_map/ppermute | solution.py:237
  27.7 12.7 %collective-permute-start.19 = (f32[88,512]{1,0:T(8,128)S(1)}, f32[88,512]{1,0:T(8,128)S(1)}, u32[]{:S(2)}, u32[]{:S(2)}) collective-permute-start(f32[88,512]{1,0:T(8,128)S(1)} %shard_map.55.send_ref), channel_id=1, source_target_pairs={{0,16},{4,20},{8,24},{12,28},{16,0},{20,4},{24,8},{28,12},{1,17},{... | collective-permute-start | bytes 540680 | tf_op jit(solution)/shard_map/ppermute | solution.py:237
  30.4 12.1 %collective-permute-start.7 = (f32[80,640]{1,0:T(8,128)S(1)}, f32[80,640]{1,0:T(8,128)S(1)}, u32[]{:S(2)}, u32[]{:S(2)}) collective-permute-start(f32[80,640]{1,0:T(8,128)S(1)} %get-tuple-element.40), channel_id=1, source_target_pairs={{0,4},{4,0},{8,12},{12,8},{16,20},{20,16},{24,28},{28,24},{1,5},{5... | collective-permute-start | bytes 614408 | tf_op jit(solution)/shard_map/ppermute | solution.py:237
  30.4 10.0 %collective-permute-start.11 = (f32[24,640]{1,0:T(8,128)S(1)}, f32[24,640]{1,0:T(8,128)S(1)}, u32[]{:S(2)}, u32[]{:S(2)}) collective-permute-start(f32[24,640]{1,0:T(8,128)S(1)} %get-tuple-element.43), channel_id=1, source_target_pairs={{0,4},{4,0},{8,12},{12,8},{16,20},{20,16},{24,28},{28,24},{1,5},{5... | collective-permute-start | bytes 184328 | tf_op jit(solution)/shard_map/ppermute | solution.py:237
  30.9 6.9 %collective-permute-start.10 = (f32[8,640]{1,0:T(8,128)S(1)}, f32[8,640]{1,0:T(8,128)S(1)}, u32[]{:S(2)}, u32[]{:S(2)}) collective-permute-start(f32[8,640]{1,0:T(8,128)S(1)} %get-tuple-element.42), channel_id=1, source_target_pairs={{0,4},{4,0},{8,12},{12,8},{16,20},{20,16},{24,28},{28,24},{1,5},{5... | collective-permute-start | bytes 61448 | tf_op jit(solution)/shard_map/ppermute | solution.py:237
  37.2 12.5 %collective-permute-start.20 = (f32[48,640]{1,0:T(8,128)S(1)}, f32[48,640]{1,0:T(8,128)S(1)}, u32[]{:S(2)}, u32[]{:S(2)}) collective-permute-start(f32[48,640]{1,0:T(8,128)S(1)} %shard_map.57), channel_id=1, source_target_pairs={{0,16},{4,20},{8,24},{12,28},{16,0},{20,4},{24,8},{28,12},{1,17},{... | collective-permute-start | bytes 368648 | tf_op jit(solution)/shard_map/ppermute | solution.py:237
  37.8 10.4 %collective-permute-start.9 = (f32[40,640]{1,0:T(8,128)S(1)}, f32[40,640]{1,0:T(8,128)S(1)}, u32[]{:S(2)}, u32[]{:S(2)}) collective-permute-start(f32[40,640]{1,0:T(8,128)S(1)} %shard_map.50), channel_id=1, source_target_pairs={{0,8},{4,12},{8,0},{12,4},{16,24},{20,28},{24,16},{28,20},{1,9},{5... | collective-permute-start | bytes 307208 | tf_op jit(solution)/shard_map/ppermute | solution.py:237
  40.4 9.0 %collective-permute-start.12 = (f32[40,640]{1,0:T(8,128)S(1)}, f32[40,640]{1,0:T(8,128)S(1)}, u32[]{:S(2)}, u32[]{:S(2)}) collective-permute-start(f32[40,640]{1,0:T(8,128)S(1)} %shard_map.51), channel_id=1, source_target_pairs={{0,8},{4,12},{8,0},{12,4},{16,24},{20,28},{24,16},{28,20},{1,9},{5... | collective-permute-start | bytes 307208 | tf_op jit(solution)/shard_map/ppermute | solution.py:237
  40.5 9.2 %collective-permute-start.21 = (f32[40,640]{1,0:T(8,128)S(1)}, f32[40,640]{1,0:T(8,128)S(1)}, u32[]{:S(2)}, u32[]{:S(2)}) collective-permute-start(f32[40,640]{1,0:T(8,128)S(1)} %shard_map.56.send_ref), channel_id=1, source_target_pairs={{0,16},{4,20},{8,24},{12,28},{16,0},{20,4},{24,8},{28,12},{1,17},{... | collective-permute-start | bytes 307208 | tf_op jit(solution)/shard_map/ppermute | solution.py:237

commit v7 on v6

--- a/solution.py
+++ b/solution.py
@@ -109,12 +109,11 @@
 def first_place_kernel(place, sizes, order_hbm, tile_hbm, bg_hbm, an_hbm, *refs):
     n_bin = sizes[0]
     out_refs, (keys_ref, bg_ref, an_ref, order_ref, tile_ref, sem) = refs[:n_bin], refs[n_bin:]
-    copies = [
-        pltpu.make_async_copy(source, target, sem.at[i])
-        for i, (source, target) in enumerate(
-            ((order_hbm, order_ref), (tile_hbm, tile_ref), (bg_hbm, bg_ref), (an_hbm, an_ref))
-        )
-    ]
+    pairs = [(order_hbm, order_ref), (tile_hbm, tile_ref)]
+    for low, high in ((0, MID), (MID, WIDE)):
+        lanes = pl.ds(low, high - low)
+        pairs += [(bg_hbm.at[:, lanes], bg_ref.at[:, lanes]), (an_hbm.at[:, lanes], an_ref.at[:, lanes])]
+    copies = [pltpu.make_async_copy(*pair, sem.at[i]) for i, pair in enumerate(pairs)]
     for copy in copies:
         copy.start()
     copies[0].wait()
@@ -123,7 +122,9 @@
     keys_ref[...] = keys
     for part, ref in enumerate((bg_ref, an_ref)):
         copies[2 + part].wait()
-        place(keys, out_refs, part, ref[...], *sizes)
+        place(keys, out_refs, part, ref[:, :MID], *sizes)
+    copies[4].wait()
+    copies[5].wait()
 
 
 def second_place_kernel(place, sizes, keys_ref, bg_ref, an_ref, *out_refs):
@@ -274,7 +275,7 @@
         scratch_shapes=[
             pltpu.SMEM((tiles,), jnp.int32),
             pltpu.VMEM((1, rows), jnp.int32),
-            pltpu.SemaphoreType.DMA((4,)),
+            pltpu.SemaphoreType.DMA((6,)),
         ],
         compiler_params=PARAMS,
     )(*(pltpu.with_memory_space_constraint(x, pltpu.HBM) for x in (owner_order, tile, obs_minus_bg, obs_minus_an)))

time: 50.7 us -> 50.7 us (level)
  no operation moved by 1% of the time
where the time goes in v7:
time: 50.7 us; the launch traced here: 50.6 us
  starting transfers between devices  24.1 us (48%)
  waiting for transfers between devices  20.6 us (41%)
  Pallas kernels  5.66 us (11%)
    ppermute x16, waiting for transfers between devices, swap(): return lax.ppermute(value, 'cycle', [(i, i ^ bit) for i in range(n)])  15.6 us
    ppermute x16, starting transfers between devices, swap(): return lax.ppermute(value, 'cycle', [(i, i ^ bit) for i in range(n)])  13.3 us
    ppermute x6, starting transfers between devices, to_owners(): lax.ppermute(parts[k], 'bin', [(i, i ^ k) for i in range(n_bin)])  10.8 us
    ppermute x6, waiting for transfers between devices, to_owners(): lax.ppermute(parts[k], 'bin', [(i, i ^ k) for i in range(n_bin)])  5.03 us
    pallas_call x1, Pallas kernels, on_device(): pl.pallas_call(functools.partial(first_place_kernel, places[lanes['F']],...  1.94 us
    pallas_call x2, Pallas kernels, make(): pl.pallas_call(functools.partial(moment_kernel, lanes[p], rows_c, n_cycle...  1.34 us
  transfers between devices with their start and end apart: 22, of which 10 were waited for; matrix products, arithmetic and copies ran while one was open for 0% of the time, Pallas kernels for 6%

profile of v7, /device:TPU:0, one launch (start us, length us, event | category | flops | bytes accessed | tf_op | source)
XLA Modules:
  0.0 50.6 jit_solution(17041164017388341647)
XLA Ops:
  0.0 1.9 %shard_map.46 = (bf16[88,896]{1,0:T(8,128)(2,1)S(1)}, bf16[88,896]{1,0:T(8,128)(2,1)S(1)}, bf16[88,896]{1,0:T(8,128)(2,1)S(1)}, bf16[88,896]{1,0:T(8,128)(2,1)S(...) custom-call(s32[12]{0:T(128)} %order_hbm.1, s32[1,512]{1,0:T(1,128)} %bitcast.1, ...), custom_call_target="tpu_custom_call" | custom-call | tf_op jit(solution)/shard_map/pallas_call | solution.py:268
  2.0 4.0 %collective-permute-start.3 = (bf16[88,896]{1,0:T(8,128)(2,1)S(1)}, bf16[88,896]{1,0:T(8,128)(2,1)S(1)}, u32[]{:S(2)}, u32[]{:S(2)}) collective-permute-start(bf16[88,896]{1,0:T(8,128)(2,1)S(1)} %get-tuple-element.35), channel_id=1, source_target_pairs={{0,3},{1,2},{2,1},{3,0},{4,7},{5,6},{6,5},{7,4},{8,11},{9,10},{10,... | collective-permute-start | bytes 473096 | tf_op jit(solution)/shard_map/ppermute | solution.py:232
  5.9 0.5 %collective-permute-start.4 = (bf16[88,896]{1,0:T(8,128)(2,1)S(1)}, bf16[88,896]{1,0:T(8,128)(2,1)S(1)}, u32[]{:S(2)}, u32[]{:S(2)}) collective-permute-start(bf16[88,896]{1,0:T(8,128)(2,1)S(1)} %get-tuple-element.36), channel_id=1, source_target_pairs={{0,2},{1,3},{2,0},{3,1},{4,6},{5,7},{6,4},{7,5},{8,10},{9,11},{10,... | collective-permute-start | bytes 473096 | tf_op jit(solution)/shard_map/ppermute | solution.py:232
  6.4 0.1 collective-permute-start.5
  6.6 1.0 %shard_map.47 = (bf16[88,1280]{1,0:T(8,128)(2,1)S(1)}, bf16[88,1280]{1,0:T(8,128)(2,1)S(1)}, bf16[88,1280]{1,0:T(8,128)(2,1)S(1)}, bf16[88,1280]{1,0:T(8,128)(2,1)S(1)}) custom-call(s32[16,512]{1,0:T(8,128)S(1)} %get-tuple-element.27.keys_ref, bf16[512,640]{1,0:T(8,128)(2,1)S(1)} %get-tuple-element.28.bg_ref, bf16[512,640]{1,0:T(8,128)(2,1)S(1)} %get-tuple-element.29.an_ref), custom_call_target="tpu_custom_call" | custom-call | tf_op jit(solution)/shard_map/pallas_call | solution.py:282
  7.6 2.0 %collective-permute-start = (bf16[88,1280]{1,0:T(8,128)(2,1)S(1)}, bf16[88,1280]{1,0:T(8,128)(2,1)S(1)}, u32[]{:S(2)}, u32[]{:S(2)}) collective-permute-start(bf16[88,1280]{1,0:T(8,128)(2,1)S(1)} %get-tuple-element.31), channel_id=1, source_target_pairs={{0,2},{1,3},{2,0},{3,1},{4,6},{5,7},{6,4},{7,5},{8,10},{9,11},{10,... | collective-permute-start | bytes 675848 | tf_op jit(solution)/shard_map/ppermute | solution.py:232
  9.5 1.5 %collective-permute-start.1 = (bf16[88,1280]{1,0:T(8,128)(2,1)S(1)}, bf16[88,1280]{1,0:T(8,128)(2,1)S(1)}, u32[]{:S(2)}, u32[]{:S(2)}) collective-permute-start(bf16[88,1280]{1,0:T(8,128)(2,1)S(1)} %get-tuple-element.32), channel_id=1, source_target_pairs={{0,1},{1,0},{2,3},{3,2},{4,5},{5,4},{6,7},{7,6},{8,9},{9,8},{10,11... | collective-permute-start | bytes 675848 | tf_op jit(solution)/shard_map/ppermute | solution.py:232
  11.0 2.7 %collective-permute-start.2 = (bf16[88,1280]{1,0:T(8,128)(2,1)S(1)}, bf16[88,1280]{1,0:T(8,128)(2,1)S(1)}, u32[]{:S(2)}, u32[]{:S(2)}) collective-permute-start(bf16[88,1280]{1,0:T(8,128)(2,1)S(1)} %get-tuple-element.33), channel_id=1, source_target_pairs={{0,3},{1,2},{2,1},{3,0},{4,7},{5,6},{6,5},{7,4},{8,11},{9,10},{10,... | collective-permute-start | bytes 675848 | tf_op jit(solution)/shard_map/ppermute | solution.py:232
  13.8 1.0 %collective-permute-done.5.refs_3_ = bf16[88,896]{1,0:T(8,128)(2,1)S(1)} collective-permute-done((bf16[88,896]{1,0:T(8,128)(2,1)S(1)}, bf16[88,896]{1,0:T(8,128)(2,1)S(1)}, u32[]{:S(2)}, u32[]{:S(2)}) %collective-permute-start.5) | collective-permute-done | bytes 157728 | tf_op jit(solution)/shard_map/ppermute | solution.py:232
  14.8 0.5 %shard_map.48 = (f32[88,512]{1,0:T(8,128)S(1)}, f32[80,512]{1,0:T(8,128)S(1)}, f32[168,512]{1,0:T(8,128)S(1)}, f32[336,512]{1,0:T(8,128)S(1)}) custom-call(bf16[88,896]{1,0:T(8,128)(2,1)S(1)} %get-tuple-element.34.refs_0_, bf16[88,896]{1,0:T(8,128)(2,1)S(1)} %collective-permute-done.3.refs_1_, bf16[88,896]{1,0:T(8,128)(2,1)S(1)} %collective-permute-done.4.refs_2_, ...), custom_call_target="tpu_custom_call" | custom-call | tf_op jit(solution)/shard_map/pallas_call | solution.py:335
  15.4 0.5 collective-permute-start.17
  15.9 1.1 %collective-permute-done.17.refs_1_ = f32[80,512]{1,0:T(8,128)S(1)} collective-permute-done((f32[80,512]{1,0:T(8,128)S(1)}, f32[80,512]{1,0:T(8,128)S(1)}, u32[]{:S(2)}, u32[]{:S(2)}) %collective-permute-start.17) | collective-permute-done | bytes 163872 | tf_op jit(solution)/shard_map/ppermute | solution.py:238
  17.1 0.3 collective-permute-start.16
  17.4 1.6 %collective-permute-start.18 = (f32[168,512]{1,0:T(8,128)S(1)}, f32[168,512]{1,0:T(8,128)S(1)}, u32[]{:S(2)}, u32[]{:S(2)}) collective-permute-start(f32[168,512]{1,0:T(8,128)S(1)} %shard_map.54), channel_id=1, source_target_pairs={{0,8},{4,12},{8,0},{12,4},{16,24},{20,28},{24,16},{28,20},{1,9},{5... | collective-permute-start | bytes 1032200 | tf_op jit(solution)/shard_map/ppermute | solution.py:238
  19.0 0.2 collective-permute-done.refs_1_
  19.2 0.4 collective-permute-done.1.refs_2_
  19.6 3.4 %collective-permute-done.2.refs_3_ = bf16[88,1280]{1,0:T(8,128)(2,1)S(1)} collective-permute-done((bf16[88,1280]{1,0:T(8,128)(2,1)S(1)}, bf16[88,1280]{1,0:T(8,128)(2,1)S(1)}, u32[]{:S(2)}, u32[]{:S(2)}) %collective-permute-start.2) | collective-permute-done | bytes 225312 | tf_op jit(solution)/shard_map/ppermute | solution.py:232
  23.0 0.8 %shard_map.49 = (f32[40,640]{1,0:T(8,128)S(1)}, f32[96,640]{1,0:T(8,128)S(1)}, f32[8,640]{1,0:T(8,128)S(1)}, f32[24,640]{1,0:T(8,128)S(1)}, f32[88,640]{1,0:T(8,...) custom-call(bf16[88,1280]{1,0:T(8,128)(2,1)S(1)} %get-tuple-element.30.refs_0_, ...), custom_call_target="tpu_custom_call" | custom-call | tf_op jit(solution)/shard_map/pallas_call | solution.py:335
  23.9 0.5 collective-permute-start.14
  24.5 1.1 %collective-permute-done.14.refs_0_ = f32[40,640]{1,0:T(8,128)S(1)} collective-permute-done((f32[40,640]{1,0:T(8,128)S(1)}, f32[40,640]{1,0:T(8,128)S(1)}, u32[]{:S(2)}, u32[]{:S(2)}) %collective-permute-start.14) | collective-permute-done | bytes 102432 | tf_op jit(solution)/shard_map/ppermute | solution.py:238
  25.6 1.8 %collective-permute-start.15 = (f32[88,640]{1,0:T(8,128)S(1)}, f32[88,640]{1,0:T(8,128)S(1)}, u32[]{:S(2)}, u32[]{:S(2)}) collective-permute-start(f32[88,640]{1,0:T(8,128)S(1)} %shard_map.53), channel_id=1, source_target_pairs={{0,8},{4,12},{8,0},{12,4},{16,24},{20,28},{24,16},{28,20},{1,9},{5... | collective-permute-start | bytes 675848 | tf_op jit(solution)/shard_map/ppermute | solution.py:238
  27.4 0.2 collective-permute-done.18.refs_1_
  27.7 2.7 %collective-permute-start.19 = (f32[88,512]{1,0:T(8,128)S(1)}, f32[88,512]{1,0:T(8,128)S(1)}, u32[]{:S(2)}, u32[]{:S(2)}) collective-permute-start(f32[88,512]{1,0:T(8,128)S(1)} %shard_map.55.send_ref), channel_id=1, source_target_pairs={{0,16},{4,20},{8,24},{12,28},{16,0},{20,4},{24,8},{28,12},{1,17},{... | collective-permute-start | bytes 540680 | tf_op jit(solution)/shard_map/ppermute | solution.py:238
  30.3 0.5 %collective-permute-start.11 = (f32[24,640]{1,0:T(8,128)S(1)}, f32[24,640]{1,0:T(8,128)S(1)}, u32[]{:S(2)}, u32[]{:S(2)}) collective-permute-start(f32[24,640]{1,0:T(8,128)S(1)} %get-tuple-element.43), channel_id=1, source_target_pairs={{0,4},{4,0},{8,12},{12,8},{16,20},{20,16},{24,28},{28,24},{1,5},{5... | collective-permute-start | bytes 184328 | tf_op jit(solution)/shard_map/ppermute | solution.py:238
  30.9 6.3 %collective-permute-done.15.refs_1_ = f32[88,640]{1,0:T(8,128)S(1)} collective-permute-done((f32[88,640]{1,0:T(8,128)S(1)}, f32[88,640]{1,0:T(8,128)S(1)}, u32[]{:S(2)}, u32[]{:S(2)}) %collective-permute-start.15) | collective-permute-done | bytes 225312 | tf_op jit(solution)/shard_map/ppermute | solution.py:238
  37.1 0.6 %collective-permute-start.20 = (f32[48,640]{1,0:T(8,128)S(1)}, f32[48,640]{1,0:T(8,128)S(1)}, u32[]{:S(2)}, u32[]{:S(2)}) collective-permute-start(f32[48,640]{1,0:T(8,128)S(1)} %shard_map.57), channel_id=1, source_target_pairs={{0,16},{4,20},{8,24},{12,28},{16,0},{20,4},{24,8},{28,12},{1,17},{... | collective-permute-start | bytes 368648 | tf_op jit(solution)/shard_map/ppermute | solution.py:238
  37.8 2.5 %collective-permute-start.9 = (f32[40,640]{1,0:T(8,128)S(1)}, f32[40,640]{1,0:T(8,128)S(1)}, u32[]{:S(2)}, u32[]{:S(2)}) collective-permute-start(f32[40,640]{1,0:T(8,128)S(1)} %shard_map.50), channel_id=1, source_target_pairs={{0,8},{4,12},{8,0},{12,4},{16,24},{20,28},{24,16},{28,20},{1,9},{5... | collective-permute-start | bytes 307208 | tf_op jit(solution)/shard_map/ppermute | solution.py:238
  40.5 2.0 %collective-permute-start.21 = (f32[40,640]{1,0:T(8,128)S(1)}, f32[40,640]{1,0:T(8,128)S(1)}, u32[]{:S(2)}, u32[]{:S(2)}) collective-permute-start(f32[40,640]{1,0:T(8,128)S(1)} %shard_map.56.send_ref), channel_id=1, source_target_pairs={{0,16},{4,20},{8,24},{12,28},{16,0},{20,4},{24,8},{28,12},{1,17},{... | collective-permute-start | bytes 307208 | tf_op jit(solution)/shard_map/ppermute | solution.py:238
  42.4 5.8 %collective-permute-done.9.refs_1_ = f32[40,640]{1,0:T(8,128)S(1)} collective-permute-done((f32[40,640]{1,0:T(8,128)S(1)}, f32[40,640]{1,0:T(8,128)S(1)}, u32[]{:S(2)}, u32[]{:S(2)}) %collective-permute-start.9) | collective-permute-done | bytes 102432 | tf_op jit(solution)/shard_map/ppermute | solution.py:238
  48.2 1.1 %collective-permute-done.12.refs_2_ = f32[40,640]{1,0:T(8,128)S(1)} collective-permute-done((f32[40,640]{1,0:T(8,128)S(1)}, f32[40,640]{1,0:T(8,128)S(1)}, u32[]{:S(2)}, u32[]{:S(2)}) %collective-permute-start.12) | collective-permute-done | bytes 102432 | tf_op jit(solution)/shard_map/ppermute | solution.py:238
  49.4 0.2 shard_map.59.refs_2_
  49.6 0.9 %shard_map.60 = f32[3,80,640]{2,1,0:T(8,128)} custom-call(f32[80,640]{1,0:T(8,128)S(1)} %shard_map.52.keep_ref, f32[40,640]{1,0:T(8,128)S(1)} %shard_map.56.send_ref, f32[48,640]{1,0:T(8,128)S(1)} %collective-permute-done.20.refs_0_, f32[40,640]{1,0:T(8,128)S(1)} %collective-permute-done.21.refs_1_, f32[80,640]{1,0:T(8,128)S(1)} %shard_map.59.refs_2_), custom_call_target="tpu_custom_call" | custom-call | tf_op jit(solution)/shard_map/pallas_call | solution.py:378
  (27 shorter events, 0.6 us)
Async XLA Ops:
  2.0 9.1 %collective-permute-start.3 = (bf16[88,896]{1,0:T(8,128)(2,1)S(1)}, bf16[88,896]{1,0:T(8,128)(2,1)S(1)}, u32[]{:S(2)}, u32[]{:S(2)}) collective-permute-start(bf16[88,896]{1,0:T(8,128)(2,1)S(1)} %get-tuple-element.35), channel_id=1, source_target_pairs={{0,3},{1,2},{2,1},{3,0},{4,7},{5,6},{6,5},{7,4},{8,11},{9,10},{10,... | collective-permute-start | bytes 473096 | tf_op jit(solution)/shard_map/ppermute | solution.py:232
  5.9 7.9 %collective-permute-start.4 = (bf16[88,896]{1,0:T(8,128)(2,1)S(1)}, bf16[88,896]{1,0:T(8,128)(2,1)S(1)}, u32[]{:S(2)}, u32[]{:S(2)}) collective-permute-start(bf16[88,896]{1,0:T(8,128)(2,1)S(1)} %get-tuple-element.36), channel_id=1, source_target_pairs={{0,2},{1,3},{2,0},{3,1},{4,6},{5,7},{6,4},{7,5},{8,10},{9,11},{10,... | collective-permute-start | bytes 473096 | tf_op jit(solution)/shard_map/ppermute | solution.py:232
  6.4 8.4 %collective-permute-start.5 = (bf16[88,896]{1,0:T(8,128)(2,1)S(1)}, bf16[88,896]{1,0:T(8,128)(2,1)S(1)}, u32[]{:S(2)}, u32[]{:S(2)}) collective-permute-start(bf16[88,896]{1,0:T(8,128)(2,1)S(1)} %get-tuple-element.37), channel_id=1, source_target_pairs={{0,1},{1,0},{2,3},{3,2},{4,5},{5,4},{6,7},{7,6},{8,9},{9,8},{10,11... | collective-permute-start | bytes 473096 | tf_op jit(solution)/shard_map/ppermute | solution.py:232
  7.6 11.7 %collective-permute-start = (bf16[88,1280]{1,0:T(8,128)(2,1)S(1)}, bf16[88,1280]{1,0:T(8,128)(2,1)S(1)}, u32[]{:S(2)}, u32[]{:S(2)}) collective-permute-start(bf16[88,1280]{1,0:T(8,128)(2,1)S(1)} %get-tuple-element.31), channel_id=1, source_target_pairs={{0,2},{1,3},{2,0},{3,1},{4,6},{5,7},{6,4},{7,5},{8,10},{9,11},{10,... | collective-permute-start | bytes 675848 | tf_op jit(solution)/shard_map/ppermute | solution.py:232
  9.5 10.1 %collective-permute-start.1 = (bf16[88,1280]{1,0:T(8,128)(2,1)S(1)}, bf16[88,1280]{1,0:T(8,128)(2,1)S(1)}, u32[]{:S(2)}, u32[]{:S(2)}) collective-permute-start(bf16[88,1280]{1,0:T(8,128)(2,1)S(1)} %get-tuple-element.32), channel_id=1, source_target_pairs={{0,1},{1,0},{2,3},{3,2},{4,5},{5,4},{6,7},{7,6},{8,9},{9,8},{10,11... | collective-permute-start | bytes 675848 | tf_op jit(solution)/shard_map/ppermute | solution.py:232
  11.0 12.0 %collective-permute-start.2 = (bf16[88,1280]{1,0:T(8,128)(2,1)S(1)}, bf16[88,1280]{1,0:T(8,128)(2,1)S(1)}, u32[]{:S(2)}, u32[]{:S(2)}) collective-permute-start(bf16[88,1280]{1,0:T(8,128)(2,1)S(1)} %get-tuple-element.33), channel_id=1, source_target_pairs={{0,3},{1,2},{2,1},{3,0},{4,7},{5,6},{6,5},{7,4},{8,11},{9,10},{10,... | collective-permute-start | bytes 675848 | tf_op jit(solution)/shard_map/ppermute | solution.py:232
  15.4 2.0 %collective-permute-start.6 = (f32[88,512]{1,0:T(8,128)S(1)}, f32[88,512]{1,0:T(8,128)S(1)}, u32[]{:S(2)}, u32[]{:S(2)}) collective-permute-start(f32[88,512]{1,0:T(8,128)S(1)} %get-tuple-element.38), channel_id=1, source_target_pairs={{0,4},{4,0},{8,12},{12,8},{16,20},{20,16},{24,28},{28,24},{1,5},{5... | collective-permute-start | bytes 540680 | tf_op jit(solution)/shard_map/ppermute | solution.py:238
  15.4 1.6 %collective-permute-start.17 = (f32[80,512]{1,0:T(8,128)S(1)}, f32[80,512]{1,0:T(8,128)S(1)}, u32[]{:S(2)}, u32[]{:S(2)}) collective-permute-start(f32[80,512]{1,0:T(8,128)S(1)} %get-tuple-element.48), channel_id=1, source_target_pairs={{0,4},{4,0},{8,12},{12,8},{16,20},{20,16},{24,28},{28,24},{1,5},{5... | collective-permute-start | bytes 491528 | tf_op jit(solution)/shard_map/ppermute | solution.py:238
  17.1 10.3 %collective-permute-start.16 = (f32[168,512]{1,0:T(8,128)S(1)}, f32[168,512]{1,0:T(8,128)S(1)}, u32[]{:S(2)}, u32[]{:S(2)}) collective-permute-start(f32[168,512]{1,0:T(8,128)S(1)} %get-tuple-element.47), channel_id=1, source_target_pairs={{0,4},{4,0},{8,12},{12,8},{16,20},{20,16},{24,28},{28,24},{1,5},{5... | collective-permute-start | bytes 1032200 | tf_op jit(solution)/shard_map/ppermute | solution.py:238
  17.4 10.3 %collective-permute-start.18 = (f32[168,512]{1,0:T(8,128)S(1)}, f32[168,512]{1,0:T(8,128)S(1)}, u32[]{:S(2)}, u32[]{:S(2)}) collective-permute-start(f32[168,512]{1,0:T(8,128)S(1)} %shard_map.54), channel_id=1, source_target_pairs={{0,8},{4,12},{8,0},{12,4},{16,24},{20,28},{24,16},{28,20},{1,9},{5... | collective-permute-start | bytes 1032200 | tf_op jit(solution)/shard_map/ppermute | solution.py:238
  23.8 1.7 %collective-permute-start.8 = (f32[96,640]{1,0:T(8,128)S(1)}, f32[96,640]{1,0:T(8,128)S(1)}, u32[]{:S(2)}, u32[]{:S(2)}) collective-permute-start(f32[96,640]{1,0:T(8,128)S(1)} %get-tuple-element.41), channel_id=1, source_target_pairs={{0,4},{4,0},{8,12},{12,8},{16,20},{20,16},{24,28},{28,24},{1,5},{5... | collective-permute-start | bytes 737288 | tf_op jit(solution)/shard_map/ppermute | solution.py:238
  23.9 1.6 %collective-permute-start.14 = (f32[40,640]{1,0:T(8,128)S(1)}, f32[40,640]{1,0:T(8,128)S(1)}, u32[]{:S(2)}, u32[]{:S(2)}) collective-permute-start(f32[40,640]{1,0:T(8,128)S(1)} %get-tuple-element.45), channel_id=1, source_target_pairs={{0,4},{4,0},{8,12},{12,8},{16,20},{20,16},{24,28},{28,24},{1,5},{5... | collective-permute-start | bytes 307208 | tf_op jit(solution)/shard_map/ppermute | solution.py:238
  24.4 6.5 %collective-permute-start.13 = (f32[88,640]{1,0:T(8,128)S(1)}, f32[88,640]{1,0:T(8,128)S(1)}, u32[]{:S(2)}, u32[]{:S(2)}) collective-permute-start(f32[88,640]{1,0:T(8,128)S(1)} %get-tuple-element.44), channel_id=1, source_target_pairs={{0,4},{4,0},{8,12},{12,8},{16,20},{20,16},{24,28},{28,24},{1,5},{5... | collective-permute-start | bytes 675848 | tf_op jit(solution)/shard_map/ppermute | solution.py:238
  25.6 11.5 %collective-permute-start.15 = (f32[88,640]{1,0:T(8,128)S(1)}, f32[88,640]{1,0:T(8,128)S(1)}, u32[]{:S(2)}, u32[]{:S(2)}) collective-permute-start(f32[88,640]{1,0:T(8,128)S(1)} %shard_map.53), channel_id=1, source_target_pairs={{0,8},{4,12},{8,0},{12,4},{16,24},{20,28},{24,16},{28,20},{1,9},{5... | collective-permute-start | bytes 675848 | tf_op jit(solution)/shard_map/ppermute | solution.py:238
  27.7 12.7 %collective-permute-start.19 = (f32[88,512]{1,0:T(8,128)S(1)}, f32[88,512]{1,0:T(8,128)S(1)}, u32[]{:S(2)}, u32[]{:S(2)}) collective-permute-start(f32[88,512]{1,0:T(8,128)S(1)} %shard_map.55.send_ref), channel_id=1, source_target_pairs={{0,16},{4,20},{8,24},{12,28},{16,0},{20,4},{24,8},{28,12},{1,17},{... | collective-permute-start | bytes 540680 | tf_op jit(solution)/shard_map/ppermute | solution.py:238
  30.3 12.1 %collective-permute-start.7 = (f32[80,640]{1,0:T(8,128)S(1)}, f32[80,640]{1,0:T(8,128)S(1)}, u32[]{:S(2)}, u32[]{:S(2)}) collective-permute-start(f32[80,640]{1,0:T(8,128)S(1)} %get-tuple-element.40), channel_id=1, source_target_pairs={{0,4},{4,0},{8,12},{12,8},{16,20},{20,16},{24,28},{28,24},{1,5},{5... | collective-permute-start | bytes 614408 | tf_op jit(solution)/shard_map/ppermute | solution.py:238
  30.3 10.0 %collective-permute-start.11 = (f32[24,640]{1,0:T(8,128)S(1)}, f32[24,640]{1,0:T(8,128)S(1)}, u32[]{:S(2)}, u32[]{:S(2)}) collective-permute-start(f32[24,640]{1,0:T(8,128)S(1)} %get-tuple-element.43), channel_id=1, source_target_pairs={{0,4},{4,0},{8,12},{12,8},{16,20},{20,16},{24,28},{28,24},{1,5},{5... | collective-permute-start | bytes 184328 | tf_op jit(solution)/shard_map/ppermute | solution.py:238
  30.9 6.9 %collective-permute-start.10 = (f32[8,640]{1,0:T(8,128)S(1)}, f32[8,640]{1,0:T(8,128)S(1)}, u32[]{:S(2)}, u32[]{:S(2)}) collective-permute-start(f32[8,640]{1,0:T(8,128)S(1)} %get-tuple-element.42), channel_id=1, source_target_pairs={{0,4},{4,0},{8,12},{12,8},{16,20},{20,16},{24,28},{28,24},{1,5},{5... | collective-permute-start | bytes 61448 | tf_op jit(solution)/shard_map/ppermute | solution.py:238
  37.1 12.5 %collective-permute-start.20 = (f32[48,640]{1,0:T(8,128)S(1)}, f32[48,640]{1,0:T(8,128)S(1)}, u32[]{:S(2)}, u32[]{:S(2)}) collective-permute-start(f32[48,640]{1,0:T(8,128)S(1)} %shard_map.57), channel_id=1, source_target_pairs={{0,16},{4,20},{8,24},{12,28},{16,0},{20,4},{24,8},{28,12},{1,17},{... | collective-permute-start | bytes 368648 | tf_op jit(solution)/shard_map/ppermute | solution.py:238
  37.8 10.4 %collective-permute-start.9 = (f32[40,640]{1,0:T(8,128)S(1)}, f32[40,640]{1,0:T(8,128)S(1)}, u32[]{:S(2)}, u32[]{:S(2)}) collective-permute-start(f32[40,640]{1,0:T(8,128)S(1)} %shard_map.50), channel_id=1, source_target_pairs={{0,8},{4,12},{8,0},{12,4},{16,24},{20,28},{24,16},{28,20},{1,9},{5... | collective-permute-start | bytes 307208 | tf_op jit(solution)/shard_map/ppermute | solution.py:238
  40.3 9.0 %collective-permute-start.12 = (f32[40,640]{1,0:T(8,128)S(1)}, f32[40,640]{1,0:T(8,128)S(1)}, u32[]{:S(2)}, u32[]{:S(2)}) collective-permute-start(f32[40,640]{1,0:T(8,128)S(1)} %shard_map.51), channel_id=1, source_target_pairs={{0,8},{4,12},{8,0},{12,4},{16,24},{20,28},{24,16},{28,20},{1,9},{5... | collective-permute-start | bytes 307208 | tf_op jit(solution)/shard_map/ppermute | solution.py:238
  40.5 9.2 %collective-permute-start.21 = (f32[40,640]{1,0:T(8,128)S(1)}, f32[40,640]{1,0:T(8,128)S(1)}, u32[]{:S(2)}, u32[]{:S(2)}) collective-permute-start(f32[40,640]{1,0:T(8,128)S(1)} %shard_map.56.send_ref), channel_id=1, source_target_pairs={{0,16},{4,20},{8,24},{12,28},{16,0},{20,4},{24,8},{28,12},{1,17},{... | collective-permute-start | bytes 307208 | tf_op jit(solution)/shard_map/ppermute | solution.py:238
